TPU v7x, 128 devices: a whole 4x4x4 slice. The times are simulated.
128 devices in a mesh: row: 8 (over z, y_hi), col: 16 (over y_lo, x, core).
Axes of the slice: x: 4, y: 4 (y_hi: 2, y_lo: 2; y = y_hi * 2 + y_lo), z: 4, core: 2. Of those that a mesh axis runs over, the one named last changes fastest.
Arguments:
- tile_u: bfloat16 [8, 16, 2688, 256], P('row', 'col'), may hold values from -6 to 6
- tile_v: bfloat16 [8, 16, 2688, 256], P('row', 'col'), may hold values from -0.125 to 0.125
- row_u: bfloat16 [8, 2688, 256], P('row', 'col'), may hold values from -6 to 6
- row_v: bfloat16 [8, 2688, 256], P('row', 'col'), may hold values from -0.125 to 0.125
- col_u: bfloat16 [16, 2688, 64], P('col', 'row'), may hold values from -0.125 to 0.125
- col_v: bfloat16 [16, 2688, 64], P('col', 'row'), may hold values from -0.125 to 0.125
- tile_rank: int32 [8, 16], P('row', 'col'), may hold values from 32 to 256, as said below
- row_rank: int32 [8], P('row'), may hold values from 128 to 256, as said below
- col_rank: int32 [16], P('col'), may hold values from 32 to 64, as said below
- target_rank: int32 [8, 16], P('row', 'col'), may hold values from 32 to 256, as said below
- sketch: float32 [320, 256], replicated, may hold values from -6 to 6
Outputs:
- new_u: float32 [8, 16, 2688, 256], P('row', 'col')
- new_v: float32 [8, 16, 2688, 256], P('row', 'col')
Inputs may be any that keep to these rules, and one draw needn't show every extreme that they name: tile_rank(i,j) is 256 for at least one tile. target_rank(i,j) is at most tile_rank(i,j), and 256 for at least one tile. Every row_rank(i) is at least every col_rank(j). Every col_rank(j) is at most every row_rank(i).
All inputs are finite; a program needn't handle non-finite values.
Results may differ from a plain program's by a relative error of at most 0.00085.
Values may be sent and summed in bfloat16 or wider, within the bound.
No kernel may reach another device: no remote copies, remote signals or barrier semaphores. Data moves between devices by JAX's collectives and lax.ppermute only.
A program may use at most 128 MiB of HBM per device.

v0:
```python
import math

import jax
import jax.numpy as jnp
from jax import lax
from jax.experimental import pallas as pl
from jax.experimental.pallas import tpu as pltpu
from jax.sharding import PartitionSpec as P

F32 = jnp.float32
BF16 = jnp.bfloat16
HIGH = lax.Precision.HIGHEST


def nn(a, b, precision=HIGH):
    return lax.dot_general(a, b, (((1,), (0,)), ((), ())), precision=precision, preferred_element_type=F32)


def nt(a, b, precision=HIGH):
    return lax.dot_general(a, b, (((1,), (1,)), ((), ())), precision=precision, preferred_element_type=F32)


def tn(a, b, precision=None):
    return lax.dot_general(a, b, (((0,), (0,)), ((), ())), precision=precision, preferred_element_type=F32)


def lane_splat(x, lane):
    return jnp.broadcast_to(x[:, lane : lane + 1], x.shape)


def row_splat(x, row):
    return jnp.broadcast_to(x[row : row + 1, :], x.shape)


def total(terms):
    while len(terms) > 1:
        terms = [terms[k] + terms[k + 1] if k + 1 < len(terms) else terms[k] for k in range(0, len(terms), 2)]
    return terms[0]


def leaf(block):
    rows = [block[8 * r : 8 * r + 8, :] for r in range(8)]
    sub = lax.broadcasted_iota(jnp.int32, (8, 128), 0)
    for b in range(8):
        cols = {r: [lane_splat(rows[r], 64 + 8 * b + m) for m in range(8)] for r in range(b, 8)}
        a = {(s, m): row_splat(cols[b][m], s) for m in range(8) for s in range(m, 8)}
        own = [row_splat(rows[b], m) for m in range(8)]
        low = {}
        inv = {}
        for k in range(8):
            scale = lax.rsqrt(a[k, k])
            inv[k, k] = scale
            for i in range(k + 1, 8):
                low[i, k] = a[i, k] * scale
            for j in range(k + 1, 8):
                for i in range(j, 8):
                    a[i, j] = a[i, j] - low[i, k] * low[j, k]
        for m in range(8):
            for i in range(m + 1, 8):
                inv[i, m] = -inv[i, i] * total([low[i, q] * inv[q, m] for q in range(m, i)])
        up = [total([inv[n, m] * own[m] for m in range(n + 1)]) for n in range(8)]
        if b < 7:
            back = [total([inv[n, m] * up[n] for n in range(m, 8)]) for m in range(8)]
            for r in range(b + 1, 8):
                rows[r] = rows[r] - total([cols[r][m] * back[m] for m in range(8)])
        own_rows = up[0]
        for n in range(1, 8):
            own_rows = jnp.where(sub == n, up[n], own_rows)
        rows[b] = own_rows
    return jnp.concatenate(rows, axis=0)


def shifted(pair):
    lane = lax.broadcasted_iota(jnp.int32, pair.shape, 1)
    return jnp.where(lane >= 64, pltpu.roll(pair, 64, 1), 0.0)


def spread(matrix, aug_ref):
    size = matrix.shape[0]
    lane = lax.broadcasted_iota(jnp.int32, (size, 128), 1)
    row = lax.broadcasted_iota(jnp.int32, (size, 128), 0)
    for k in range(size // 64):
        half = matrix[:, 128 * (k // 2) : 128 * (k // 2) + 128]
        if k % 2 == 0:
            half = pltpu.roll(half, 64, 1)
        eye = (row == lane + 64 * k).astype(F32)
        aug_ref[:, 128 * k : 128 * k + 128] = jnp.where(lane >= 64, half, eye)


def gather_inverse(aug_ref):
    lane = lax.broadcasted_iota(jnp.int32, (aug_ref.shape[0], 128), 1)
    parts = []
    for t in range(aug_ref.shape[1] // 256):
        even = aug_ref[:, 256 * t : 256 * t + 128]
        odd = aug_ref[:, 256 * t + 128 : 256 * t + 256]
        parts.append(jnp.where(lane < 64, even, pltpu.roll(odd, 64, 1)))
    return jnp.concatenate(parts, axis=1)


def factor(aug_ref, low_refs=None):
    size = aug_ref.shape[0]
    for k in range(size // 64):
        here = slice(64 * k, 64 * k + 64)
        tile = slice(128 * k, 128 * k + 128)
        pair = leaf(aug_ref[here, tile])
        wide = shifted(pair)
        first = 64 * k if low_refs is not None else 64 * k + 64
        if first < size:
            left = nt(aug_ref[first:, tile], wide)
        ahead = nn(pair[:, :64], aug_ref[here, :])
        aug_ref[here, :] = ahead
        if low_refs is not None:
            low_refs[k][64 * k :, :] = left
            left = left[64:]
        if 64 * k + 64 < size:
            aug_ref[64 * k + 64 :, :] = aug_ref[64 * k + 64 :, :] - nn(left, ahead)


def masked_gram(gram, rank):
    size = gram.shape[0]
    row = lax.broadcasted_iota(jnp.int32, gram.shape, 0)
    col = lax.broadcasted_iota(jnp.int32, gram.shape, 1)
    both = (row < rank) & (col < rank)
    dead = (row == col) & (row >= rank)
    return jnp.where(both, gram, 0.0), dead.astype(F32)


def own_kernel(ranks, tile_u, tile_v, gram_u, low, low_inv, aug_ref, l0, l1, l2, l3):
    rank = ranks[0]
    plain, dead = masked_gram(tn(tile_v[...], tile_v[...]), rank)
    spread(plain + dead, aug_ref)
    plain_u, unused = masked_gram(tn(tile_u[...], tile_u[...]), rank)
    gram_u[...] = plain_u
    lows = (l0, l1, l2, l3)
    factor(aug_ref, lows)
    low_inv[...] = gather_inverse(aug_ref)
    row = lax.broadcasted_iota(jnp.int32, (256, 256), 0)
    col = lax.broadcasted_iota(jnp.int32, (256, 256), 1)
    joined = jnp.concatenate([l0[...], l1[...], l2[...], l3[...]], axis=1)
    low[...] = jnp.where(row >= col, joined, 0.0)


def own_call(ranks, tile_u, tile_v):
    square = jax.ShapeDtypeStruct((256, 256), F32)
    vmem = pl.BlockSpec(memory_space=pltpu.VMEM)
    return pl.pallas_call(
        own_kernel,
        out_shape=(square,) * 3,
        in_specs=[pl.BlockSpec(memory_space=pltpu.SMEM), vmem, vmem],
        out_specs=(vmem,) * 3,
        scratch_shapes=[pltpu.VMEM((256, 512), F32)] + [pltpu.VMEM((256, 64), F32)] * 4,
        compiler_params=pltpu.CompilerParams(vmem_limit_bytes=40 * 1024 * 1024),
        cost_estimate=pl.CostEstimate(flops=20 * 10**9, bytes_accessed=4 * 10**6, transcendentals=0),
        name="own_factor",
    )(ranks, tile_u, tile_v)


CHUNK = 336
SHIFTS = (0, 1, 3, 2)
TOLERANCE = 3e-4


def main_kernel(ranks, gram_tt, low, low_inv, sketch_t, tile_u_hbm, tile_v_hbm, mine_hbm, other_hbm, side0, side1, side2, side3,
                out_u_hbm, out_v_hbm,
                tile_u, tile_v, panel, col_uv, up, wide_u, out_u, out_v, aug_ref, w_t, w_p, g_t, g_p,
                in_sem, out_sem):
    rows = tile_u.shape[0]
    block = side0.shape[1]

    def place(first, second):
        return pl.ds(pl.multiple_of((first * 4 + second) * block, block), block)

    mine, high, z, x = ranks[4], ranks[5], ranks[6], ranks[7]
    y_half = ranks[8]
    side_loads = []
    for hop, side in enumerate((side0, side1, side2, side3)):
        for k in range(2):
            start = (lax.rem(z - SHIFTS[hop] + 4, 4) * 2 + lax.rem(y_half + k, 2)) * block
            spot = pl.ds(pl.multiple_of(start, block), block)
            side_loads.append(pltpu.make_async_copy(side.at[k], col_uv.at[spot, :], in_sem.at[2 * hop + k]))
    row_loads = []
    for which, array in enumerate((mine_hbm, other_hbm)):
        slot = lax.rem(mine + which, 2)
        for hop in range(4):
            for k in range(2):
                spot = place(lax.rem(high + k, 2), lax.rem(x - SHIFTS[hop] + 4, 4))
                sem = in_sem.at[8 + 8 * which + 2 * hop + k]
                row_loads.append(pltpu.make_async_copy(array.at[hop, k], panel.at[slot, spot, :], sem))
    load_v = pltpu.make_async_copy(tile_v_hbm, tile_v, in_sem.at[24])
    load_u = pltpu.make_async_copy(tile_u_hbm, tile_u, in_sem.at[25])
    for load in side_loads + [load_v] + row_loads + [load_u]:
        load.start()
    t_rank, i_rank, j_rank, s_rank = ranks[0], ranks[1], ranks[2], ranks[3]
    iota = lambda shape, dim: lax.broadcasted_iota(jnp.int32, shape, dim)
    for load in side_loads + [load_v]:
        load.wait()
    both = col_uv[...]
    mask_pt = (iota((64, 256), 0) < j_rank) & (iota((64, 256), 1) < t_rank)
    side = jnp.where(mask_pt, -tn(both, tile_v[...])[:64], 0.0)
    corner, dead = masked_gram(tn(both, both)[:64, :64], j_rank)
    low_pt = nt(side, low_inv[...])
    schur = corner + dead - nt(low_pt, low_pt)
    eye = (iota((64, 64), 0) == iota((64, 64), 1)).astype(F32)
    start = jnp.concatenate([eye, schur], axis=1)
    pair = leaf(start)
    low_pp = nt(start, shifted(pair))
    low_pp = jnp.where(iota((64, 64), 0) >= iota((64, 64), 1), low_pp, 0.0)
    keep_rows = iota((256, 320), 0) < s_rank
    st = jnp.where(keep_rows, sketch_t[...], 0.0)
    st_t, st_p = st[:, :256], st[:, 256:]
    keep_tt = iota((256, 256), 1) < t_rank
    keep_tp = iota((256, 64), 1) < j_rank
    y_t = jnp.where(keep_tt, nt(st_t, low[...]), 0.0)
    y_p = jnp.where(keep_tp, nt(st_t, low_pt) + nt(st_p, low_pp), 0.0)
    for load in row_loads:
        load.wait()
    mask_ij = (iota((64, 256), 0) < j_rank) & (iota((64, 256), 1) < i_rank)
    cross_t = jnp.where(mask_ij, tn(col_uv[...], panel[1])[64:], 0.0).astype(BF16)

    def expand(step, carry):
        here = pl.ds(pl.multiple_of(step * CHUNK, CHUNK), CHUNK)
        update = nt(panel[0, here, :], cross_t, None)
        top = update.astype(BF16)
        rest = (update - top.astype(F32)).astype(BF16)
        up[here, :] = jnp.concatenate([top, rest], axis=1)
        side_u = col_uv[here, :][:, :64]
        wide_u[here, :] = jnp.concatenate([side_u, side_u], axis=1)
        return carry

    lax.fori_loop(0, rows // CHUNK, expand, 0)
    load_u.wait()
    both_t = tn(up[...], tile_u[...])
    gram_pt = jnp.where(mask_pt, both_t[:64] + both_t[64:], 0.0)
    four = tn(up[...], up[...])
    four = four[:64] + four[64:]
    gram_pp = (four + pltpu.roll(four, 64, 1))[:, :64]
    x_t = nn(y_t, gram_tt[...]) + nn(y_p, gram_pt)
    x_p = nt(y_t, gram_pt) + nn(y_p, gram_pp)
    middle = nt(x_t, y_t) + nt(x_p, y_p)
    same = iota((256, 256), 0) == iota((256, 256), 1)
    off = (iota((256, 256), 0) >= s_rank) & same
    spread(middle + off.astype(F32), aug_ref)
    factor(aug_ref)
    inverse = gather_inverse(aug_ref)
    w_t[...] = nn(inverse, y_t)
    w_p[...] = nn(inverse, y_p)
    g_t[...] = nn(inverse, x_t)
    g_p[...] = nn(inverse, x_p)
    live = (iota((256, 256), 0) < s_rank) & same
    lower = jnp.where(iota((256, 256), 0) > iota((256, 256), 1), 1.0, 0.0) + jnp.where(same, 0.5, 0.0)

    def refine(state):
        count, unused = state
        error = nt(w_t[...], g_t[...]) + nt(w_p[...], g_p[...]) - live.astype(F32)
        size = jnp.max(jnp.sum(jnp.abs(error), axis=1, keepdims=True))
        error = error * lower
        for ref in (w_t, w_p, g_t, g_p):
            ref[...] = ref[...] - nn(error, ref[...])
        return count + 1, size

    lax.while_loop(lambda s: (s[0] < 12) & (s[1] > TOLERANCE), refine, (jnp.int32(0), jnp.float32(1.0)))
    scale = math.sqrt(rows)

    def halves(x):
        top = x.astype(BF16)
        return top, (x - top.astype(F32)).astype(BF16)

    u_hi, u_lo = halves(w_t[...] * scale)
    p_hi, p_lo = halves(w_p[...] * scale)
    p_hi2 = jnp.concatenate([p_hi, p_hi], axis=1)
    p_lo2 = jnp.concatenate([p_lo, p_lo], axis=1)
    v_hi, v_lo = halves(g_t[...])
    q2 = jnp.concatenate(halves(-g_p[...]), axis=1)

    def send(step, carry):
        here = pl.ds(pl.multiple_of(step * CHUNK, CHUNK), CHUNK)
        tile = tile_u[here, :]
        extra = up[here, :]
        out_u[here, :] = nt(tile, u_hi, None) + nt(tile, u_lo, None) + nt(extra, p_hi2, None) + nt(extra, p_lo2, None)
        pltpu.make_async_copy(out_u.at[here, :], out_u_hbm.at[here, :], out_sem.at[0, step]).start()
        tile = tile_v[here, :]
        out_v[here, :] = nt(tile, v_hi, None) + nt(tile, v_lo, None) + nt(wide_u[here, :], q2, None)
        pltpu.make_async_copy(out_v.at[here, :], out_v_hbm.at[here, :], out_sem.at[1, step]).start()
        return carry

    lax.fori_loop(0, rows // CHUNK, send, 0)
    for step in range(rows // CHUNK):
        here = pl.ds(step * CHUNK, CHUNK)
        pltpu.make_async_copy(out_u.at[here, :], out_u_hbm.at[here, :], out_sem.at[0, step]).wait()
        pltpu.make_async_copy(out_v.at[here, :], out_v_hbm.at[here, :], out_sem.at[1, step]).wait()


def main_call(ranks, gram_tt, low, low_inv, sketch_t, tile_u, tile_v, mine, other, sides):
    rows = tile_u.shape[0]
    vmem = pl.BlockSpec(memory_space=pltpu.VMEM)
    hbm = pl.BlockSpec(memory_space=pl.ANY)
    out = jax.ShapeDtypeStruct((rows, 256), F32)
    wide = pltpu.VMEM((rows, 256), BF16)
    thin = pltpu.VMEM((rows, 128), BF16)
    return pl.pallas_call(
        main_kernel,
        out_shape=(out, out),
        in_specs=[pl.BlockSpec(memory_space=pltpu.SMEM)] + [vmem] * 4 + [hbm] * 8,
        out_specs=(hbm, hbm),
        scratch_shapes=[wide, wide, pltpu.VMEM((2, rows, 256), BF16), thin, thin, thin,
                        pltpu.VMEM((rows, 256), F32), pltpu.VMEM((rows, 256), F32), pltpu.VMEM((256, 512), F32),
                        pltpu.VMEM((256, 256), F32), pltpu.VMEM((256, 64), F32), pltpu.VMEM((256, 256), F32), pltpu.VMEM((256, 64), F32),
                        pltpu.SemaphoreType.DMA((26,)), pltpu.SemaphoreType.DMA((2, rows // CHUNK))],
        compiler_params=pltpu.CompilerParams(vmem_limit_bytes=48 * 1024 * 1024),
        cost_estimate=pl.CostEstimate(flops=20 * 10**9, bytes_accessed=15 * 10**6, transcendentals=0),
        name="recompress",
    )(ranks, gram_tt, low, low_inv, sketch_t, tile_u, tile_v, mine, other, *sides)


def send(x, axis, count, step):
    return lax.ppermute(x, axis, [(i, step(i)) for i in range(count)])


def body(tile_u, tile_v, row_u, row_v, col_u, col_v, tile_rank, row_rank, col_rank, target_rank, sketch):
    spot_i, spot_j = lax.axis_index("row"), lax.axis_index("col")
    core, x, y_low = spot_j % 2, spot_j // 2 % 4, spot_j // 8
    z, y_half = spot_i // 2, spot_i % 2
    first = core == 0
    side = jnp.concatenate([col_u[0], col_v[0]], axis=1)
    side_other = send(side, "row", 8, lambda i: i ^ 1)
    give = jnp.where(first, row_v[0], row_u[0])
    keep = jnp.where(first, row_u[0], row_v[0])
    got = send(give, "col", 16, lambda i: i ^ 1)
    chip = jnp.concatenate([jnp.where(first, keep, got), jnp.where(first, got, keep)], axis=0)
    chip_other = send(chip, "col", 16, lambda i: i ^ 8)
    ranks = jnp.stack([tile_rank[0, 0], row_rank[0], col_rank[0], target_rank[0, 0], core, y_low, z, x, y_half]).astype(jnp.int32)
    gram_tt, low, low_inv = own_call(ranks, tile_u[0, 0], tile_v[0, 0])
    side_other, chip_other = lax.optimization_barrier((side_other, chip_other))
    sides = [jnp.stack([side, side_other])]
    chips = [jnp.stack([chip, chip_other])]
    for shift in SHIFTS[1:]:
        sides.append(send(sides[0], "row", 8, lambda i: (i + 2 * shift) % 8))
        chips.append(send(chips[0], "col", 16, lambda i: i // 8 * 8 + (i + 2 * shift) % 8))
    mine = jnp.stack(chips)
    other = send(mine, "col", 16, lambda i: i ^ 1)
    new_u, new_v = main_call(ranks, gram_tt, low, low_inv, sketch.T, tile_u[0, 0], tile_v[0, 0], mine, other, sides)
    return (new_u[None, None], new_v[None, None])


def solution(mesh):
    placed = (
        P("row", "col", None, None),
        P("row", "col", None, None),
        P("row", "col", None),
        P("row", "col", None),
        P("col", "row", None),
        P("col", "row", None),
        P("row", "col"),
        P("row"),
        P("col"),
        P("row", "col"),
        P(),
    )
    return jax.shard_map(
        body,
        mesh=mesh,
        in_specs=placed,
        out_specs=(P("row", "col", None, None), P("row", "col", None, None)),
        check_vma=False,
    )
```

profile of v0, /device:TPU:1, one launch (start us, length us, event | category | flops | bytes accessed | tf_op | source)
XLA Modules:
  0.0 93.8 jit_solution(10097821025102618638)
XLA Ops:
  0.6 0.9 select_bitcast_fusion
  1.6 1.5 %collective-permute-start = (bf16[168,256]{1,0:T(8,128)(2,1)S(1)}, bf16[168,256]{1,0:T(8,128)(2,1)S(1)}, u32[]{:S(2)}, u32[]{:S(2)}) collective-permute-start(bf16[168,256]{1,0:T(8,128)(2,1)S(1)} %select_bitcast_fusion), channel_id=1, source_target_pairs={{0,1},{1,0},{2,3},{3,2},{4,5},{5,4},{6,7},{7,6},{8,9},{9,8},{10,11... | collective-permute-start | bytes 258056 | tf_op jit(solution)/shard_map/ppermute | solution.py:316
  3.1 0.9 copy.14
  4.0 0.9 copy.15
  4.9 0.0 collective-permute-done
  4.9 0.9 bitcast_select_fusion.1
  5.9 1.5 %collective-permute-start.2 = (bf16[336,256]{1,0:T(8,128)(2,1)S(1)}, bf16[336,256]{1,0:T(8,128)(2,1)S(1)}, u32[]{:S(2)}, u32[]{:S(2)}) collective-permute-start(bf16[336,256]{1,0:T(8,128)(2,1)S(1)} %get-tuple-element.21), channel_id=1, source_target_pairs={{0,8},{1,9},{2,10},{3,11},{4,12},{5,13},{6,14},{7,15},{8,0},{9,1},... | collective-permute-start | bytes 516104 | tf_op jit(solution)/shard_map/ppermute | solution.py:316
  7.3 0.1 pad_maximum_fusion.4
  7.4 2.7 %collective-permute-start.1 = (bf16[336,128]{1,0:T(8,128)(2,1)S(1)}, bf16[336,128]{1,0:T(8,128)(2,1)S(1)}, u32[]{:S(2)}, u32[]{:S(2)}) collective-permute-start(bf16[336,128]{1,0:T(8,128)(2,1)S(1)} %pad_maximum_fusion.4), channel_id=1, source_target_pairs={{0,16},{16,0},{32,48},{48,32},{64,80},{80,64},{96,112},{112,96},{1... | collective-permute-start | bytes 258056 | tf_op jit(solution)/shard_map/ppermute | solution.py:316
  10.1 6.2 %collective-permute-done.1 = bf16[336,128]{1,0:T(8,128)(2,1)S(1)} collective-permute-done((bf16[336,128]{1,0:T(8,128)(2,1)S(1)}, bf16[336,128]{1,0:T(8,128)(2,1)S(1)}, u32[]{:S(2)}, u32[]{:S(2)}) %collective-permute-start.1) | collective-permute-done | bytes 86048 | tf_op jit(solution)/shard_map/ppermute | solution.py:316
  16.3 0.0 collective-permute-done.2
  16.4 2.5 %collective-permute-start.4 = (bf16[2,336,256]{2,1,0:T(8,128)(2,1)S(1)}, bf16[2,336,256]{2,1,0:T(8,128)(2,1)}, u32[]{:S(2)}, u32[]{:S(2)}) collective-permute-start(bf16[2,336,256]{2,1,0:T(8,128)(2,1)S(1)} %get-tuple-element.17), channel_id=1, source_target_pairs={{0,6},{1,7},{2,0},{3,1},{4,2},{5,3},{6,4},{7,5},{8,14},{9,15},{10,... | collective-permute-start | bytes 1032200 | tf_op jit(solution)/shard_map/ppermute | solution.py:316
  18.9 0.0 collective-permute-start.3
  18.9 1.7 %collective-permute-start.5 = (bf16[2,336,256]{2,1,0:T(8,128)(2,1)S(1)}, bf16[2,336,256]{2,1,0:T(8,128)(2,1)}, u32[]{:S(2)}, u32[]{:S(2)}) collective-permute-start(bf16[2,336,256]{2,1,0:T(8,128)(2,1)S(1)} %get-tuple-element.17), channel_id=1, source_target_pairs={{0,4},{1,5},{2,6},{3,7},{4,0},{5,1},{6,2},{7,3},{8,12},{9,13},{10,... | collective-permute-start | bytes 1032200 | tf_op jit(solution)/shard_map/ppermute | solution.py:316
  23.3 0.1 stack.56.ranks
  23.3 0.1 fusion.2
  23.5 3.7 %collective-permute-start.9 = (bf16[2,336,128]{2,1,0:T(8,128)(2,1)S(1)}, bf16[2,336,128]{2,1,0:T(8,128)(2,1)S(1)}, u32[]{:S(2)}, u32[]{:S(2)}) collective-permute-start(bf16[2,336,128]{2,1,0:T(8,128)(2,1)S(1)} %pad_maximum_fusion.3.side0), channel_id=1, source_target_pairs={{0,64},{16,80},{32,96},{48,112},{64,0},{80,16},{96,32},{112,48},{1... | collective-permute-start | bytes 516104 | tf_op jit(solution)/shard_map/ppermute | solution.py:316
  27.2 0.4 collective-permute-start.8
  27.6 0.0 collective-permute-done.4
  27.6 1.0 %collective-permute-start.7 = (bf16[2,336,128]{2,1,0:T(8,128)(2,1)S(1)}, bf16[2,336,128]{2,1,0:T(8,128)(2,1)}, u32[]{:S(2)}, u32[]{:S(2)}) collective-permute-start(bf16[2,336,128]{2,1,0:T(8,128)(2,1)S(1)} %pad_maximum_fusion.3.side0), channel_id=1, source_target_pairs={{0,32},{16,48},{32,64},{48,80},{64,96},{80,112},{96,0},{112,16},{1... | collective-permute-start | bytes 516104 | tf_op jit(solution)/shard_map/ppermute | solution.py:316
  28.6 1.0 %collective-permute-done.3 = bf16[2,336,256]{2,1,0:T(8,128)(2,1)} collective-permute-done((bf16[2,336,256]{2,1,0:T(8,128)(2,1)S(1)}, bf16[2,336,256]{2,1,0:T(8,128)(2,1)}, u32[]{:S(2)}, u32[]{:S(2)}) %collective-permute-start.3) | collective-permute-done | bytes 344096 | tf_op jit(solution)/shard_map/ppermute | solution.py:316
  29.7 5.5 %collective-permute-done.5 = bf16[2,336,256]{2,1,0:T(8,128)(2,1)} collective-permute-done((bf16[2,336,256]{2,1,0:T(8,128)(2,1)S(1)}, bf16[2,336,256]{2,1,0:T(8,128)(2,1)}, u32[]{:S(2)}, u32[]{:S(2)}) %collective-permute-start.5) | collective-permute-done | bytes 344096 | tf_op jit(solution)/shard_map/ppermute | solution.py:316
  35.2 0.0 copy-start
  35.2 0.0 copy-start.1
  35.2 1.5 %pad_maximum_fusion.mine_hbm = bf16[4,2,336,256]{3,2,1,0:T(8,128)(2,1)S(1)} fusion(bf16[1,2,336,256]{3,2,1,0:T(8,128)(2,1)} %bitcast.19, bf16[1,2,336,256]{3,2,1,0:T(8,128)(2,1)} %bitcast.18, bf16[1,2,336,256]{3,2,1,0:T(8,128)(2,1)} %bitcast.17, bf16[1,2,336,256]{3,2,1,0:T(8,128)(2,1)S(1)} %get-tuple-element.16), kind=kLoop, calls=%fused_computation | loop fusion | flops 2064384 | bytes 2752512 | tf_op jit(solution)/shard_map/stack | solution.py:339
  36.7 3.2 %collective-permute-start.6 = (bf16[4,2,336,256]{3,2,1,0:T(8,128)(2,1)S(1)}, bf16[4,2,336,256]{3,2,1,0:T(8,128)(2,1)}, u32[]{:S(2)}, u32[]{:S(2)}) collective-permute-start(bf16[4,2,336,256]{3,2,1,0:T(8,128)(2,1)S(1)} %pad_maximum_fusion.mine_hbm), channel_id=1, source_target_pairs={{0,1},{1,0},{2,3},{3,2},{4,5},{5,4},{6,7},{7,6},{8,9},{9,8},{10,11... | collective-permute-start | bytes 4128776 | tf_op jit(solution)/shard_map/ppermute | solution.py:316
  39.9 0.0 copy-done
  39.9 0.0 copy-done.1
  39.9 12.9 %own_factor.1 = (f32[256,256]{1,0:T(8,128)S(1)}, f32[256,256]{1,0:T(8,128)S(1)}, f32[256,256]{1,0:T(8,128)S(1)}) custom-call(s32[9]{0:T(128)S(1)} %stack.56.ranks, bf16[2688,256]{1,0:T(8,128)(2,1)S(1)} %bitcast.33, bf16[2688,256]{1,0:T(8,128)(2,1)S(1)} %bitcast.35), custom_call_target="tpu_custom_call" | custom-call | flops 20000000000 | bytes 4000000 | tf_op jit(solution)/shard_map/own_factor/pallas_call | solution.py:146
  52.8 0.0 copy-start.3
  52.8 0.7 copy-done.3
  53.5 0.0 copy-start.5
  53.5 0.7 copy-done.5
  54.2 0.0 copy-start.7
  54.2 0.7 copy-done.7
  54.9 1.1 %copy.13 = f32[320,256]{0,1:T(8,128)S(1)} copy(f32[320,256]{1,0:T(8,128)} %param.21) | data formatting | bytes 655360 | tf_op args[10]
  56.0 0.0 collective-permute-done.9.side3
  56.0 0.0 collective-permute-done.8.side2
  56.0 0.0 collective-permute-done.7.side1
  56.0 0.0 collective-permute-done.6.other_hbm
  56.1 0.0 copy-start.2
  56.1 1.3 %copy-done.2 = bf16[1,1,2688,256]{3,2,1,0:T(8,128)(2,1)S(1)} copy-done((bf16[1,1,2688,256]{3,2,1,0:T(8,128)(2,1)S(1)}, bf16[1,1,2688,256]{3,2,1,0:T(8,128)(2,1)}, u32[]{:S(2)}) %copy-start.2) | copy-done | bytes 1376280
  57.4 0.0 copy-start.4
  57.4 0.9 %copy-done.4 = f32[256,256]{1,0:T(8,128)S(1)} copy-done((f32[256,256]{1,0:T(8,128)S(1)}, f32[256,256]{1,0:T(8,128)}, u32[]{:S(2)}) %copy-start.4) | copy-done | bytes 262168
  58.3 0.0 copy-start.6
  58.4 0.9 %copy-done.6 = f32[256,256]{1,0:T(8,128)S(1)} copy-done((f32[256,256]{1,0:T(8,128)S(1)}, f32[256,256]{1,0:T(8,128)}, u32[]{:S(2)}) %copy-start.6) | copy-done | bytes 262168
  59.3 0.9 %copy-done.8 = f32[256,256]{1,0:T(8,128)S(1)} copy-done((f32[256,256]{1,0:T(8,128)S(1)}, f32[256,256]{1,0:T(8,128)}, u32[]{:S(2)}) %copy-start.8) | copy-done | bytes 262168
  60.2 33.3 %recompress.1 = (f32[2688,256]{1,0:T(8,128)}, f32[2688,256]{1,0:T(8,128)}) custom-call(s32[9]{0:T(128)S(1)} %stack.56.ranks, f32[256,256]{1,0:T(8,128)S(1)} %copy-done.4, f32[256,256]{1,0:T(8,128)S(1)} %copy-done.6, f32[256,256]{1,0:T(8,128)S(1)} %copy-done.8, f32[256,320]{1,0:T(8,128)S(1)} %bitcast.32, bf16[2688,256]{1,0:T(8,128)(2,1)S(1)} %bitcast.34, ...), custom_call_target="tpu_custom_call" | custom-call | flops 20000000000 | bytes 15000000 | tf_op jit(solution)/shard_map/recompress/pallas_call | solution.py:300
  (4 shorter events, 0.1 us)
Async XLA Ops:
  1.6 3.3 %collective-permute-start = (bf16[168,256]{1,0:T(8,128)(2,1)S(1)}, bf16[168,256]{1,0:T(8,128)(2,1)S(1)}, u32[]{:S(2)}, u32[]{:S(2)}) collective-permute-start(bf16[168,256]{1,0:T(8,128)(2,1)S(1)} %select_bitcast_fusion), channel_id=1, source_target_pairs={{0,1},{1,0},{2,3},{3,2},{4,5},{5,4},{6,7},{7,6},{8,9},{9,8},{10,11... | collective-permute-start | bytes 258056 | tf_op jit(solution)/shard_map/ppermute | solution.py:316
  5.9 10.5 %collective-permute-start.2 = (bf16[336,256]{1,0:T(8,128)(2,1)S(1)}, bf16[336,256]{1,0:T(8,128)(2,1)S(1)}, u32[]{:S(2)}, u32[]{:S(2)}) collective-permute-start(bf16[336,256]{1,0:T(8,128)(2,1)S(1)} %get-tuple-element.21), channel_id=1, source_target_pairs={{0,8},{1,9},{2,10},{3,11},{4,12},{5,13},{6,14},{7,15},{8,0},{9,1},... | collective-permute-start | bytes 516104 | tf_op jit(solution)/shard_map/ppermute | solution.py:316
  7.4 8.9 %collective-permute-start.1 = (bf16[336,128]{1,0:T(8,128)(2,1)S(1)}, bf16[336,128]{1,0:T(8,128)(2,1)S(1)}, u32[]{:S(2)}, u32[]{:S(2)}) collective-permute-start(bf16[336,128]{1,0:T(8,128)(2,1)S(1)} %pad_maximum_fusion.4), channel_id=1, source_target_pairs={{0,16},{16,0},{32,48},{48,32},{64,80},{80,64},{96,112},{112,96},{1... | collective-permute-start | bytes 258056 | tf_op jit(solution)/shard_map/ppermute | solution.py:316
  16.4 11.2 %collective-permute-start.4 = (bf16[2,336,256]{2,1,0:T(8,128)(2,1)S(1)}, bf16[2,336,256]{2,1,0:T(8,128)(2,1)}, u32[]{:S(2)}, u32[]{:S(2)}) collective-permute-start(bf16[2,336,256]{2,1,0:T(8,128)(2,1)S(1)} %get-tuple-element.17), channel_id=1, source_target_pairs={{0,6},{1,7},{2,0},{3,1},{4,2},{5,3},{6,4},{7,5},{8,14},{9,15},{10,... | collective-permute-start | bytes 1032200 | tf_op jit(solution)/shard_map/ppermute | solution.py:316
  18.9 10.7 %collective-permute-start.3 = (bf16[2,336,256]{2,1,0:T(8,128)(2,1)S(1)}, bf16[2,336,256]{2,1,0:T(8,128)(2,1)}, u32[]{:S(2)}, u32[]{:S(2)}) collective-permute-start(bf16[2,336,256]{2,1,0:T(8,128)(2,1)S(1)} %get-tuple-element.17), channel_id=1, source_target_pairs={{0,2},{1,3},{2,4},{3,5},{4,6},{5,7},{6,0},{7,1},{8,10},{9,11},{10,... | collective-permute-start | bytes 1032200 | tf_op jit(solution)/shard_map/ppermute | solution.py:316
  18.9 16.3 %collective-permute-start.5 = (bf16[2,336,256]{2,1,0:T(8,128)(2,1)S(1)}, bf16[2,336,256]{2,1,0:T(8,128)(2,1)}, u32[]{:S(2)}, u32[]{:S(2)}) collective-permute-start(bf16[2,336,256]{2,1,0:T(8,128)(2,1)S(1)} %get-tuple-element.17), channel_id=1, source_target_pairs={{0,4},{1,5},{2,6},{3,7},{4,0},{5,1},{6,2},{7,3},{8,12},{9,13},{10,... | collective-permute-start | bytes 1032200 | tf_op jit(solution)/shard_map/ppermute | solution.py:316
  23.5 32.5 %collective-permute-start.9 = (bf16[2,336,128]{2,1,0:T(8,128)(2,1)S(1)}, bf16[2,336,128]{2,1,0:T(8,128)(2,1)S(1)}, u32[]{:S(2)}, u32[]{:S(2)}) collective-permute-start(bf16[2,336,128]{2,1,0:T(8,128)(2,1)S(1)} %pad_maximum_fusion.3.side0), channel_id=1, source_target_pairs={{0,64},{16,80},{32,96},{48,112},{64,0},{80,16},{96,32},{112,48},{1... | collective-permute-start | bytes 516104 | tf_op jit(solution)/shard_map/ppermute | solution.py:316
  27.2 28.9 %collective-permute-start.8 = (bf16[2,336,128]{2,1,0:T(8,128)(2,1)S(1)}, bf16[2,336,128]{2,1,0:T(8,128)(2,1)}, u32[]{:S(2)}, u32[]{:S(2)}) collective-permute-start(bf16[2,336,128]{2,1,0:T(8,128)(2,1)S(1)} %pad_maximum_fusion.3.side0), channel_id=1, source_target_pairs={{0,96},{16,112},{32,0},{48,16},{64,32},{80,48},{96,64},{112,80},{1... | collective-permute-start | bytes 516104 | tf_op jit(solution)/shard_map/ppermute | solution.py:316
  27.6 28.5 %collective-permute-start.7 = (bf16[2,336,128]{2,1,0:T(8,128)(2,1)S(1)}, bf16[2,336,128]{2,1,0:T(8,128)(2,1)}, u32[]{:S(2)}, u32[]{:S(2)}) collective-permute-start(bf16[2,336,128]{2,1,0:T(8,128)(2,1)S(1)} %pad_maximum_fusion.3.side0), channel_id=1, source_target_pairs={{0,32},{16,48},{32,64},{48,80},{64,96},{80,112},{96,0},{112,16},{1... | collective-permute-start | bytes 516104 | tf_op jit(solution)/shard_map/ppermute | solution.py:316
  35.2 4.7 %copy-start = (bf16[1,1,2688,256]{3,2,1,0:T(8,128)(2,1)S(1)}, bf16[1,1,2688,256]{3,2,1,0:T(8,128)(2,1)}, u32[]{:S(2)}) copy-start(bf16[1,1,2688,256]{3,2,1,0:T(8,128)(2,1)} %param.11) | copy-start | bytes 4128772
  35.2 4.7 %copy-start.1 = (bf16[1,1,2688,256]{3,2,1,0:T(8,128)(2,1)S(1)}, bf16[1,1,2688,256]{3,2,1,0:T(8,128)(2,1)}, u32[]{:S(2)}) copy-start(bf16[1,1,2688,256]{3,2,1,0:T(8,128)(2,1)} %param.12) | copy-start | bytes 4128772
  36.7 19.3 %collective-permute-start.6 = (bf16[4,2,336,256]{3,2,1,0:T(8,128)(2,1)S(1)}, bf16[4,2,336,256]{3,2,1,0:T(8,128)(2,1)}, u32[]{:S(2)}, u32[]{:S(2)}) collective-permute-start(bf16[4,2,336,256]{3,2,1,0:T(8,128)(2,1)S(1)} %pad_maximum_fusion.mine_hbm), channel_id=1, source_target_pairs={{0,1},{1,0},{2,3},{3,2},{4,5},{5,4},{6,7},{7,6},{8,9},{9,8},{10,11... | collective-permute-start | bytes 4128776 | tf_op jit(solution)/shard_map/ppermute | solution.py:316
  52.8 0.7 copy-start.3
  53.5 0.7 copy-start.5
  54.2 0.7 copy-start.7
  56.1 1.3 %copy-start.2 = (bf16[1,1,2688,256]{3,2,1,0:T(8,128)(2,1)S(1)}, bf16[1,1,2688,256]{3,2,1,0:T(8,128)(2,1)}, u32[]{:S(2)}) copy-start(bf16[1,1,2688,256]{3,2,1,0:T(8,128)(2,1)} %param.12) | copy-start | bytes 4128772
  57.4 0.9 %copy-start.4 = (f32[256,256]{1,0:T(8,128)S(1)}, f32[256,256]{1,0:T(8,128)}, u32[]{:S(2)}) copy-start(f32[256,256]{1,0:T(8,128)} %copy-done.3) | copy-start | bytes 786436
  58.3 0.9 %copy-start.6 = (f32[256,256]{1,0:T(8,128)S(1)}, f32[256,256]{1,0:T(8,128)}, u32[]{:S(2)}) copy-start(f32[256,256]{1,0:T(8,128)} %copy-done.5) | copy-start | bytes 786436
  59.3 0.9 %copy-start.8 = (f32[256,256]{1,0:T(8,128)S(1)}, f32[256,256]{1,0:T(8,128)}, u32[]{:S(2)}) copy-start(f32[256,256]{1,0:T(8,128)} %copy-done.7) | copy-start | bytes 786436
where the time goes:
time: 94.3 us; the launch traced here: 93.8 us
  Pallas kernels  46.2 us (49%)
  starting transfers between devices  18.2 us (19%)
  waiting for transfers between devices  12.8 us (14%)
  local copies, waits for them, and re-layouts  9.34 us (10%)
  other arithmetic  3.63 us (4%)
  between operations  3.56 us (4%)
    pallas_call x1, Pallas kernels, main_call(): pl.pallas_call(main_kernel, out_shape=(out, out), in_specs=[pl.BlockSpec(...  33.3 us
    ppermute x10, starting transfers between devices, send(): return lax.ppermute(x, axis, [(i, step(i)) for i in range(count)])  18.2 us
    pallas_call x1, Pallas kernels, own_call(): pl.pallas_call(own_kernel, out_shape=(square,) * 3, in_specs=[pl.BlockSpe...  12.9 us
    ppermute x10, waiting for transfers between devices, send(): return lax.ppermute(x, axis, [(i, step(i)) for i in range(count)])  12.8 us
    unnamed x21, local copies, waits for them, and re-layouts  9.25 us
  transfers between devices with their start and end apart: 10, of which 3 were waited for; matrix products, arithmetic and copies ran while one was open for 5% of the time, Pallas kernels for 14%

commit v1 on v0

v1 whole, which is shorter than its diff:
```python
import math

import jax
import jax.numpy as jnp
from jax import lax
from jax.experimental import pallas as pl
from jax.experimental.pallas import tpu as pltpu
from jax.sharding import PartitionSpec as P

F32 = jnp.float32
BF16 = jnp.bfloat16
HIGH = lax.Precision.HIGHEST
CHUNK = 896
TOLERANCE = 3e-4
SHIFTS = (0, 1, 3, 2)
VMEM_LIMIT = 60 * 1024 * 1024


def nn(a, b, precision=HIGH):
    return lax.dot_general(a, b, (((1,), (0,)), ((), ())), precision=precision, preferred_element_type=F32)


def nt(a, b, precision=HIGH):
    return lax.dot_general(a, b, (((1,), (1,)), ((), ())), precision=precision, preferred_element_type=F32)


def tn(a, b, precision=None):
    return lax.dot_general(a, b, (((0,), (0,)), ((), ())), precision=precision, preferred_element_type=F32)


def lane_splat(x, lane):
    return jnp.broadcast_to(x[:, lane : lane + 1], x.shape)


def row_splat(x, row):
    return jnp.broadcast_to(x[row : row + 1, :], x.shape)


def total(terms):
    while len(terms) > 1:
        terms = [terms[k] + terms[k + 1] if k + 1 < len(terms) else terms[k] for k in range(0, len(terms), 2)]
    return terms[0]


def leaf(block):
    count = 8
    rows = [block[8 * r : 8 * r + 8, :] for r in range(count)]
    sub = lax.broadcasted_iota(jnp.int32, (8, 128), 0)
    diag = [lane_splat(rows[0], 64 + m) for m in range(8)]
    for b in range(count):
        more = b + 1 < count
        x = rows[b]
        if more:
            ahead = rows[b + 1]
            side = [lane_splat(ahead, 64 + 8 * b + m) for m in range(8)]
            following = [lane_splat(ahead, 72 + 8 * b + m) for m in range(8)]
        far = {r: [lane_splat(rows[r], 64 + 8 * b + m) for m in range(8)] for r in range(b + 2, count)}
        inverse, pivot_rows, low = [], [], []
        pivots = diag[0]
        for k in range(8):
            r = 1.0 / row_splat(diag[k], k)
            inverse.append(r)
            if k:
                pivots = jnp.where(sub == k, diag[k], pivots)
            below = jnp.where(sub > k, diag[k], 0.0)
            low.append(below)
            pivot = row_splat(x, k) * r
            pivot_rows.append(pivot)
            for m in range(k + 1, 8):
                entry = row_splat(diag[m], k)
                diag[m] = diag[m] - (below * entry) * r
                if more:
                    side[m] = side[m] - side[k] * (entry * r)
            x = x - below * pivot
            if more:
                ahead = ahead - side[k] * pivot
        if more:
            scaled = [side[k] * inverse[k] for k in range(8)]
            diag = [
                following[m] - total([scaled[k] * row_splat(side[k], m) for k in range(8)]) for m in range(8)
            ]
            rows[b + 1] = ahead
        if far:
            back = [None] * 8
            for k in range(7, -1, -1):
                column = low[k] * inverse[k]
                back[k] = pivot_rows[k]
                for i in range(k + 1, 8):
                    back[k] = back[k] - row_splat(column, i) * back[i]
            for r in far:
                rows[r] = rows[r] - total([far[r][m] * back[m] for m in range(8)])
        rows[b] = x * lax.rsqrt(pivots)
    return jnp.concatenate(rows, axis=0)


def shifted(pair):
    lane = lax.broadcasted_iota(jnp.int32, pair.shape, 1)
    return jnp.where(lane >= 64, pltpu.roll(pair, 64, 1), 0.0)


def spread(matrix, aug_ref):
    size = matrix.shape[0]
    lane = lax.broadcasted_iota(jnp.int32, (size, 128), 1)
    row = lax.broadcasted_iota(jnp.int32, (size, 128), 0)
    for k in range(size // 64):
        half = matrix[:, 128 * (k // 2) : 128 * (k // 2) + 128]
        if k % 2 == 0:
            half = pltpu.roll(half, 64, 1)
        eye = (row == lane + 64 * k).astype(F32)
        aug_ref[:, 128 * k : 128 * k + 128] = jnp.where(lane >= 64, half, eye)


def gather_inverse(aug_ref):
    lane = lax.broadcasted_iota(jnp.int32, (aug_ref.shape[0], 128), 1)
    parts = []
    for t in range(aug_ref.shape[1] // 256):
        even = aug_ref[:, 256 * t : 256 * t + 128]
        odd = aug_ref[:, 256 * t + 128 : 256 * t + 256]
        parts.append(jnp.where(lane < 64, even, pltpu.roll(odd, 64, 1)))
    return jnp.concatenate(parts, axis=1)


def factor(aug_ref, low_refs=None):
    size = aug_ref.shape[0]
    count = size // 64
    start = aug_ref[:64, :128]
    for k in range(count):
        here = slice(64 * k, 64 * k + 64)
        tile = slice(128 * k, 128 * k + 128)
        pair = leaf(start)
        wide = shifted(pair)
        inverse = pair[:, :64]
        if low_refs is not None:
            low_refs[k][here, :] = nt(start, wide)
        if k + 1 == count:
            aug_ref[here, :] = nn(inverse, aug_ref[here, :])
            break
        below = slice(64 * k + 64, 64 * k + 128)
        after = slice(128 * k + 128, 128 * k + 256)
        near = nt(aug_ref[below, tile], wide)
        start = aug_ref[below, after] - nn(near, nn(inverse, aug_ref[here, after]))
        ahead = nn(inverse, aug_ref[here, :])
        left = nt(aug_ref[64 * k + 64 :, tile], wide)
        aug_ref[here, :] = ahead
        if low_refs is not None:
            low_refs[k][64 * k + 64 :, :] = left
        aug_ref[64 * k + 64 :, :] = aug_ref[64 * k + 64 :, :] - nn(left, ahead)


def masked_gram(gram, rank):
    size = gram.shape[0]
    row = lax.broadcasted_iota(jnp.int32, gram.shape, 0)
    col = lax.broadcasted_iota(jnp.int32, gram.shape, 1)
    both = (row < rank) & (col < rank)
    dead = (row == col) & (row >= rank)
    return jnp.where(both, gram, 0.0), dead.astype(F32)


def iota(shape, dim):
    return lax.broadcasted_iota(jnp.int32, shape, dim)


def halves(x):
    top = x.astype(BF16)
    return top, (x - top.astype(F32)).astype(BF16)


def lower_only(x):
    return jnp.where(iota(x.shape, 0) >= iota(x.shape, 1), x, 0.0)


def copy_all(pairs, sem):
    copies = [pltpu.make_async_copy(source, target, sem.at[k]) for k, (source, target) in enumerate(pairs)]
    for copy in copies:
        copy.start()
    return copies


def own_kernel(
    ranks, sketch_hbm, tile_u_hbm, tile_v_hbm,
    low_inv_hbm, sketch_t_hbm, y_hbm, x_hbm,
    sketch, tile_u, tile_v, aug_ref, low0, low1, low2, low3, low_inv, sketch_t, y_ref, x_ref,
    in_sem, out_sem,
):
    loads = copy_all([(tile_v_hbm, tile_v), (tile_u_hbm, tile_u), (sketch_hbm, sketch)], in_sem)
    rank = ranks[0]
    loads[0].wait()
    gram_v, dead = masked_gram(tn(tile_v[...], tile_v[...]), rank)
    spread(gram_v + dead, aug_ref)
    loads[1].wait()
    gram_u, unused = masked_gram(tn(tile_u[...], tile_u[...]), rank)
    loads[2].wait()
    flipped = sketch[...].T
    flipped = jnp.where(iota(flipped.shape, 0) < ranks[3], flipped, 0.0)
    sketch_t[...] = flipped
    lows = (low0, low1, low2, low3)
    factor(aug_ref, lows)
    low_inv[...] = gather_inverse(aug_ref)
    for k in range(1, 4):
        lows[k][: 64 * k, :] = jnp.zeros((64 * k, 64), F32)
    low = lower_only(jnp.concatenate([ref[...] for ref in lows], axis=1))
    y = jnp.where(iota((256, 256), 1) < rank, nt(flipped[:, :256], low), 0.0)
    y_ref[...] = y
    x_ref[...] = nn(y, gram_u)
    stores = copy_all([(low_inv, low_inv_hbm), (sketch_t, sketch_t_hbm), (y_ref, y_hbm), (x_ref, x_hbm)], out_sem)
    for store in stores:
        store.wait()


def own_call(ranks, sketch, tile_u, tile_v):
    square = jax.ShapeDtypeStruct((256, 256), F32)
    wide = pltpu.VMEM(tile_u.shape, BF16)
    block = pltpu.VMEM((256, 256), F32)
    hbm = pl.BlockSpec(memory_space=pl.ANY)
    return pl.pallas_call(
        own_kernel,
        out_shape=(square, jax.ShapeDtypeStruct((256, 320), F32), square, square),
        in_specs=[pl.BlockSpec(memory_space=pltpu.SMEM)] + [hbm] * 3,
        out_specs=(hbm,) * 4,
        scratch_shapes=[pltpu.VMEM((320, 256), F32), wide, wide, pltpu.VMEM((256, 512), F32)]
        + [pltpu.VMEM((256, 64), F32)] * 4
        + [block, pltpu.VMEM((256, 320), F32), block, block, pltpu.SemaphoreType.DMA((3,)), pltpu.SemaphoreType.DMA((4,))],
        compiler_params=pltpu.CompilerParams(vmem_limit_bytes=VMEM_LIMIT),
        cost_estimate=pl.CostEstimate(flops=14 * 10**9, bytes_accessed=4 * 10**6, transcendentals=0),
        name="own_factor",
    )(ranks, sketch, tile_u, tile_v)


def side_copies(ranks, sides, target, sem, base):
    block = sides[0].shape[1]
    z, y_half = ranks[6], ranks[8]
    copies = []
    for hop, side in enumerate(sides):
        for k in range(2):
            start = (lax.rem(z - SHIFTS[hop] + 4, 4) * 2 + lax.rem(y_half + k, 2)) * block
            spot = pl.ds(pl.multiple_of(start, block), block)
            copies.append(pltpu.make_async_copy(side.at[k], target.at[spot, :], sem.at[base + 2 * hop + k]))
    return copies


def side_kernel(
    ranks, low_inv_hbm, sketch_t_hbm, tile_v_hbm, side0, side1, side2, side3,
    y_hbm,
    low_inv, sketch_t, tile_v, col_uv, y_ref, in_sem, out_sem,
):
    loads = side_copies(ranks, (side0, side1, side2, side3), col_uv, in_sem, 3)
    loads.append(pltpu.make_async_copy(tile_v_hbm, tile_v, in_sem.at[2]))
    small = [
        pltpu.make_async_copy(low_inv_hbm, low_inv, in_sem.at[0]),
        pltpu.make_async_copy(sketch_t_hbm, sketch_t, in_sem.at[1]),
    ]
    for load in loads + small:
        load.start()
    for load in loads:
        load.wait()
    t_rank, j_rank = ranks[0], ranks[2]
    both = col_uv[...]
    keep = (iota((64, 256), 0) < j_rank) & (iota((64, 256), 1) < t_rank)
    side = jnp.where(keep, -tn(both, tile_v[...])[:64], 0.0)
    corner, dead = masked_gram(tn(both, both)[:64, :64], j_rank)
    for load in small:
        load.wait()
    low_pt = nt(side, low_inv[...])
    schur = corner + dead - nt(low_pt, low_pt)
    eye = (iota((64, 64), 0) == iota((64, 64), 1)).astype(F32)
    start = jnp.concatenate([eye, schur], axis=1)
    low_pp = lower_only(nt(start, shifted(leaf(start))))
    y = nt(sketch_t[:, :256], low_pt) + nt(sketch_t[:, 256:], low_pp)
    y_ref[...] = jnp.where(iota((256, 64), 1) < j_rank, y, 0.0)
    store = pltpu.make_async_copy(y_ref, y_hbm, out_sem)
    store.start()
    store.wait()


def side_call(ranks, low_inv, sketch_t, tile_v, sides):
    hbm = pl.BlockSpec(memory_space=pl.ANY)
    rows = tile_v.shape[0]
    return pl.pallas_call(
        side_kernel,
        out_shape=jax.ShapeDtypeStruct((256, 64), F32),
        in_specs=[pl.BlockSpec(memory_space=pltpu.SMEM)] + [hbm] * 7,
        out_specs=hbm,
        scratch_shapes=[
            pltpu.VMEM((256, 256), F32), pltpu.VMEM((256, 320), F32), pltpu.VMEM((rows, 256), BF16),
            pltpu.VMEM((rows, 128), BF16), pltpu.VMEM((256, 64), F32),
            pltpu.SemaphoreType.DMA((11,)), pltpu.SemaphoreType.DMA,
        ],
        compiler_params=pltpu.CompilerParams(vmem_limit_bytes=VMEM_LIMIT),
        cost_estimate=pl.CostEstimate(flops=5 * 10**9, bytes_accessed=2 * 10**6, transcendentals=0),
        name="side_factor",
    )(ranks, low_inv, sketch_t, tile_v, *sides)


def main_kernel(
    ranks, y_t_hbm, x_t_hbm, y_p_hbm, tile_u_hbm, tile_v_hbm,
    mine0, mine1, mine2, mine3, other0, other1, other2, other3, side0, side1, side2, side3,
    out_u_hbm, out_v_hbm,
    y_t, x_t, y_p, tile_u, tile_v, panel, col_uv, up, wide_u, out_u, out_v, aug_ref, w_t, w_p, g_t, g_p,
    in_sem, out_sem,
):
    rows = tile_u.shape[0]
    t_rank, i_rank, j_rank, s_rank = ranks[0], ranks[1], ranks[2], ranks[3]
    core, y_low, x = ranks[4], ranks[5], ranks[7]
    side_loads = side_copies(ranks, (side0, side1, side2, side3), col_uv, in_sem, 0)
    row_loads = []
    block = mine0.shape[1]
    for which, arrays in enumerate(((mine0, mine1, mine2, mine3), (other0, other1, other2, other3))):
        slot = lax.rem(core + which, 2)
        for hop in range(4):
            for k in range(2):
                start = (lax.rem(y_low + k, 2) * 4 + lax.rem(x - SHIFTS[hop] + 4, 4)) * block
                spot = pl.ds(pl.multiple_of(start, block), block)
                sem = in_sem.at[8 + 8 * which + 2 * hop + k]
                row_loads.append(pltpu.make_async_copy(arrays[hop].at[k], panel.at[slot, spot, :], sem))
    load_u = pltpu.make_async_copy(tile_u_hbm, tile_u, in_sem.at[24])
    small = [
        pltpu.make_async_copy(source, target, in_sem.at[26 + k])
        for k, (source, target) in enumerate([(y_t_hbm, y_t), (x_t_hbm, x_t), (y_p_hbm, y_p)])
    ]
    load_v = pltpu.make_async_copy(tile_v_hbm, tile_v, in_sem.at[25])
    for load in side_loads + row_loads + [load_u] + small + [load_v]:
        load.start()
    for load in side_loads + row_loads:
        load.wait()
    keep = (iota((64, 256), 0) < j_rank) & (iota((64, 256), 1) < i_rank)
    cross_t = jnp.where(keep, tn(col_uv[...], panel[1])[64:], 0.0).astype(BF16)
    for step in range(rows // CHUNK):
        here = slice(step * CHUNK, step * CHUNK + CHUNK)
        top, rest = halves(nt(panel[0, here, :], cross_t, None))
        up[here, :] = jnp.concatenate([top, rest, top, rest], axis=1)
        part = col_uv[here, :][:, :64]
        wide_u[here, :] = jnp.concatenate([part, part], axis=1)
    load_u.wait()
    both = tn(up[:, :128], tile_u[...])
    keep = (iota((64, 256), 0) < j_rank) & (iota((64, 256), 1) < t_rank)
    gram_pt = jnp.where(keep, both[:64] + both[64:], 0.0)
    four = tn(up[:, :128], up[:, :128])
    four = four[:64] + four[64:]
    gram_pp = (four + pltpu.roll(four, 64, 1))[:, :64]
    for load in small:
        load.wait()
    ys, yp = y_t[...], y_p[...]
    xs = x_t[...] + nn(yp, gram_pt)
    xp = nt(ys, gram_pt) + nn(yp, gram_pp)
    same = iota((256, 256), 0) == iota((256, 256), 1)
    dead = (same & (iota((256, 256), 0) >= s_rank)).astype(F32)
    spread(nt(xs, ys) + nt(xp, yp) + dead, aug_ref)
    factor(aug_ref)
    inverse = gather_inverse(aug_ref)
    w_t[...] = nn(inverse, ys)
    w_p[...] = nn(inverse, yp)
    g_t[...] = nn(inverse, xs)
    g_p[...] = nn(inverse, xp)
    live = (same & (iota((256, 256), 0) < s_rank)).astype(F32)

    def refine(state):
        count, unused = state
        error = nt(w_t[...], g_t[...]) + nt(w_p[...], g_p[...]) - live
        size = jnp.max(jnp.sum(jnp.abs(error), axis=1, keepdims=True))
        step = lower_only(error) - jnp.where(same, 0.5 * error, 0.0)
        for ref in (w_t, w_p, g_t, g_p):
            ref[...] = ref[...] - nn(step, ref[...])
        return count + 1, size

    lax.while_loop(lambda s: (s[0] < 12) & (s[1] > TOLERANCE), refine, (jnp.int32(0), jnp.float32(1.0)))
    scale = math.sqrt(rows)
    u_hi, u_lo = halves(w_t[...] * scale)
    p_hi, p_lo = halves(w_p[...] * scale)
    p_all = jnp.concatenate([p_hi, p_hi, p_lo, p_lo], axis=1)
    v_hi, v_lo = halves(g_t[...])
    q_all = jnp.concatenate(halves(-g_p[...]), axis=1)
    load_v.wait()
    stores = []
    for step in range(rows // CHUNK):
        here = slice(step * CHUNK, step * CHUNK + CHUNK)
        tile = tile_u[here, :]
        out_u[here, :] = nt(tile, u_hi, None) + nt(tile, u_lo, None) + nt(up[here, :], p_all, None)
        tile = tile_v[here, :]
        stores.append(pltpu.make_async_copy(out_u.at[here, :], out_u_hbm.at[here, :], out_sem.at[0, step]))
        stores[-1].start()
        out_v[here, :] = nt(tile, v_hi, None) + nt(tile, v_lo, None) + nt(wide_u[here, :], q_all, None)
        stores.append(pltpu.make_async_copy(out_v.at[here, :], out_v_hbm.at[here, :], out_sem.at[1, step]))
        stores[-1].start()
    for store in stores:
        store.wait()


def main_call(ranks, y_t, x_t, y_p, tile_u, tile_v, mine, other, sides):
    rows = tile_u.shape[0]
    hbm = pl.BlockSpec(memory_space=pl.ANY)
    out = jax.ShapeDtypeStruct((rows, 256), F32)
    block = pltpu.VMEM((256, 256), F32)
    thin = pltpu.VMEM((256, 64), F32)
    wide = pltpu.VMEM((rows, 256), BF16)
    half = pltpu.VMEM((rows, 128), BF16)
    result = pltpu.VMEM((rows, 256), F32)
    return pl.pallas_call(
        main_kernel,
        out_shape=(out, out),
        in_specs=[pl.BlockSpec(memory_space=pltpu.SMEM)] + [hbm] * 17,
        out_specs=(hbm, hbm),
        scratch_shapes=[
            block, block, thin, wide, wide, pltpu.VMEM((2, rows, 256), BF16), half, wide, half, result, result,
            pltpu.VMEM((256, 512), F32), block, thin, block, thin,
            pltpu.SemaphoreType.DMA((29,)), pltpu.SemaphoreType.DMA((2, rows // CHUNK)),
        ],
        compiler_params=pltpu.CompilerParams(vmem_limit_bytes=VMEM_LIMIT),
        cost_estimate=pl.CostEstimate(flops=20 * 10**9, bytes_accessed=15 * 10**6, transcendentals=0),
        name="recompress",
    )(ranks, y_t, x_t, y_p, tile_u, tile_v, *mine, *other, *sides)


def send(x, axis, count, step):
    return lax.ppermute(x, axis, [(i, step(i)) for i in range(count)])


def body(tile_u, tile_v, row_u, row_v, col_u, col_v, tile_rank, row_rank, col_rank, target_rank, sketch):
    spot_i, spot_j = lax.axis_index("row"), lax.axis_index("col")
    core, x, y_low = spot_j % 2, spot_j // 2 % 4, spot_j // 8
    z, y_half = spot_i // 2, spot_i % 2
    first = core == 0
    own_u, own_v = tile_u[0, 0], tile_v[0, 0]
    numbers = [tile_rank[0, 0], row_rank[0], col_rank[0], target_rank[0, 0], core, y_low, z, x, y_half]
    ranks = jnp.stack(numbers).astype(jnp.int32)
    side = jnp.concatenate([col_u[0], col_v[0]], axis=1)
    side_other = send(side, "row", 8, lambda i: i ^ 1)
    give = jnp.where(first, row_v[0], row_u[0])
    keep = jnp.where(first, row_u[0], row_v[0])
    got = send(give, "col", 16, lambda i: i ^ 1)
    chip = jnp.concatenate([jnp.where(first, keep, got), jnp.where(first, got, keep)], axis=0)
    chip_other = send(chip, "col", 16, lambda i: i ^ 8)
    side_other, chip_other, own_u, own_v = lax.optimization_barrier((side_other, chip_other, own_u, own_v))
    sides = [jnp.stack([side, side_other])]
    mine = [jnp.stack([chip, chip_other])]
    for shift in SHIFTS[1:]:
        mine.append(send(mine[0], "col", 16, lambda i: i // 8 * 8 + (i + 2 * shift) % 8))
    for shift in SHIFTS[1:]:
        sides.append(send(sides[0], "row", 8, lambda i: (i + 2 * shift) % 8))
    low_inv, sketch_t, y_t, x_t = own_call(ranks, sketch, own_u, own_v)
    low_inv, mine, sides = lax.optimization_barrier((low_inv, mine, sides))
    other = [send(piece, "col", 16, lambda i: i ^ 1) for piece in mine]
    y_p = side_call(ranks, low_inv, sketch_t, own_v, sides)
    new_u, new_v = main_call(ranks, y_t, x_t, y_p, own_u, own_v, mine, other, sides)
    return (new_u[None, None], new_v[None, None])


def solution(mesh):
    placed = (
        P("row", "col", None, None),
        P("row", "col", None, None),
        P("row", "col", None),
        P("row", "col", None),
        P("col", "row", None),
        P("col", "row", None),
        P("row", "col"),
        P("row"),
        P("col"),
        P("row", "col"),
        P(),
    )
    return jax.shard_map(
        body,
        mesh=mesh,
        in_specs=placed,
        out_specs=(P("row", "col", None, None), P("row", "col", None, None)),
        check_vma=False,
    )
```

time: 94.3 us -> 75.2 us (0.80)
  local copies, waits for them, and re-layouts: 9.34 us -> 3.56 us
  waiting for transfers between devices: 12.8 us -> 7.27 us
  Pallas kernels: 46.2 us -> 40.9 us
  other arithmetic: 3.63 us -> 2.11 us
  starting transfers between devices: 18.2 us -> 17.1 us
    pallas_call x1, Pallas kernels: 33.3 us -> 21 us  [main_call(): pl.pallas_call(main_kernel, out_shape=(out, out), in_specs=[pl.BlockSpec(...]
    pallas_call x1 -> x2, Pallas kernels: 12.9 us -> 19.9 us  [the longest x1 13 us: own_call(): pl.pallas_call(own_kernel, out_shape=(square, jax.ShapeDtypeStruct((256,...]
    unnamed x21 -> x26, local copies, waits for them, and re-layouts: 9.25 us -> 2.89 us
    ppermute x10 -> x13, waiting for transfers between devices: 12.8 us -> 7.27 us  [send(): return lax.ppermute(x, axis, [(i, step(i)) for i in range(count)])]
    another operation x3 -> x2, other arithmetic: 1.58 us -> 0.06 us  [body(): mine = [jnp.stack([chip, chip_other])]]
    ppermute x10 -> x13, starting transfers between devices: 18.2 us -> 17.1 us  [send(): return lax.ppermute(x, axis, [(i, step(i)) for i in range(count)])]
  transfers between devices with their start and end apart: 10 -> 13, of which waited for: 3 -> 3; matrix products, arithmetic and copies ran while one was open for 5% -> 4% of each run, Pallas kernels for 14% -> 27%
where the time goes in v1:
time: 75.2 us; the launch traced here: 74.7 us
  Pallas kernels  40.9 us (54%)
  starting transfers between devices  17.1 us (23%)
  waiting for transfers between devices  7.27 us (10%)
  between operations  3.66 us (5%)
  local copies, waits for them, and re-layouts  3.56 us (5%)
  other arithmetic  2.11 us (3%)
    pallas_call x1, Pallas kernels, main_call(): pl.pallas_call(main_kernel, out_shape=(out, out), in_specs=[pl.BlockSpec(...  21 us
    ppermute x13, starting transfers between devices, send(): return lax.ppermute(x, axis, [(i, step(i)) for i in range(count)])  17.1 us
    pallas_call x1, Pallas kernels, own_call(): pl.pallas_call(own_kernel, out_shape=(square, jax.ShapeDtypeStruct((256,...  13 us
    ppermute x13, waiting for transfers between devices, send(): return lax.ppermute(x, axis, [(i, step(i)) for i in range(count)])  7.27 us
    pallas_call x1, Pallas kernels, side_call(): pl.pallas_call(side_kernel, out_shape=jax.ShapeDtypeStruct((256, 64), F32...  6.85 us
    unnamed x26, local copies, waits for them, and re-layouts  2.89 us
  transfers between devices with their start and end apart: 13, of which 3 were waited for; matrix products, arithmetic and copies ran while one was open for 4% of the time, Pallas kernels for 27%

profile of v1, /device:TPU:1, one launch (start us, length us, event | category | flops | bytes accessed | tf_op | source)
XLA Modules:
  0.0 74.7 jit_solution(12719750986289514216)
XLA Ops:
  0.6 0.9 %select_bitcast_fusion = bf16[168,256]{1,0:T(8,128)(2,1)S(1)} fusion(bf16[1,168,256]{2,1,0:T(8,128)(2,1)} %param.14, bf16[1,168,256]{2,1,0:T(8,128)(2,1)} %param.13, pred[]{:T(512)S(6)} %eq.7), kind=kLoop, calls=%fused_computation.6 | loop fusion | flops 43008 | bytes 258049 | tf_op jit(solution)/shard_map/jit(_where)/select_n | solution.py:427
  1.6 1.5 %collective-permute-start.1 = (bf16[168,256]{1,0:T(8,128)(2,1)S(1)}, bf16[168,256]{1,0:T(8,128)(2,1)S(1)}, u32[]{:S(2)}, u32[]{:S(2)}) collective-permute-start(bf16[168,256]{1,0:T(8,128)(2,1)S(1)} %select_bitcast_fusion), channel_id=1, source_target_pairs={{0,1},{1,0},{2,3},{3,2},{4,5},{5,4},{6,7},{7,6},{8,9},{9,8},{10,11... | collective-permute-start | bytes 258056 | tf_op jit(solution)/shard_map/ppermute | solution.py:414
  3.1 0.9 %copy.13 = bf16[1,336,64]{2,1,0:T(8,128)(2,1)S(1)} copy(bf16[1,336,64]{1,2,0:T(8,128)(2,1)} %param.15) | data formatting | bytes 86016 | tf_op args[4]
  4.0 0.9 %copy.14 = bf16[1,336,64]{2,1,0:T(8,128)(2,1)S(1)} copy(bf16[1,336,64]{1,2,0:T(8,128)(2,1)} %param.16) | data formatting | bytes 86016 | tf_op args[5]
  4.9 0.0 collective-permute-done.1
  4.9 0.9 %bitcast_select_fusion.1 = (bf16[168,256]{1,0:T(8,128)(2,1)S(1)}, bf16[168,256]{1,0:T(8,128)(2,1)S(1)}) fusion(bf16[168,256]{1,0:T(8,128)(2,1)S(1)} %collective-permute-done.1, pred[]{:T(512)S(6)} %eq.7, bf16[1,168,256]{2,1,0:T(8,128)(2,1)} %param.13, bf16[1,168,256]{2,1,0:T(8,128)(2,1)} %param.14), kind=kLoop, calls=%fused_computation.5 | loop fusion | flops 129024 | bytes 430081 | tf_op jit(solution)/shard_map/jit(_where)/select_n | solution.py:430
  5.9 1.5 %collective-permute-start.2 = (bf16[336,256]{1,0:T(8,128)(2,1)S(1)}, bf16[336,256]{1,0:T(8,128)(2,1)S(1)}, u32[]{:S(2)}, u32[]{:S(2)}) collective-permute-start(bf16[336,256]{1,0:T(8,128)(2,1)S(1)} %get-tuple-element.43), channel_id=1, source_target_pairs={{0,8},{1,9},{2,10},{3,11},{4,12},{5,13},{6,14},{7,15},{8,0},{9,1},... | collective-permute-start | bytes 516104 | tf_op jit(solution)/shard_map/ppermute | solution.py:414
  7.3 0.1 pad_maximum_fusion.3
  7.4 2.7 %collective-permute-start = (bf16[336,128]{1,0:T(8,128)(2,1)S(1)}, bf16[336,128]{1,0:T(8,128)(2,1)S(1)}, u32[]{:S(2)}, u32[]{:S(2)}) collective-permute-start(bf16[336,128]{1,0:T(8,128)(2,1)S(1)} %pad_maximum_fusion.3), channel_id=1, source_target_pairs={{0,16},{16,0},{32,48},{48,32},{64,80},{80,64},{96,112},{112,96},{1... | collective-permute-start | bytes 258056 | tf_op jit(solution)/shard_map/ppermute | solution.py:414
  10.1 0.1 fusion.1
  10.2 6.1 %collective-permute-done = bf16[336,128]{1,0:T(8,128)(2,1)S(1)} collective-permute-done((bf16[336,128]{1,0:T(8,128)(2,1)S(1)}, bf16[336,128]{1,0:T(8,128)(2,1)S(1)}, u32[]{:S(2)}, u32[]{:S(2)}) %collective-permute-start) | collective-permute-done | bytes 86048 | tf_op jit(solution)/shard_map/ppermute | solution.py:414
  16.3 0.0 collective-permute-done.2
  16.3 0.0 copy-start.1
  16.4 3.7 %collective-permute-start.8 = (bf16[2,336,128]{2,1,0:T(8,128)(2,1)S(1)}, bf16[2,336,128]{2,1,0:T(8,128)(2,1)S(1)}, u32[]{:S(2)}, u32[]{:S(2)}) collective-permute-start(bf16[2,336,128]{2,1,0:T(8,128)(2,1)S(1)} %pad_maximum_fusion.2.side0), channel_id=1, source_target_pairs={{0,64},{16,80},{32,96},{48,112},{64,0},{80,16},{96,32},{112,48},{1... | collective-permute-start | bytes 516104 | tf_op jit(solution)/shard_map/ppermute | solution.py:414
  22.6 0.7 stack.41.ranks
  23.3 0.4 collective-permute-start.7
  23.7 1.0 %collective-permute-start.6 = (bf16[2,336,128]{2,1,0:T(8,128)(2,1)S(1)}, bf16[2,336,128]{2,1,0:T(8,128)(2,1)S(1)}, u32[]{:S(2)}, u32[]{:S(2)}) collective-permute-start(bf16[2,336,128]{2,1,0:T(8,128)(2,1)S(1)} %pad_maximum_fusion.2.side0), channel_id=1, source_target_pairs={{0,32},{16,48},{32,64},{48,80},{64,96},{80,112},{96,0},{112,16},{1... | collective-permute-start | bytes 516104 | tf_op jit(solution)/shard_map/ppermute | solution.py:414
  24.8 0.0 copy-start
  24.8 2.8 %collective-permute-start.5 = (bf16[2,336,256]{2,1,0:T(8,128)(2,1)S(1)}, bf16[2,336,256]{2,1,0:T(8,128)(2,1)S(1)}, u32[]{:S(2)}, u32[]{:S(2)}) collective-permute-start(bf16[2,336,256]{2,1,0:T(8,128)(2,1)S(1)} %pad_maximum_fusion.mine0), channel_id=1, source_target_pairs={{0,4},{1,5},{2,6},{3,7},{4,0},{5,1},{6,2},{7,3},{8,12},{9,13},{10,... | collective-permute-start | bytes 1032200 | tf_op jit(solution)/shard_map/ppermute | solution.py:414
  27.6 0.9 %collective-permute-start.4 = (bf16[2,336,256]{2,1,0:T(8,128)(2,1)S(1)}, bf16[2,336,256]{2,1,0:T(8,128)(2,1)S(1)}, u32[]{:S(2)}, u32[]{:S(2)}) collective-permute-start(bf16[2,336,256]{2,1,0:T(8,128)(2,1)S(1)} %pad_maximum_fusion.mine0), channel_id=1, source_target_pairs={{0,6},{1,7},{2,0},{3,1},{4,2},{5,3},{6,4},{7,5},{8,14},{9,15},{10,... | collective-permute-start | bytes 1032200 | tf_op jit(solution)/shard_map/ppermute | solution.py:414
  28.5 0.0 collective-permute-done.8.side3
  28.5 0.6 collective-permute-start.3
  29.1 13.0 %own_factor.1 = (f32[256,256]{1,0:T(8,128)}, f32[256,320]{1,0:T(8,128)}, f32[256,256]{1,0:T(8,128)}, f32[256,256]{1,0:T(8,128)}) custom-call(s32[9]{0:T(128)} %stack.41.ranks, f32[320,256]{1,0:T(8,128)} %sketch_hbm.1, bf16[2688,256]{1,0:T(8,128)(2,1)} %bitcast.32, bf16[2688,256]{1,0:T(8,128)(2,1)} %bitcast.34), custom_call_target="tpu_custom_call" | custom-call | flops 14000000000 | bytes 4000000 | tf_op jit(solution)/shard_map/own_factor/pallas_call | solution.py:215
  42.2 0.0 copy-done.1
  42.2 0.0 copy-done.9
  42.2 0.0 collective-permute-done.7.side2
  42.2 0.0 copy-start.10
  42.2 0.0 collective-permute-done.6.side1
  42.2 0.0 copy-start.11
  42.2 0.0 collective-permute-done.5.mine3
  42.2 0.6 collective-permute-done.4.mine2
  42.8 0.6 collective-permute-done.3.mine1
  43.4 1.4 %collective-permute-start.9 = (bf16[2,336,256]{2,1,0:T(8,128)(2,1)S(1)}, bf16[2,336,256]{2,1,0:T(8,128)(2,1)S(1)}, u32[]{:S(2)}, u32[]{:S(2)}) collective-permute-start(bf16[2,336,256]{2,1,0:T(8,128)(2,1)S(1)} %pad_maximum_fusion.mine0), channel_id=1, source_target_pairs={{0,1},{1,0},{2,3},{3,2},{4,5},{5,4},{6,7},{7,6},{8,9},{9,8},{10,11... | collective-permute-start | bytes 1032200 | tf_op jit(solution)/shard_map/ppermute | solution.py:414
  44.8 0.1 collective-permute-start.10
  44.9 0.4 collective-permute-start.11
  45.4 0.1 collective-permute-start.12
  45.4 0.0 copy-done.11
  45.5 6.8 %side_factor.1.y_p_hbm = f32[256,64]{1,0:T(8,128)} custom-call(s32[9]{0:T(128)} %stack.41.ranks, f32[256,256]{1,0:T(8,128)} %get-tuple-element.28.low_inv_hbm, f32[256,320]{1,0:T(8,128)} %get-tuple-element.29.sketch_t_hbm, bf16[2688,256]{1,0:T(8,128)(2,1)} %bitcast.35, bf16[2,336,128]{2,1,0:T(8,128)(2,1)} %copy-done.1, bf16[2,336,128]{2,1,0:T(8,128)(2,1)} %copy-done.11, ...), custom_call_target="tpu_custom_call" | custom-call | flops 5000000000 | bytes 2000000 | tf_op jit(solution)/shard_map/side_factor/pallas_call | solution.py:278
  52.3 0.0 collective-permute-done.9.other0
  52.4 0.0 collective-permute-done.10.other1
  52.4 0.0 copy-start.6
  52.4 0.0 collective-permute-done.11.other2
  52.4 0.0 collective-permute-done.12.other3
  52.4 0.7 copy-done.5
  53.1 0.1 copy-done.6
  53.2 0.1 copy-done.7
  53.3 0.1 copy-done.8
  53.4 21.0 %recompress.1 = (f32[2688,256]{1,0:T(8,128)}, f32[2688,256]{1,0:T(8,128)}) custom-call(s32[9]{0:T(128)} %stack.41.ranks, f32[256,256]{1,0:T(8,128)} %get-tuple-element.23.y_t_hbm, f32[256,256]{1,0:T(8,128)} %get-tuple-element.24.x_t_hbm, f32[256,64]{1,0:T(8,128)} %side_factor.1.y_p_hbm, bf16[2688,256]{1,0:T(8,128)(2,1)} %bitcast.33, ...), custom_call_target="tpu_custom_call" | custom-call | flops 20000000000 | bytes 15000000 | tf_op jit(solution)/shard_map/recompress/pallas_call | solution.py:397
  (15 shorter events, 0.1 us)
Async XLA Ops:
  1.6 3.3 %collective-permute-start.1 = (bf16[168,256]{1,0:T(8,128)(2,1)S(1)}, bf16[168,256]{1,0:T(8,128)(2,1)S(1)}, u32[]{:S(2)}, u32[]{:S(2)}) collective-permute-start(bf16[168,256]{1,0:T(8,128)(2,1)S(1)} %select_bitcast_fusion), channel_id=1, source_target_pairs={{0,1},{1,0},{2,3},{3,2},{4,5},{5,4},{6,7},{7,6},{8,9},{9,8},{10,11... | collective-permute-start | bytes 258056 | tf_op jit(solution)/shard_map/ppermute | solution.py:414
  5.9 10.5 %collective-permute-start.2 = (bf16[336,256]{1,0:T(8,128)(2,1)S(1)}, bf16[336,256]{1,0:T(8,128)(2,1)S(1)}, u32[]{:S(2)}, u32[]{:S(2)}) collective-permute-start(bf16[336,256]{1,0:T(8,128)(2,1)S(1)} %get-tuple-element.43), channel_id=1, source_target_pairs={{0,8},{1,9},{2,10},{3,11},{4,12},{5,13},{6,14},{7,15},{8,0},{9,1},... | collective-permute-start | bytes 516104 | tf_op jit(solution)/shard_map/ppermute | solution.py:414
  7.4 8.9 %collective-permute-start = (bf16[336,128]{1,0:T(8,128)(2,1)S(1)}, bf16[336,128]{1,0:T(8,128)(2,1)S(1)}, u32[]{:S(2)}, u32[]{:S(2)}) collective-permute-start(bf16[336,128]{1,0:T(8,128)(2,1)S(1)} %pad_maximum_fusion.3), channel_id=1, source_target_pairs={{0,16},{16,0},{32,48},{48,32},{64,80},{80,64},{96,112},{112,96},{1... | collective-permute-start | bytes 258056 | tf_op jit(solution)/shard_map/ppermute | solution.py:414
  16.3 25.8 %copy-start.1 = (bf16[2,336,128]{2,1,0:T(8,128)(2,1)}, bf16[2,336,128]{2,1,0:T(8,128)(2,1)S(1)}, u32[]{:S(2)}) copy-start(bf16[2,336,128]{2,1,0:T(8,128)(2,1)S(1)} %pad_maximum_fusion.2.side0) | copy-start | bytes 516100
  16.4 12.2 %collective-permute-start.8 = (bf16[2,336,128]{2,1,0:T(8,128)(2,1)S(1)}, bf16[2,336,128]{2,1,0:T(8,128)(2,1)S(1)}, u32[]{:S(2)}, u32[]{:S(2)}) collective-permute-start(bf16[2,336,128]{2,1,0:T(8,128)(2,1)S(1)} %pad_maximum_fusion.2.side0), channel_id=1, source_target_pairs={{0,64},{16,80},{32,96},{48,112},{64,0},{80,16},{96,32},{112,48},{1... | collective-permute-start | bytes 516104 | tf_op jit(solution)/shard_map/ppermute | solution.py:414
  23.3 18.9 %collective-permute-start.7 = (bf16[2,336,128]{2,1,0:T(8,128)(2,1)S(1)}, bf16[2,336,128]{2,1,0:T(8,128)(2,1)S(1)}, u32[]{:S(2)}, u32[]{:S(2)}) collective-permute-start(bf16[2,336,128]{2,1,0:T(8,128)(2,1)S(1)} %pad_maximum_fusion.2.side0), channel_id=1, source_target_pairs={{0,96},{16,112},{32,0},{48,16},{64,32},{80,48},{96,64},{112,80},{1... | collective-permute-start | bytes 516104 | tf_op jit(solution)/shard_map/ppermute | solution.py:414
  23.7 18.5 %collective-permute-start.6 = (bf16[2,336,128]{2,1,0:T(8,128)(2,1)S(1)}, bf16[2,336,128]{2,1,0:T(8,128)(2,1)S(1)}, u32[]{:S(2)}, u32[]{:S(2)}) collective-permute-start(bf16[2,336,128]{2,1,0:T(8,128)(2,1)S(1)} %pad_maximum_fusion.2.side0), channel_id=1, source_target_pairs={{0,32},{16,48},{32,64},{48,80},{64,96},{80,112},{96,0},{112,16},{1... | collective-permute-start | bytes 516104 | tf_op jit(solution)/shard_map/ppermute | solution.py:414
  24.8 18.6 %copy-start = (bf16[2,336,256]{2,1,0:T(8,128)(2,1)}, bf16[2,336,256]{2,1,0:T(8,128)(2,1)S(1)}, u32[]{:S(2)}) copy-start(bf16[2,336,256]{2,1,0:T(8,128)(2,1)S(1)} %pad_maximum_fusion.mine0) | copy-start | bytes 1032196
  24.8 17.4 %collective-permute-start.5 = (bf16[2,336,256]{2,1,0:T(8,128)(2,1)S(1)}, bf16[2,336,256]{2,1,0:T(8,128)(2,1)S(1)}, u32[]{:S(2)}, u32[]{:S(2)}) collective-permute-start(bf16[2,336,256]{2,1,0:T(8,128)(2,1)S(1)} %pad_maximum_fusion.mine0), channel_id=1, source_target_pairs={{0,4},{1,5},{2,6},{3,7},{4,0},{5,1},{6,2},{7,3},{8,12},{9,13},{10,... | collective-permute-start | bytes 1032200 | tf_op jit(solution)/shard_map/ppermute | solution.py:414
  27.6 15.2 %collective-permute-start.4 = (bf16[2,336,256]{2,1,0:T(8,128)(2,1)S(1)}, bf16[2,336,256]{2,1,0:T(8,128)(2,1)S(1)}, u32[]{:S(2)}, u32[]{:S(2)}) collective-permute-start(bf16[2,336,256]{2,1,0:T(8,128)(2,1)S(1)} %pad_maximum_fusion.mine0), channel_id=1, source_target_pairs={{0,6},{1,7},{2,0},{3,1},{4,2},{5,3},{6,4},{7,5},{8,14},{9,15},{10,... | collective-permute-start | bytes 1032200 | tf_op jit(solution)/shard_map/ppermute | solution.py:414
  28.5 13.7 %copy-start.9 = (bf16[2,336,128]{2,1,0:T(8,128)(2,1)}, bf16[2,336,128]{2,1,0:T(8,128)(2,1)S(1)}, u32[]{:S(2)}) copy-start(bf16[2,336,128]{2,1,0:T(8,128)(2,1)S(1)} %collective-permute-done.8.side3) | copy-start | bytes 516100
  28.5 14.9 %collective-permute-start.3 = (bf16[2,336,256]{2,1,0:T(8,128)(2,1)S(1)}, bf16[2,336,256]{2,1,0:T(8,128)(2,1)S(1)}, u32[]{:S(2)}, u32[]{:S(2)}) collective-permute-start(bf16[2,336,256]{2,1,0:T(8,128)(2,1)S(1)} %pad_maximum_fusion.mine0), channel_id=1, source_target_pairs={{0,2},{1,3},{2,4},{3,5},{4,6},{5,7},{6,0},{7,1},{8,10},{9,11},{10,... | collective-permute-start | bytes 1032200 | tf_op jit(solution)/shard_map/ppermute | solution.py:414
  42.2 3.3 %copy-start.10 = (bf16[2,336,128]{2,1,0:T(8,128)(2,1)}, bf16[2,336,128]{2,1,0:T(8,128)(2,1)S(1)}, u32[]{:S(2)}) copy-start(bf16[2,336,128]{2,1,0:T(8,128)(2,1)S(1)} %collective-permute-done.7.side2) | copy-start | bytes 516100
  42.2 3.2 %copy-start.11 = (bf16[2,336,128]{2,1,0:T(8,128)(2,1)}, bf16[2,336,128]{2,1,0:T(8,128)(2,1)S(1)}, u32[]{:S(2)}) copy-start(bf16[2,336,128]{2,1,0:T(8,128)(2,1)S(1)} %collective-permute-done.6.side1) | copy-start | bytes 516100
  42.2 10.1 %copy-start.2 = (bf16[2,336,256]{2,1,0:T(8,128)(2,1)}, bf16[2,336,256]{2,1,0:T(8,128)(2,1)S(1)}, u32[]{:S(2)}) copy-start(bf16[2,336,256]{2,1,0:T(8,128)(2,1)S(1)} %collective-permute-done.5.mine3) | copy-start | bytes 1032196
  42.8 9.5 %copy-start.3 = (bf16[2,336,256]{2,1,0:T(8,128)(2,1)}, bf16[2,336,256]{2,1,0:T(8,128)(2,1)S(1)}, u32[]{:S(2)}) copy-start(bf16[2,336,256]{2,1,0:T(8,128)(2,1)S(1)} %collective-permute-done.4.mine2) | copy-start | bytes 1032196
  43.4 8.9 %copy-start.4 = (bf16[2,336,256]{2,1,0:T(8,128)(2,1)}, bf16[2,336,256]{2,1,0:T(8,128)(2,1)S(1)}, u32[]{:S(2)}) copy-start(bf16[2,336,256]{2,1,0:T(8,128)(2,1)S(1)} %collective-permute-done.3.mine1) | copy-start | bytes 1032196
  43.4 8.9 %collective-permute-start.9 = (bf16[2,336,256]{2,1,0:T(8,128)(2,1)S(1)}, bf16[2,336,256]{2,1,0:T(8,128)(2,1)S(1)}, u32[]{:S(2)}, u32[]{:S(2)}) collective-permute-start(bf16[2,336,256]{2,1,0:T(8,128)(2,1)S(1)} %pad_maximum_fusion.mine0), channel_id=1, source_target_pairs={{0,1},{1,0},{2,3},{3,2},{4,5},{5,4},{6,7},{7,6},{8,9},{9,8},{10,11... | collective-permute-start | bytes 1032200 | tf_op jit(solution)/shard_map/ppermute | solution.py:414
  44.8 7.5 %collective-permute-start.10 = (bf16[2,336,256]{2,1,0:T(8,128)(2,1)S(1)}, bf16[2,336,256]{2,1,0:T(8,128)(2,1)S(1)}, u32[]{:S(2)}, u32[]{:S(2)}) collective-permute-start(bf16[2,336,256]{2,1,0:T(8,128)(2,1)S(1)} %collective-permute-done.3.mine1), channel_id=1, source_target_pairs={{0,1},{1,0},{2,3},{3,2},{4,5},{5,4},{6,7},{7,6},{8,9},{9,8},{10,11... | collective-permute-start | bytes 1032200 | tf_op jit(solution)/shard_map/ppermute | solution.py:414
  44.9 7.4 %collective-permute-start.11 = (bf16[2,336,256]{2,1,0:T(8,128)(2,1)S(1)}, bf16[2,336,256]{2,1,0:T(8,128)(2,1)S(1)}, u32[]{:S(2)}, u32[]{:S(2)}) collective-permute-start(bf16[2,336,256]{2,1,0:T(8,128)(2,1)S(1)} %collective-permute-done.4.mine2), channel_id=1, source_target_pairs={{0,1},{1,0},{2,3},{3,2},{4,5},{5,4},{6,7},{7,6},{8,9},{9,8},{10,11... | collective-permute-start | bytes 1032200 | tf_op jit(solution)/shard_map/ppermute | solution.py:414
  45.4 7.0 %collective-permute-start.12 = (bf16[2,336,256]{2,1,0:T(8,128)(2,1)S(1)}, bf16[2,336,256]{2,1,0:T(8,128)(2,1)S(1)}, u32[]{:S(2)}, u32[]{:S(2)}) collective-permute-start(bf16[2,336,256]{2,1,0:T(8,128)(2,1)S(1)} %collective-permute-done.5.mine3), channel_id=1, source_target_pairs={{0,1},{1,0},{2,3},{3,2},{4,5},{5,4},{6,7},{7,6},{8,9},{9,8},{10,11... | collective-permute-start | bytes 1032200 | tf_op jit(solution)/shard_map/ppermute | solution.py:414
  52.3 0.7 copy-start.5
  52.4 0.8 %copy-start.6 = (bf16[2,336,256]{2,1,0:T(8,128)(2,1)}, bf16[2,336,256]{2,1,0:T(8,128)(2,1)S(1)}, u32[]{:S(2)}) copy-start(bf16[2,336,256]{2,1,0:T(8,128)(2,1)S(1)} %collective-permute-done.10.other1) | copy-start | bytes 1032196
  52.4 0.9 %copy-start.7 = (bf16[2,336,256]{2,1,0:T(8,128)(2,1)}, bf16[2,336,256]{2,1,0:T(8,128)(2,1)S(1)}, u32[]{:S(2)}) copy-start(bf16[2,336,256]{2,1,0:T(8,128)(2,1)S(1)} %collective-permute-done.11.other2) | copy-start | bytes 1032196
  52.4 1.0 %copy-start.8 = (bf16[2,336,256]{2,1,0:T(8,128)(2,1)}, bf16[2,336,256]{2,1,0:T(8,128)(2,1)S(1)}, u32[]{:S(2)}) copy-start(bf16[2,336,256]{2,1,0:T(8,128)(2,1)S(1)} %collective-permute-done.12.other3) | copy-start | bytes 1032196

commit v2 on v1

v2 whole, which is shorter than its diff:
```python
import math

import jax
import jax.numpy as jnp
from jax import lax
from jax.experimental import pallas as pl
from jax.experimental.pallas import tpu as pltpu
from jax.sharding import PartitionSpec as P

F32 = jnp.float32
BF16 = jnp.bfloat16
HIGH = lax.Precision.HIGHEST
CHUNK = 896
TOLERANCE = 3e-4
VMEM_LIMIT = 60 * 1024 * 1024


def nn(a, b, precision=HIGH):
    return lax.dot_general(a, b, (((1,), (0,)), ((), ())), precision=precision, preferred_element_type=F32)


def nt(a, b, precision=HIGH):
    return lax.dot_general(a, b, (((1,), (1,)), ((), ())), precision=precision, preferred_element_type=F32)


def tn(a, b, precision=None):
    return lax.dot_general(a, b, (((0,), (0,)), ((), ())), precision=precision, preferred_element_type=F32)


def lane_splat(x, lane):
    return jnp.broadcast_to(x[:, lane : lane + 1], x.shape)


def row_splat(x, row):
    return jnp.broadcast_to(x[row : row + 1, :], x.shape)


def total(terms):
    while len(terms) > 1:
        terms = [terms[k] + terms[k + 1] if k + 1 < len(terms) else terms[k] for k in range(0, len(terms), 2)]
    return terms[0]


def leaf(block):
    count = 8
    rows = [block[8 * r : 8 * r + 8, :] for r in range(count)]
    sub = lax.broadcasted_iota(jnp.int32, (8, 128), 0)
    diag = [lane_splat(rows[0], 64 + m) for m in range(8)]
    for b in range(count):
        more = b + 1 < count
        x = rows[b]
        if more:
            ahead = rows[b + 1]
            side = [lane_splat(ahead, 64 + 8 * b + m) for m in range(8)]
            following = [lane_splat(ahead, 72 + 8 * b + m) for m in range(8)]
        far = {r: [lane_splat(rows[r], 64 + 8 * b + m) for m in range(8)] for r in range(b + 2, count)}
        inverse, pivot_rows, low = [], [], []
        pivots = diag[0]
        for k in range(8):
            r = 1.0 / row_splat(diag[k], k)
            inverse.append(r)
            if k:
                pivots = jnp.where(sub == k, diag[k], pivots)
            below = jnp.where(sub > k, diag[k], 0.0)
            low.append(below)
            pivot = row_splat(x, k) * r
            pivot_rows.append(pivot)
            for m in range(k + 1, 8):
                entry = row_splat(diag[m], k)
                diag[m] = diag[m] - (below * entry) * r
                if more:
                    side[m] = side[m] - side[k] * (entry * r)
            x = x - below * pivot
            if more:
                ahead = ahead - side[k] * pivot
        if more:
            scaled = [side[k] * inverse[k] for k in range(8)]
            diag = [
                following[m] - total([scaled[k] * row_splat(side[k], m) for k in range(8)]) for m in range(8)
            ]
            rows[b + 1] = ahead
        if far:
            back = [None] * 8
            for k in range(7, -1, -1):
                column = low[k] * inverse[k]
                back[k] = pivot_rows[k]
                for i in range(k + 1, 8):
                    back[k] = back[k] - row_splat(column, i) * back[i]
            for r in far:
                rows[r] = rows[r] - total([far[r][m] * back[m] for m in range(8)])
        rows[b] = x * lax.rsqrt(pivots)
    return jnp.concatenate(rows, axis=0)


def shifted(pair):
    lane = lax.broadcasted_iota(jnp.int32, pair.shape, 1)
    return jnp.where(lane >= 64, pltpu.roll(pair, 64, 1), 0.0)


def spread(matrix, aug_ref):
    size = matrix.shape[0]
    lane = lax.broadcasted_iota(jnp.int32, (size, 128), 1)
    row = lax.broadcasted_iota(jnp.int32, (size, 128), 0)
    for k in range(size // 64):
        half = matrix[:, 128 * (k // 2) : 128 * (k // 2) + 128]
        if k % 2 == 0:
            half = pltpu.roll(half, 64, 1)
        eye = (row == lane + 64 * k).astype(F32)
        aug_ref[:, 128 * k : 128 * k + 128] = jnp.where(lane >= 64, half, eye)


def gather_inverse(aug_ref):
    lane = lax.broadcasted_iota(jnp.int32, (aug_ref.shape[0], 128), 1)
    parts = []
    for t in range(aug_ref.shape[1] // 256):
        even = aug_ref[:, 256 * t : 256 * t + 128]
        odd = aug_ref[:, 256 * t + 128 : 256 * t + 256]
        parts.append(jnp.where(lane < 64, even, pltpu.roll(odd, 64, 1)))
    return jnp.concatenate(parts, axis=1)


def factor(aug_ref, low_refs=None, begin=0, end=None, start=None):
    size = aug_ref.shape[0]
    count = size // 64
    if start is None:
        start = aug_ref[:64, :128]
    for k in range(begin, count if end is None else end):
        here = slice(64 * k, 64 * k + 64)
        tile = slice(128 * k, 128 * k + 128)
        pair = leaf(start)
        wide = shifted(pair)
        inverse = pair[:, :64]
        if low_refs is not None:
            low_refs[k][here, :] = nt(start, wide)
        if k + 1 == count:
            aug_ref[here, :] = nn(inverse, aug_ref[here, :])
            break
        below = slice(64 * k + 64, 64 * k + 128)
        after = slice(128 * k + 128, 128 * k + 256)
        near = nt(aug_ref[below, tile], wide)
        start = aug_ref[below, after] - nn(near, nn(inverse, aug_ref[here, after]))
        ahead = nn(inverse, aug_ref[here, :])
        left = nt(aug_ref[64 * k + 64 :, tile], wide)
        aug_ref[here, :] = ahead
        if low_refs is not None:
            low_refs[k][64 * k + 64 :, :] = left
        aug_ref[64 * k + 64 :, :] = aug_ref[64 * k + 64 :, :] - nn(left, ahead)
    return start


def masked_gram(gram, rank):
    size = gram.shape[0]
    row = lax.broadcasted_iota(jnp.int32, gram.shape, 0)
    col = lax.broadcasted_iota(jnp.int32, gram.shape, 1)
    both = (row < rank) & (col < rank)
    dead = (row == col) & (row >= rank)
    return jnp.where(both, gram, 0.0), dead.astype(F32)


def iota(shape, dim):
    return lax.broadcasted_iota(jnp.int32, shape, dim)


def halves(x):
    top = x.astype(BF16)
    return top, (x - top.astype(F32)).astype(BF16)


def lower_only(x):
    return jnp.where(iota(x.shape, 0) >= iota(x.shape, 1), x, 0.0)


def places():
    spot_i, spot_j = lax.axis_index("row"), lax.axis_index("col")
    return lax.rem(spot_j, 2), spot_j // 8, spot_i // 2, lax.rem(spot_j // 2, 4), lax.rem(spot_i, 2)


def copy_all(pairs, sem):
    copies = [pltpu.make_async_copy(source, target, sem.at[k]) for k, (source, target) in enumerate(pairs)]
    for copy in copies:
        copy.start()
    return copies


def early_kernel(
    rank_t, sketch_hbm, tile_u_hbm, tile_v_hbm,
    gram_hbm, sketch_t_hbm, aug_hbm, low0_hbm,
    sketch, tile_u, tile_v, gram, sketch_t, aug_ref, low0, in_sem, out_sem
):
    loads = copy_all([(tile_v_hbm, tile_v), (tile_u_hbm, tile_u), (sketch_hbm, sketch)], in_sem)
    rank = rank_t[0, 0]
    loads[0].wait()
    gram_v, dead = masked_gram(tn(tile_v[...], tile_v[...]), rank)
    spread(gram_v + dead, aug_ref)
    loads[1].wait()
    loads[2].wait()
    gram[...] = masked_gram(tn(tile_u[...], tile_u[...]), rank)[0]
    flipped = sketch[...].T
    sketch_t[...] = flipped
    factor(aug_ref, (low0,), 0, 1)
    pairs = [(gram, gram_hbm), (sketch_t, sketch_t_hbm), (aug_ref, aug_hbm), (low0, low0_hbm)]
    for store in copy_all(pairs, out_sem):
        store.wait()


def early_call(rank, sketch, tile_u, tile_v):
    wide = pltpu.VMEM(tile_u.shape, BF16)
    hbm = pl.BlockSpec(memory_space=pl.ANY)
    shapes = [(256, 256), (256, 320), (256, 512), (256, 64)]
    return pl.pallas_call(
        early_kernel,
        out_shape=[jax.ShapeDtypeStruct(shape, F32) for shape in shapes],
        in_specs=[pl.BlockSpec(memory_space=pltpu.SMEM)] + [hbm] * 3,
        out_specs=[hbm] * 4,
        scratch_shapes=[pltpu.VMEM((320, 256), F32), wide, wide]
        + [pltpu.VMEM(shape, F32) for shape in shapes]
        + [pltpu.SemaphoreType.DMA((3,)), pltpu.SemaphoreType.DMA((4,))],
        compiler_params=pltpu.CompilerParams(vmem_limit_bytes=VMEM_LIMIT),
        cost_estimate=pl.CostEstimate(flops=7 * 10**9, bytes_accessed=4 * 10**6, transcendentals=0),
        name="early_factor",
    )(rank, sketch, tile_u, tile_v)


def middle_kernel(aug_hbm, aug_out_hbm, low1_hbm, low2_hbm, aug_ref, low1, low2, in_sem, out_sem):
    load = pltpu.make_async_copy(aug_hbm, aug_ref, in_sem)
    load.start()
    low1[:64, :] = jnp.zeros((64, 64), F32)
    low2[:128, :] = jnp.zeros((128, 64), F32)
    load.wait()
    factor(aug_ref, (None, low1, low2), 1, 3, aug_ref[64:128, 128:256])
    for store in copy_all([(aug_ref, aug_out_hbm), (low1, low1_hbm), (low2, low2_hbm)], out_sem):
        store.wait()


def middle_call(aug):
    hbm = pl.BlockSpec(memory_space=pl.ANY)
    shapes = [(256, 512), (256, 64), (256, 64)]
    return pl.pallas_call(
        middle_kernel,
        out_shape=[jax.ShapeDtypeStruct(shape, F32) for shape in shapes],
        in_specs=[hbm],
        out_specs=[hbm] * 3,
        scratch_shapes=[pltpu.VMEM(shape, F32) for shape in shapes] + [pltpu.SemaphoreType.DMA, pltpu.SemaphoreType.DMA((3,))],
        compiler_params=pltpu.CompilerParams(vmem_limit_bytes=VMEM_LIMIT),
        cost_estimate=pl.CostEstimate(flops=6 * 10**9, bytes_accessed=2 * 10**6, transcendentals=0),
        name="middle_factor",
    )(aug)


def late_kernel(
    rank_t, aug_hbm, low0_hbm, low1_hbm, low2_hbm, sketch_t_hbm, gram_hbm,
    low_inv_hbm, y_hbm, x_hbm,
    aug_ref, low0, low1, low2, sketch_t, gram, low3, low_inv, y_ref, x_ref, in_sem, out_sem,
):
    pairs = [(aug_hbm, aug_ref), (low0_hbm, low0), (low1_hbm, low1), (low2_hbm, low2), (sketch_t_hbm, sketch_t), (gram_hbm, gram)]
    loads = copy_all(pairs, in_sem)
    low3[:192, :] = jnp.zeros((192, 64), F32)
    for load in loads:
        load.wait()
    lows = (low0, low1, low2, low3)
    factor(aug_ref, lows, 3, 4, aug_ref[192:256, 384:512])
    low_inv[...] = gather_inverse(aug_ref)
    low = lower_only(jnp.concatenate([ref[...] for ref in lows], axis=1))
    y = jnp.where(iota((256, 256), 1) < rank_t[0, 0], nt(sketch_t[:, :256], low), 0.0)
    y_ref[...] = y
    x_ref[...] = nn(y, gram[...])
    for store in copy_all([(low_inv, low_inv_hbm), (y_ref, y_hbm), (x_ref, x_hbm)], out_sem):
        store.wait()


def late_call(rank, aug, low0, low1, low2, sketch_t, gram):
    hbm = pl.BlockSpec(memory_space=pl.ANY)
    square = jax.ShapeDtypeStruct((256, 256), F32)
    block, thin = pltpu.VMEM((256, 256), F32), pltpu.VMEM((256, 64), F32)
    return pl.pallas_call(
        late_kernel,
        out_shape=[square] * 3,
        in_specs=[pl.BlockSpec(memory_space=pltpu.SMEM)] + [hbm] * 6,
        out_specs=[hbm] * 3,
        scratch_shapes=[pltpu.VMEM((256, 512), F32), thin, thin, thin, pltpu.VMEM((256, 320), F32), block, thin, block, block, block]
        + [pltpu.SemaphoreType.DMA((6,)), pltpu.SemaphoreType.DMA((3,))],
        compiler_params=pltpu.CompilerParams(vmem_limit_bytes=VMEM_LIMIT),
        cost_estimate=pl.CostEstimate(flops=6 * 10**9, bytes_accessed=2 * 10**6, transcendentals=0),
        name="late_factor",
    )(rank, aug, low0, low1, low2, sketch_t, gram)


def panel_copies(pieces, target, sem):
    core, y_low, z, x, y_half = places()
    block = pieces[0].shape[1]
    left, right = lax.rem(x + 3, 4), lax.rem(x + 1, 4)
    come, back = jnp.where(core == 0, left, right), jnp.where(core == 0, right, left)
    across = lax.rem(x + 2, 4)
    other = 1 - core
    spots = [
        (core, x), (other, x), (core, come), (other, come),
        (other, back), (core, back), (core, across), (other, across),
    ]
    copies = []
    for array, (slot, place) in zip(pieces, spots):
        for k in range(2):
            start = (lax.rem(y_low + k, 2) * 4 + place) * block
            spot = pl.ds(pl.multiple_of(start, block), block)
            copies.append(pltpu.make_async_copy(array.at[k], target.at[slot, spot, :], sem.at[len(copies)]))
    return copies


def side_copies(own, near, swapped, far, target, sem):
    core, y_low, z, x, y_half = places()
    block = own.shape[1]
    down, up = lax.rem(z + 3, 4), lax.rem(z + 1, 4)
    come, back = jnp.where(core == 0, down, up), jnp.where(core == 0, up, down)
    copies = []
    for array, place in ((own, z), (near, come), (swapped, back), (far, lax.rem(z + 2, 4))):
        for k in range(2):
            start = (place * 2 + lax.rem(y_half + k, 2)) * block
            spot = pl.ds(pl.multiple_of(start, block), block)
            copies.append(pltpu.make_async_copy(array.at[k], target.at[spot, :], sem.at[16 + len(copies)]))
    return copies


def main_kernel(
    rank_t, rank_i, rank_j, rank_s, low_inv_hbm, sketch_t_hbm, y_t_hbm, x_t_hbm, tile_u_hbm, tile_v_hbm,
    row0, row1, row2, row3, row4, row5, row6, row7, side_own, side_near, side_swapped, side_far,
    out_u_hbm, out_v_hbm,
    low_inv, sketch_t, y_t, x_t, tile_u, tile_v, panel, col_uv, up, wide_u, out_u, out_v, aug_ref, w_t, g_t, p_ref,
    in_sem, out_sem
):
    rows = tile_u.shape[0]
    t_rank, i_rank, j_rank, s_rank = rank_t[0, 0], rank_i[0], rank_j[0], rank_s[0, 0]
    arrived = side_copies(side_own, side_near, side_swapped, side_far, col_uv, in_sem)
    arrived += panel_copies((row0, row1, row2, row3, row4, row5, row6, row7), panel, in_sem)
    pairs = [
        (tile_v_hbm, tile_v), (low_inv_hbm, low_inv), (sketch_t_hbm, sketch_t),
        (y_t_hbm, y_t), (x_t_hbm, x_t), (tile_u_hbm, tile_u),
    ]
    kept = [pltpu.make_async_copy(source, target, in_sem.at[24 + k]) for k, (source, target) in enumerate(pairs)]
    for load in arrived + kept:
        load.start()
    for load in arrived:
        load.wait()
    sides = col_uv[...]
    keep = (iota((64, 256), 0) < j_rank) & (iota((64, 256), 1) < i_rank)
    cross_t = jnp.where(keep, tn(sides, panel[1])[64:], 0.0).astype(BF16)
    for load in kept:
        load.wait()
    keep = (iota((64, 256), 0) < j_rank) & (iota((64, 256), 1) < t_rank)
    side = jnp.where(keep, -tn(sides, tile_v[...])[:64], 0.0)
    corner, dead = masked_gram(tn(sides, sides)[:64, :64], j_rank)
    low_pt = nt(side, low_inv[...])
    schur = corner + dead - nt(low_pt, low_pt)
    eye = (iota((64, 64), 0) == iota((64, 64), 1)).astype(F32)
    start = jnp.concatenate([eye, schur], axis=1)
    low_pp = lower_only(nt(start, shifted(leaf(start))))
    for step in range(rows // CHUNK):
        here = slice(step * CHUNK, step * CHUNK + CHUNK)
        top, rest = halves(nt(panel[0, here, :], cross_t, None))
        up[here, :] = jnp.concatenate([top, rest, top, rest], axis=1)
        part = col_uv[here, :][:, :64]
        wide_u[here, :] = jnp.concatenate([part, part], axis=1)
    both = tn(up[:, :128], tile_u[...])
    gram_pt = jnp.where(keep, both[:64] + both[64:], 0.0)
    four = tn(up[:, :128], up[:, :128])
    four = four[:64] + four[64:]
    gram_pp = (four + pltpu.roll(four, 64, 1))[:, :64]
    drawn = iota((256, 256), 0) < s_rank
    ys = jnp.where(drawn, y_t[...], 0.0)
    yp = nt(sketch_t[:, :256], low_pt) + nt(sketch_t[:, 256:], low_pp)
    yp = jnp.where((iota((256, 64), 1) < j_rank) & (iota((256, 64), 0) < s_rank), yp, 0.0)
    xs = jnp.where(drawn, x_t[...], 0.0) + nn(yp, gram_pt)
    xp = nt(ys, gram_pt) + nn(yp, gram_pp)
    same = iota((256, 256), 0) == iota((256, 256), 1)
    dead = (same & (iota((256, 256), 0) >= s_rank)).astype(F32)
    spread(nt(xs, ys) + nt(xp, yp) + dead, aug_ref)
    factor(aug_ref)
    inverse = gather_inverse(aug_ref)
    w_t[...] = nn(inverse, ys)
    g_t[...] = nn(inverse, xs)
    p_ref[...] = nn(inverse, jnp.concatenate([yp, xp], axis=1))
    live = (same & (iota((256, 256), 0) < s_rank)).astype(F32)

    def refine(state):
        count, unused = state
        pair = p_ref[...]
        upper = jnp.where(iota(pair.shape, 1) < 64, pair, 0.0)
        error = nt(w_t[...], g_t[...]) + nt(upper, pltpu.roll(pair, 64, 1)) - live
        size = jnp.max(jnp.sum(jnp.abs(error), axis=1, keepdims=True))
        step = (lower_only(error) - jnp.where(same, 0.5 * error, 0.0)).astype(BF16)
        for ref in (w_t, g_t, p_ref):
            ref[...] = ref[...] - nn(step, ref[...].astype(BF16), None)
        return count + 1, size

    lax.while_loop(lambda s: (s[0] < 12) & (s[1] > TOLERANCE), refine, (jnp.int32(0), jnp.float32(1.0)))
    scale = math.sqrt(rows)
    u_hi, u_lo = halves(w_t[...] * scale)
    pair = p_ref[...]
    p_hi, p_lo = halves(pair[:, :64] * scale)
    v_hi, v_lo = halves(g_t[...])
    u_all = jnp.concatenate([u_hi, u_lo, p_hi, p_hi, p_lo, p_lo], axis=1)
    v_all = jnp.concatenate([v_hi, v_lo, *halves(-pair[:, 64:])], axis=1)
    stores = []
    for step in range(rows // CHUNK):
        here = slice(step * CHUNK, step * CHUNK + CHUNK)
        tile = tile_u[here, :]
        out_u[here, :] = nt(jnp.concatenate([tile, tile, up[here, :]], axis=1), u_all, None)
        tile = tile_v[here, :]
        stores.append(pltpu.make_async_copy(out_u.at[here, :], out_u_hbm.at[here, :], out_sem.at[0, step]))
        stores[-1].start()
        out_v[here, :] = nt(jnp.concatenate([tile, tile, wide_u[here, :]], axis=1), v_all, None)
        stores.append(pltpu.make_async_copy(out_v.at[here, :], out_v_hbm.at[here, :], out_sem.at[1, step]))
        stores[-1].start()
    for store in stores:
        store.wait()


def main_call(ranks, low_inv, sketch_t, y_t, x_t, tile_u, tile_v, panels, sides):
    rows = tile_u.shape[0]
    hbm = pl.BlockSpec(memory_space=pl.ANY)
    out = jax.ShapeDtypeStruct((rows, 256), F32)
    block = pltpu.VMEM((256, 256), F32)
    wide = pltpu.VMEM((rows, 256), BF16)
    half = pltpu.VMEM((rows, 128), BF16)
    result = pltpu.VMEM((rows, 256), F32)
    return pl.pallas_call(
        main_kernel,
        out_shape=(out, out),
        in_specs=[pl.BlockSpec(memory_space=pltpu.SMEM)] * 4 + [hbm] * 18,
        out_specs=(hbm, hbm),
        scratch_shapes=[
            block, pltpu.VMEM((256, 320), F32), block, block, wide, wide, pltpu.VMEM((2, rows, 256), BF16), half, wide, half, result, result,
            pltpu.VMEM((256, 512), F32), block, block, pltpu.VMEM((256, 128), F32),
            pltpu.SemaphoreType.DMA((30,)), pltpu.SemaphoreType.DMA((2, rows // CHUNK)),
        ],
        compiler_params=pltpu.CompilerParams(vmem_limit_bytes=VMEM_LIMIT),
        cost_estimate=pl.CostEstimate(flops=20 * 10**9, bytes_accessed=15 * 10**6, transcendentals=0),
        name="recompress",
    )(*ranks, low_inv, sketch_t, y_t, x_t, tile_u, tile_v, *panels, *sides)


def send(x, axis, count, step):
    return lax.ppermute(x, axis, [(i, step(i)) for i in range(count)])


def swap(x):
    return send(x, "col", 16, lambda i: i ^ 1)


def round_x(x):
    return send(x, "col", 16, lambda i: i // 8 * 8 + (i + (2 if i % 2 == 0 else 6)) % 8)


def round_z(x):
    return send(x, ("row", "col"), 128, lambda i: (i + (32 if i % 2 == 0 else 96)) % 128)


def body(tile_u, tile_v, row_u, row_v, col_u, col_v, tile_rank, row_rank, col_rank, target_rank, sketch):
    first = lax.axis_index("col") % 2 == 0
    own_u, own_v = tile_u[0, 0], tile_v[0, 0]
    side = jnp.concatenate([col_u[0], col_v[0]], axis=1)
    give = jnp.where(first, row_v[0], row_u[0])
    keep = jnp.where(first, row_u[0], row_v[0])
    got = swap(give)
    chip = jnp.concatenate([jnp.where(first, keep, got), jnp.where(first, got, keep)], axis=0)
    chip, side = lax.optimization_barrier((chip, side))
    chip_other = send(chip, "col", 16, lambda i: i ^ 8)
    side_other = send(side, "row", 8, lambda i: i ^ 1)
    chip_swapped, side_swapped = swap(chip), swap(side)
    early = early_call(tile_rank, sketch, own_u, own_v)
    early, side_other, chip_other, chip_swapped, side_swapped = lax.optimization_barrier(
        (early, side_other, chip_other, chip_swapped, side_swapped)
    )
    gram, sketch_t, aug, low0 = early
    mine = jnp.stack([chip, chip_other])
    side_all = jnp.stack([side, side_other, side_swapped, swap(side_other)])
    near = round_x(mine)
    theirs = jnp.stack([chip_swapped, swap(chip_other)])
    near_theirs = round_x(theirs)
    side_near = round_z(side_all)
    aug, low1, low2 = middle_call(aug)
    aug, near, side_near = lax.optimization_barrier((aug, near, side_near))
    far, side_far = round_x(near), round_z(side_near[:2])
    near_swapped, side_back = swap(near), swap(side_near[2:])
    low_inv, y_t, x_t = late_call(tile_rank, aug, low0, low1, low2, sketch_t, gram)
    theirs_swapped = swap(near_theirs)
    far, side_far, near_swapped, side_back, theirs_swapped, y_t, row_rank, col_rank, target_rank = lax.optimization_barrier(
        (far, side_far, near_swapped, side_back, theirs_swapped, y_t, row_rank, col_rank, target_rank)
    )
    ranks = (tile_rank, row_rank, col_rank, target_rank)
    panels = [mine, theirs, near, near_theirs, near_swapped, theirs_swapped, far, swap(far)]
    sides = [side_all, side_near, side_back, side_far]
    new_u, new_v = main_call(ranks, low_inv, sketch_t, y_t, x_t, own_u, own_v, panels, sides)
    return (new_u[None, None], new_v[None, None])


def solution(mesh):
    placed = (
        P("row", "col", None, None),
        P("row", "col", None, None),
        P("row", "col", None),
        P("row", "col", None),
        P("col", "row", None),
        P("col", "row", None),
        P("row", "col"),
        P("row"),
        P("col"),
        P("row", "col"),
        P(),
    )
    return jax.shard_map(
        body,
        mesh=mesh,
        in_specs=placed,
        out_specs=(P("row", "col", None, None), P("row", "col", None, None)),
        check_vma=False,
    )
```

time: 75.2 us -> 65.9 us (0.88)
  waiting for transfers between devices: 7.27 us -> 0.04 us
  Pallas kernels: 40.9 us -> 39.3 us
  local copies, waits for them, and re-layouts: 3.56 us -> 2.57 us
    ppermute x13 -> x16, waiting for transfers between devices: 7.27 us -> 0.04 us  [send(): return lax.ppermute(x, axis, [(i, step(i)) for i in range(count)])]
    pallas_call x2 -> x3, Pallas kernels: 19.9 us -> 16.5 us  [the longest x1 5.86 us: middle_call(): pl.pallas_call(middle_kernel, out_shape=[jax.ShapeDtypeStruct(shape, F32)...]
    pallas_call x1, Pallas kernels: 21 us -> 22.8 us  [main_call(): pl.pallas_call(main_kernel, out_shape=(out, out), in_specs=[pl.BlockSpec(...]
    ppermute x13 -> x16, starting transfers between devices: 17.1 us -> 17.7 us  [send(): return lax.ppermute(x, axis, [(i, step(i)) for i in range(count)])]
  transfers between devices with their start and end apart: 13 -> 16, of which waited for: 3 -> 0; matrix products, arithmetic and copies ran while one was open for 4% -> 3% of each run, Pallas kernels for 27% -> 25%
where the time goes in v2:
time: 65.9 us; the launch traced here: 65.5 us
  Pallas kernels  39.3 us (60%)
  starting transfers between devices  17.7 us (27%)
  between operations  3.78 us (6%)
  local copies, waits for them, and re-layouts  2.57 us (4%)
  other arithmetic  2.07 us (3%)
    pallas_call x1, Pallas kernels, main_call(): pl.pallas_call(main_kernel, out_shape=(out, out), in_specs=[pl.BlockSpec(...  22.8 us
    ppermute x16, starting transfers between devices, send(): return lax.ppermute(x, axis, [(i, step(i)) for i in range(count)])  17.7 us
    pallas_call x1, Pallas kernels, middle_call(): pl.pallas_call(middle_kernel, out_shape=[jax.ShapeDtypeStruct(shape, F32)...  5.86 us
    pallas_call x1, Pallas kernels, early_call(): pl.pallas_call(early_kernel, out_shape=[jax.ShapeDtypeStruct(shape, F32)...  5.84 us
    pallas_call x1, Pallas kernels, late_call(): pl.pallas_call(late_kernel, out_shape=[square] * 3, in_specs=[pl.BlockSpe...  4.78 us
    unnamed x26, local copies, waits for them, and re-layouts  2.54 us
  transfers between devices with their start and end apart: 16, of which 0 were waited for; matrix products, arithmetic and copies ran while one was open for 3% of the time, Pallas kernels for 25%

profile of v2, /device:TPU:1, one launch (start us, length us, event | category | flops | bytes accessed | tf_op | source)
XLA Modules:
  0.0 65.5 jit_solution(3028957711901981757)
XLA Ops:
  0.6 0.9 %select_bitcast_fusion = bf16[168,256]{1,0:T(8,128)(2,1)S(1)} fusion(bf16[1,168,256]{2,1,0:T(8,128)(2,1)} %param.14, bf16[1,168,256]{2,1,0:T(8,128)(2,1)} %param.13, pred[]{:T(512)S(6)} %eq.5), kind=kLoop, calls=%fused_computation.7 | loop fusion | flops 43008 | bytes 258049 | tf_op jit(solution)/shard_map/jit(_where)/select_n | solution.py:460
  1.6 1.5 %collective-permute-start = (bf16[168,256]{1,0:T(8,128)(2,1)S(1)}, bf16[168,256]{1,0:T(8,128)(2,1)S(1)}, u32[]{:S(2)}, u32[]{:S(2)}) collective-permute-start(bf16[168,256]{1,0:T(8,128)(2,1)S(1)} %select_bitcast_fusion), channel_id=1, source_target_pairs={{0,1},{1,0},{2,3},{3,2},{4,5},{5,4},{6,7},{7,6},{8,9},{9,8},{10,11... | collective-permute-start | bytes 258056 | tf_op jit(solution)/shard_map/ppermute | solution.py:441
  3.7 0.9 %copy.13 = bf16[1,336,64]{2,1,0:T(8,128)(2,1)S(1)} copy(bf16[1,336,64]{1,2,0:T(8,128)(2,1)} %param.15) | data formatting | bytes 86016 | tf_op args[4]
  4.6 0.9 %copy.14 = bf16[1,336,64]{2,1,0:T(8,128)(2,1)S(1)} copy(bf16[1,336,64]{1,2,0:T(8,128)(2,1)} %param.16) | data formatting | bytes 86016 | tf_op args[5]
  5.5 0.1 pad_maximum_fusion.4
  5.7 0.0 collective-permute-done
  5.7 0.9 %bitcast_select_fusion.1 = (bf16[168,256]{1,0:T(8,128)(2,1)S(1)}, bf16[168,256]{1,0:T(8,128)(2,1)S(1)}) fusion(bf16[168,256]{1,0:T(8,128)(2,1)S(1)} %collective-permute-done, pred[]{:T(512)S(6)} %eq.5, bf16[1,168,256]{2,1,0:T(8,128)(2,1)} %param.13, bf16[1,168,256]{2,1,0:T(8,128)(2,1)} %param.14), kind=kLoop, calls=%fused_computation.6 | loop fusion | flops 129024 | bytes 430081 | tf_op jit(solution)/shard_map/jit(_where)/select_n | solution.py:463
  6.6 0.1 collective-permute-start.4
  6.7 3.1 %collective-permute-start.1 = (bf16[336,128]{1,0:T(8,128)(2,1)S(1)}, bf16[336,128]{1,0:T(8,128)(2,1)S(1)}, u32[]{:S(2)}, u32[]{:S(2)}) collective-permute-start(bf16[336,128]{1,0:T(8,128)(2,1)S(1)} %pad_maximum_fusion.4), channel_id=1, source_target_pairs={{0,16},{16,0},{32,48},{48,32},{64,80},{80,64},{96,112},{112,96},{1... | collective-permute-start | bytes 258056 | tf_op jit(solution)/shard_map/ppermute | solution.py:441
  9.8 0.7 %collective-permute-start.3 = (bf16[336,256]{1,0:T(8,128)(2,1)S(1)}, bf16[336,256]{1,0:T(8,128)(2,1)S(1)}, u32[]{:S(2)}, u32[]{:S(2)}) collective-permute-start(bf16[336,256]{1,0:T(8,128)(2,1)S(1)} %pad_maximum_fusion.3), channel_id=1, source_target_pairs={{0,1},{1,0},{2,3},{3,2},{4,5},{5,4},{6,7},{7,6},{8,9},{9,8},{10,11... | collective-permute-start | bytes 516104 | tf_op jit(solution)/shard_map/ppermute | solution.py:441
  10.5 0.4 collective-permute-start.2
  10.9 5.8 %early_factor.1 = (f32[256,256]{1,0:T(8,128)}, f32[256,320]{1,0:T(8,128)}, f32[256,512]{1,0:T(8,128)}, f32[256,64]{1,0:T(8,128)}) custom-call(s32[1,1]{1,0:T(1,128)S(6)} %copy.15.rank_t, f32[320,256]{1,0:T(8,128)} %sketch_hbm.1, bf16[2688,256]{1,0:T(8,128)(2,1)} %bitcast.29, bf16[2688,256]{1,0:T(8,128)(2,1)} %bitcast.31), custom_call_target="tpu_custom_call" | custom-call | flops 7000000000 | bytes 4000000 | tf_op jit(solution)/shard_map/early_factor/pallas_call | solution.py:210
  16.7 0.0 collective-permute-done.4
  16.7 0.0 collective-permute-done.1
  16.8 0.0 collective-permute-done.3
  16.8 0.0 collective-permute-done.2
  16.8 0.6 collective-permute-start.6
  17.4 0.0 collective-permute-start.12
  17.4 0.0 copy-start
  17.4 2.5 %collective-permute-start.5 = (bf16[2,336,256]{2,1,0:T(8,128)(2,1)S(1)}, bf16[2,336,256]{2,1,0:T(8,128)(2,1)S(1)}, u32[]{:S(2)}, u32[]{:S(2)}) collective-permute-start(bf16[2,336,256]{2,1,0:T(8,128)(2,1)S(1)} %pad_maximum_fusion.row0), channel_id=1, source_target_pairs={{0,2},{1,7},{2,4},{3,1},{4,6},{5,3},{6,0},{7,5},{8,10},{9,15},{10,... | collective-permute-start | bytes 1032200 | tf_op jit(solution)/shard_map/ppermute | solution.py:441
  20.0 0.0 collective-permute-done.6
  20.0 0.0 copy-start.1
  20.0 3.8 %collective-permute-start.7 = (bf16[4,336,128]{2,1,0:T(8,128)(2,1)S(1)}, bf16[4,336,128]{2,1,0:T(8,128)(2,1)S(1)}, u32[]{:S(2)}, u32[]{:S(2)}) collective-permute-start(bf16[4,336,128]{2,1,0:T(8,128)(2,1)S(1)} %pad_maximum_fusion.1.side_own), channel_id=1, source_target_pairs={{0,32},{1,97},{2,34},{3,99},{4,36},{5,101},{6,38},{7,103},{8,40},{... | collective-permute-start | bytes 1032200 | tf_op jit(solution)/shard_map/ppermute | solution.py:441
  23.9 0.0 collective-permute-done.12
  23.9 0.0 copy-start.3
  23.9 0.9 %collective-permute-start.13 = (bf16[2,336,256]{2,1,0:T(8,128)(2,1)S(1)}, bf16[2,336,256]{2,1,0:T(8,128)(2,1)S(1)}, u32[]{:S(2)}, u32[]{:S(2)}) collective-permute-start(bf16[2,336,256]{2,1,0:T(8,128)(2,1)S(1)} %pad_maximum_fusion.2.row1), channel_id=1, source_target_pairs={{0,2},{1,7},{2,4},{3,1},{4,6},{5,3},{6,0},{7,5},{8,10},{9,15},{10,... | collective-permute-start | bytes 1032200 | tf_op jit(solution)/shard_map/ppermute | solution.py:441
  24.8 5.9 %middle_factor.1 = (f32[256,512]{1,0:T(8,128)}, f32[256,64]{1,0:T(8,128)}, f32[256,64]{1,0:T(8,128)}) custom-call(f32[256,512]{1,0:T(8,128)} %get-tuple-element.42.aug_hbm), custom_call_target="tpu_custom_call" | custom-call | flops 6000000000 | bytes 2000000 | tf_op jit(solution)/shard_map/middle_factor/pallas_call | solution.py:238
  30.7 0.0 collective-permute-done.5.row2
  30.7 0.0 copy-start.4
  30.7 0.0 collective-permute-done.7.side_near
  30.7 0.1 collective-permute-start.10
  30.8 0.6 collective-permute-start.8
  31.4 0.9 %collective-permute-start.11 = (bf16[2,336,128]{2,1,0:T(8,128)(2,1)S(1)}, bf16[2,336,128]{2,1,0:T(8,128)(2,1)S(1)}, u32[]{:S(2)}, u32[]{:S(2)}) collective-permute-start(bf16[2,336,128]{2,1,0:T(8,128)(2,1)S(1)} %get-tuple-element.70), channel_id=1, source_target_pairs={{0,1},{1,0},{2,3},{3,2},{4,5},{5,4},{6,7},{7,6},{8,9},{9,8},{10,11... | collective-permute-start | bytes 516104 | tf_op jit(solution)/shard_map/ppermute | solution.py:441
  32.4 0.3 collective-permute-start.9
  32.7 0.0 collective-permute-done.13.row3
  32.7 0.5 collective-permute-start.14
  33.2 4.8 %late_factor.1 = (f32[256,256]{1,0:T(8,128)}, f32[256,256]{1,0:T(8,128)}, f32[256,256]{1,0:T(8,128)}) custom-call(s32[1,1]{1,0:T(1,128)S(6)} %copy.15.rank_t, f32[256,512]{1,0:T(8,128)} %get-tuple-element.50.aug_hbm, f32[256,64]{1,0:T(8,128)} %get-tuple-element.51.low0_hbm, f32[256,64]{1,0:T(8,128)} %get-tuple-element.52.low1_hbm, ...), custom_call_target="tpu_custom_call" | custom-call | flops 6000000000 | bytes 2000000 | tf_op jit(solution)/shard_map/late_factor/pallas_call | solution.py:275
  38.0 0.0 collective-permute-done.11.side_swapped
  38.0 0.0 collective-permute-done.9.side_far
  38.0 0.0 copy-start.11
  38.0 0.0 collective-permute-done.10.row4
  38.0 0.0 collective-permute-done.8.row6
  38.1 0.0 collective-permute-done.14.row5
  38.1 0.0 copy-start.8
  38.1 1.8 %collective-permute-start.15 = (bf16[2,336,256]{2,1,0:T(8,128)(2,1)S(1)}, bf16[2,336,256]{2,1,0:T(8,128)(2,1)S(1)}, u32[]{:S(2)}, u32[]{:S(2)}) collective-permute-start(bf16[2,336,256]{2,1,0:T(8,128)(2,1)S(1)} %collective-permute-done.8.row6), channel_id=1, source_target_pairs={{0,1},{1,0},{2,3},{3,2},{4,5},{5,4},{6,7},{7,6},{8,9},{9,8},{10,11... | collective-permute-start | bytes 1032200 | tf_op jit(solution)/shard_map/ppermute | solution.py:441
  41.8 0.0 collective-permute-done.15.row7
  41.9 0.7 %copy-done.9 = bf16[2,336,256]{2,1,0:T(8,128)(2,1)} copy-done((bf16[2,336,256]{2,1,0:T(8,128)(2,1)}, bf16[2,336,256]{2,1,0:T(8,128)(2,1)S(1)}, u32[]{:S(2)}) %copy-start.9) | copy-done | bytes 344088
  42.5 22.8 %recompress.1 = (f32[2688,256]{1,0:T(8,128)}, f32[2688,256]{1,0:T(8,128)}) custom-call(s32[1,1]{1,0:T(1,128)S(6)} %copy.15.rank_t, s32[1]{0:T(128)S(6)} %copy.16.rank_i, s32[1]{0:T(128)S(6)} %copy.17.rank_j, s32[1,1]{1,0:T(1,128)S(6)} %copy.18.rank_s, f32[256,256]{1,0:T(8,128)} %get-tuple-element.60.low_inv_hbm, f32[256,320]{1,0:T(8,128)} %get-tuple-element.54.sketch_t_hbm, ...), custom_call_target="tpu_custom_call" | custom-call | flops 20000000000 | bytes 15000000 | tf_op jit(solution)/shard_map/recompress/pallas_call | solution.py:424
  (22 shorter events, 0.2 us)
Async XLA Ops:
  1.6 4.1 %collective-permute-start = (bf16[168,256]{1,0:T(8,128)(2,1)S(1)}, bf16[168,256]{1,0:T(8,128)(2,1)S(1)}, u32[]{:S(2)}, u32[]{:S(2)}) collective-permute-start(bf16[168,256]{1,0:T(8,128)(2,1)S(1)} %select_bitcast_fusion), channel_id=1, source_target_pairs={{0,1},{1,0},{2,3},{3,2},{4,5},{5,4},{6,7},{7,6},{8,9},{9,8},{10,11... | collective-permute-start | bytes 258056 | tf_op jit(solution)/shard_map/ppermute | solution.py:441
  6.6 10.1 %collective-permute-start.4 = (bf16[336,128]{1,0:T(8,128)(2,1)S(1)}, bf16[336,128]{1,0:T(8,128)(2,1)S(1)}, u32[]{:S(2)}, u32[]{:S(2)}) collective-permute-start(bf16[336,128]{1,0:T(8,128)(2,1)S(1)} %pad_maximum_fusion.4), channel_id=1, source_target_pairs={{0,1},{1,0},{2,3},{3,2},{4,5},{5,4},{6,7},{7,6},{8,9},{9,8},{10,11... | collective-permute-start | bytes 258056 | tf_op jit(solution)/shard_map/ppermute | solution.py:441
  6.7 10.0 %collective-permute-start.1 = (bf16[336,128]{1,0:T(8,128)(2,1)S(1)}, bf16[336,128]{1,0:T(8,128)(2,1)S(1)}, u32[]{:S(2)}, u32[]{:S(2)}) collective-permute-start(bf16[336,128]{1,0:T(8,128)(2,1)S(1)} %pad_maximum_fusion.4), channel_id=1, source_target_pairs={{0,16},{16,0},{32,48},{48,32},{64,80},{80,64},{96,112},{112,96},{1... | collective-permute-start | bytes 258056 | tf_op jit(solution)/shard_map/ppermute | solution.py:441
  9.8 7.0 %collective-permute-start.3 = (bf16[336,256]{1,0:T(8,128)(2,1)S(1)}, bf16[336,256]{1,0:T(8,128)(2,1)S(1)}, u32[]{:S(2)}, u32[]{:S(2)}) collective-permute-start(bf16[336,256]{1,0:T(8,128)(2,1)S(1)} %pad_maximum_fusion.3), channel_id=1, source_target_pairs={{0,1},{1,0},{2,3},{3,2},{4,5},{5,4},{6,7},{7,6},{8,9},{9,8},{10,11... | collective-permute-start | bytes 516104 | tf_op jit(solution)/shard_map/ppermute | solution.py:441
  10.5 6.3 %collective-permute-start.2 = (bf16[336,256]{1,0:T(8,128)(2,1)S(1)}, bf16[336,256]{1,0:T(8,128)(2,1)S(1)}, u32[]{:S(2)}, u32[]{:S(2)}) collective-permute-start(bf16[336,256]{1,0:T(8,128)(2,1)S(1)} %pad_maximum_fusion.3), channel_id=1, source_target_pairs={{0,8},{1,9},{2,10},{3,11},{4,12},{5,13},{6,14},{7,15},{8,0},{9,1},... | collective-permute-start | bytes 516104 | tf_op jit(solution)/shard_map/ppermute | solution.py:441
  16.8 3.2 %collective-permute-start.6 = (bf16[336,128]{1,0:T(8,128)(2,1)S(1)}, bf16[336,128]{1,0:T(8,128)(2,1)S(1)}, u32[]{:S(2)}, u32[]{:S(2)}) collective-permute-start(bf16[336,128]{1,0:T(8,128)(2,1)S(1)} %collective-permute-done.1), channel_id=1, source_target_pairs={{0,1},{1,0},{2,3},{3,2},{4,5},{5,4},{6,7},{7,6},{8,9},{9,8},{10,11... | collective-permute-start | bytes 258056 | tf_op jit(solution)/shard_map/ppermute | solution.py:441
  17.4 6.5 %collective-permute-start.12 = (bf16[336,256]{1,0:T(8,128)(2,1)S(1)}, bf16[336,256]{1,0:T(8,128)(2,1)S(1)}, u32[]{:S(2)}, u32[]{:S(2)}) collective-permute-start(bf16[336,256]{1,0:T(8,128)(2,1)S(1)} %collective-permute-done.2), channel_id=1, source_target_pairs={{0,1},{1,0},{2,3},{3,2},{4,5},{5,4},{6,7},{7,6},{8,9},{9,8},{10,11... | collective-permute-start | bytes 516104 | tf_op jit(solution)/shard_map/ppermute | solution.py:441
  17.4 13.2 %copy-start = (bf16[2,336,256]{2,1,0:T(8,128)(2,1)}, bf16[2,336,256]{2,1,0:T(8,128)(2,1)S(1)}, u32[]{:S(2)}) copy-start(bf16[2,336,256]{2,1,0:T(8,128)(2,1)S(1)} %pad_maximum_fusion.row0) | copy-start | bytes 1032196
  17.4 13.3 %collective-permute-start.5 = (bf16[2,336,256]{2,1,0:T(8,128)(2,1)S(1)}, bf16[2,336,256]{2,1,0:T(8,128)(2,1)S(1)}, u32[]{:S(2)}, u32[]{:S(2)}) collective-permute-start(bf16[2,336,256]{2,1,0:T(8,128)(2,1)S(1)} %pad_maximum_fusion.row0), channel_id=1, source_target_pairs={{0,2},{1,7},{2,4},{3,1},{4,6},{5,3},{6,0},{7,5},{8,10},{9,15},{10,... | collective-permute-start | bytes 1032200 | tf_op jit(solution)/shard_map/ppermute | solution.py:441
  20.0 10.6 %copy-start.1 = (bf16[4,336,128]{2,1,0:T(8,128)(2,1)}, bf16[4,336,128]{2,1,0:T(8,128)(2,1)S(1)}, u32[]{:S(2)}) copy-start(bf16[4,336,128]{2,1,0:T(8,128)(2,1)S(1)} %pad_maximum_fusion.1.side_own) | copy-start | bytes 1032196
  20.0 10.7 %collective-permute-start.7 = (bf16[4,336,128]{2,1,0:T(8,128)(2,1)S(1)}, bf16[4,336,128]{2,1,0:T(8,128)(2,1)S(1)}, u32[]{:S(2)}, u32[]{:S(2)}) collective-permute-start(bf16[4,336,128]{2,1,0:T(8,128)(2,1)S(1)} %pad_maximum_fusion.1.side_own), channel_id=1, source_target_pairs={{0,32},{1,97},{2,34},{3,99},{4,36},{5,101},{6,38},{7,103},{8,40},{... | collective-permute-start | bytes 1032200 | tf_op jit(solution)/shard_map/ppermute | solution.py:441
  23.9 6.8 %copy-start.3 = (bf16[2,336,256]{2,1,0:T(8,128)(2,1)}, bf16[2,336,256]{2,1,0:T(8,128)(2,1)S(1)}, u32[]{:S(2)}) copy-start(bf16[2,336,256]{2,1,0:T(8,128)(2,1)S(1)} %pad_maximum_fusion.2.row1) | copy-start | bytes 1032196
  23.9 8.8 %collective-permute-start.13 = (bf16[2,336,256]{2,1,0:T(8,128)(2,1)S(1)}, bf16[2,336,256]{2,1,0:T(8,128)(2,1)S(1)}, u32[]{:S(2)}, u32[]{:S(2)}) collective-permute-start(bf16[2,336,256]{2,1,0:T(8,128)(2,1)S(1)} %pad_maximum_fusion.2.row1), channel_id=1, source_target_pairs={{0,2},{1,7},{2,4},{3,1},{4,6},{5,3},{6,0},{7,5},{8,10},{9,15},{10,... | collective-permute-start | bytes 1032200 | tf_op jit(solution)/shard_map/ppermute | solution.py:441
  30.7 7.3 %copy-start.4 = (bf16[2,336,256]{2,1,0:T(8,128)(2,1)}, bf16[2,336,256]{2,1,0:T(8,128)(2,1)S(1)}, u32[]{:S(2)}) copy-start(bf16[2,336,256]{2,1,0:T(8,128)(2,1)S(1)} %collective-permute-done.5.row2) | copy-start | bytes 1032196
  30.7 7.3 %copy-start.2 = (bf16[4,336,128]{2,1,0:T(8,128)(2,1)}, bf16[4,336,128]{2,1,0:T(8,128)(2,1)S(1)}, u32[]{:S(2)}) copy-start(bf16[4,336,128]{2,1,0:T(8,128)(2,1)S(1)} %collective-permute-done.7.side_near) | copy-start | bytes 1032196
  30.7 7.3 %collective-permute-start.10 = (bf16[2,336,256]{2,1,0:T(8,128)(2,1)S(1)}, bf16[2,336,256]{2,1,0:T(8,128)(2,1)S(1)}, u32[]{:S(2)}, u32[]{:S(2)}) collective-permute-start(bf16[2,336,256]{2,1,0:T(8,128)(2,1)S(1)} %collective-permute-done.5.row2), channel_id=1, source_target_pairs={{0,1},{1,0},{2,3},{3,2},{4,5},{5,4},{6,7},{7,6},{8,9},{9,8},{10,11... | collective-permute-start | bytes 1032200 | tf_op jit(solution)/shard_map/ppermute | solution.py:441
  30.8 7.2 %collective-permute-start.8 = (bf16[2,336,256]{2,1,0:T(8,128)(2,1)S(1)}, bf16[2,336,256]{2,1,0:T(8,128)(2,1)S(1)}, u32[]{:S(2)}, u32[]{:S(2)}) collective-permute-start(bf16[2,336,256]{2,1,0:T(8,128)(2,1)S(1)} %collective-permute-done.5.row2), channel_id=1, source_target_pairs={{0,2},{1,7},{2,4},{3,1},{4,6},{5,3},{6,0},{7,5},{8,10},{9,15},{10,... | collective-permute-start | bytes 1032200 | tf_op jit(solution)/shard_map/ppermute | solution.py:441
  31.4 6.5 %collective-permute-start.11 = (bf16[2,336,128]{2,1,0:T(8,128)(2,1)S(1)}, bf16[2,336,128]{2,1,0:T(8,128)(2,1)S(1)}, u32[]{:S(2)}, u32[]{:S(2)}) collective-permute-start(bf16[2,336,128]{2,1,0:T(8,128)(2,1)S(1)} %get-tuple-element.70), channel_id=1, source_target_pairs={{0,1},{1,0},{2,3},{3,2},{4,5},{5,4},{6,7},{7,6},{8,9},{9,8},{10,11... | collective-permute-start | bytes 516104 | tf_op jit(solution)/shard_map/ppermute | solution.py:441
  32.4 5.6 %collective-permute-start.9 = (bf16[2,336,128]{2,1,0:T(8,128)(2,1)S(1)}, bf16[2,336,128]{2,1,0:T(8,128)(2,1)S(1)}, u32[]{:S(2)}, u32[]{:S(2)}) collective-permute-start(bf16[2,336,128]{2,1,0:T(8,128)(2,1)S(1)} %get-tuple-element.71), channel_id=1, source_target_pairs={{0,32},{1,97},{2,34},{3,99},{4,36},{5,101},{6,38},{7,103},{8,40},{... | collective-permute-start | bytes 516104 | tf_op jit(solution)/shard_map/ppermute | solution.py:441
  32.7 5.3 %copy-start.5 = (bf16[2,336,256]{2,1,0:T(8,128)(2,1)}, bf16[2,336,256]{2,1,0:T(8,128)(2,1)S(1)}, u32[]{:S(2)}) copy-start(bf16[2,336,256]{2,1,0:T(8,128)(2,1)S(1)} %collective-permute-done.13.row3) | copy-start | bytes 1032196
  32.7 5.4 %collective-permute-start.14 = (bf16[2,336,256]{2,1,0:T(8,128)(2,1)S(1)}, bf16[2,336,256]{2,1,0:T(8,128)(2,1)S(1)}, u32[]{:S(2)}, u32[]{:S(2)}) collective-permute-start(bf16[2,336,256]{2,1,0:T(8,128)(2,1)S(1)} %collective-permute-done.13.row3), channel_id=1, source_target_pairs={{0,1},{1,0},{2,3},{3,2},{4,5},{5,4},{6,7},{7,6},{8,9},{9,8},{10,11... | collective-permute-start | bytes 1032200 | tf_op jit(solution)/shard_map/ppermute | solution.py:441
  38.0 3.8 %copy-start.10 = (bf16[2,336,128]{2,1,0:T(8,128)(2,1)}, bf16[2,336,128]{2,1,0:T(8,128)(2,1)S(1)}, u32[]{:S(2)}) copy-start(bf16[2,336,128]{2,1,0:T(8,128)(2,1)S(1)} %collective-permute-done.11.side_swapped) | copy-start | bytes 516100
  38.0 3.8 %copy-start.11 = (bf16[2,336,128]{2,1,0:T(8,128)(2,1)}, bf16[2,336,128]{2,1,0:T(8,128)(2,1)S(1)}, u32[]{:S(2)}) copy-start(bf16[2,336,128]{2,1,0:T(8,128)(2,1)S(1)} %collective-permute-done.9.side_far) | copy-start | bytes 516100
  38.0 3.8 %copy-start.6 = (bf16[2,336,256]{2,1,0:T(8,128)(2,1)}, bf16[2,336,256]{2,1,0:T(8,128)(2,1)S(1)}, u32[]{:S(2)}) copy-start(bf16[2,336,256]{2,1,0:T(8,128)(2,1)S(1)} %collective-permute-done.10.row4) | copy-start | bytes 1032196
  38.0 3.8 %copy-start.7 = (bf16[2,336,256]{2,1,0:T(8,128)(2,1)}, bf16[2,336,256]{2,1,0:T(8,128)(2,1)S(1)}, u32[]{:S(2)}) copy-start(bf16[2,336,256]{2,1,0:T(8,128)(2,1)S(1)} %collective-permute-done.8.row6) | copy-start | bytes 1032196
  38.1 3.8 %copy-start.8 = (bf16[2,336,256]{2,1,0:T(8,128)(2,1)}, bf16[2,336,256]{2,1,0:T(8,128)(2,1)S(1)}, u32[]{:S(2)}) copy-start(bf16[2,336,256]{2,1,0:T(8,128)(2,1)S(1)} %collective-permute-done.14.row5) | copy-start | bytes 1032196
  38.1 3.7 %collective-permute-start.15 = (bf16[2,336,256]{2,1,0:T(8,128)(2,1)S(1)}, bf16[2,336,256]{2,1,0:T(8,128)(2,1)S(1)}, u32[]{:S(2)}, u32[]{:S(2)}) collective-permute-start(bf16[2,336,256]{2,1,0:T(8,128)(2,1)S(1)} %collective-permute-done.8.row6), channel_id=1, source_target_pairs={{0,1},{1,0},{2,3},{3,2},{4,5},{5,4},{6,7},{7,6},{8,9},{9,8},{10,11... | collective-permute-start | bytes 1032200 | tf_op jit(solution)/shard_map/ppermute | solution.py:441
  41.8 0.7 %copy-start.9 = (bf16[2,336,256]{2,1,0:T(8,128)(2,1)}, bf16[2,336,256]{2,1,0:T(8,128)(2,1)S(1)}, u32[]{:S(2)}) copy-start(bf16[2,336,256]{2,1,0:T(8,128)(2,1)S(1)} %collective-permute-done.15.row7) | copy-start | bytes 1032196

commit v3 on v2

--- a/solution.py
+++ b/solution.py
@@ -194,12 +194,19 @@
     spread(gram_v + dead, aug_ref)
     loads[1].wait()
     loads[2].wait()
-    gram[...] = masked_gram(tn(tile_u[...], tile_u[...]), rank)[0]
     flipped = sketch[...].T
     sketch_t[...] = flipped
+    gram[...] = masked_gram(tn(tile_u[...], tile_u[...]), rank)[0]
+    stores = [
+        pltpu.make_async_copy(source, target, out_sem.at[k])
+        for k, (source, target) in enumerate([(gram, gram_hbm), (sketch_t, sketch_t_hbm), (low0, low0_hbm), (aug_ref, aug_hbm)])
+    ]
+    stores[0].start()
+    stores[1].start()
     factor(aug_ref, (low0,), 0, 1)
-    pairs = [(gram, gram_hbm), (sketch_t, sketch_t_hbm), (aug_ref, aug_hbm), (low0, low0_hbm)]
-    for store in copy_all(pairs, out_sem):
+    stores[2].start()
+    stores[3].start()
+    for store in stores:
         store.wait()
 
 
@@ -255,11 +262,12 @@
     pairs = [(aug_hbm, aug_ref), (low0_hbm, low0), (low1_hbm, low1), (low2_hbm, low2), (sketch_t_hbm, sketch_t), (gram_hbm, gram)]
     loads = copy_all(pairs, in_sem)
     low3[:192, :] = jnp.zeros((192, 64), F32)
-    for load in loads:
-        load.wait()
+    loads[0].wait()
     lows = (low0, low1, low2, low3)
     factor(aug_ref, lows, 3, 4, aug_ref[192:256, 384:512])
     low_inv[...] = gather_inverse(aug_ref)
+    for load in loads[1:]:
+        load.wait()
     low = lower_only(jnp.concatenate([ref[...] for ref in lows], axis=1))
     y = jnp.where(iota((256, 256), 1) < rank_t[0, 0], nt(sketch_t[:, :256], low), 0.0)
     y_ref[...] = y
@@ -328,27 +336,28 @@
 ):
     rows = tile_u.shape[0]
     t_rank, i_rank, j_rank, s_rank = rank_t[0, 0], rank_i[0], rank_j[0], rank_s[0, 0]
-    arrived = side_copies(side_own, side_near, side_swapped, side_far, col_uv, in_sem)
-    arrived += panel_copies((row0, row1, row2, row3, row4, row5, row6, row7), panel, in_sem)
+    first = side_copies(side_own, side_near, side_swapped, side_far, col_uv, in_sem)
     pairs = [
         (tile_v_hbm, tile_v), (low_inv_hbm, low_inv), (sketch_t_hbm, sketch_t),
-        (y_t_hbm, y_t), (x_t_hbm, x_t), (tile_u_hbm, tile_u),
+        (tile_u_hbm, tile_u), (y_t_hbm, y_t), (x_t_hbm, x_t),
     ]
     kept = [pltpu.make_async_copy(source, target, in_sem.at[24 + k]) for k, (source, target) in enumerate(pairs)]
-    for load in arrived + kept:
+    first += kept[:3]
+    then = panel_copies((row0, row1, row2, row3, row4, row5, row6, row7), panel, in_sem) + kept[3:]
+    for load in first + then:
         load.start()
-    for load in arrived:
+    for load in first:
         load.wait()
     sides = col_uv[...]
-    keep = (iota((64, 256), 0) < j_rank) & (iota((64, 256), 1) < i_rank)
-    cross_t = jnp.where(keep, tn(sides, panel[1])[64:], 0.0).astype(BF16)
-    for load in kept:
-        load.wait()
     keep = (iota((64, 256), 0) < j_rank) & (iota((64, 256), 1) < t_rank)
     side = jnp.where(keep, -tn(sides, tile_v[...])[:64], 0.0)
     corner, dead = masked_gram(tn(sides, sides)[:64, :64], j_rank)
     low_pt = nt(side, low_inv[...])
     schur = corner + dead - nt(low_pt, low_pt)
+    for load in then:
+        load.wait()
+    keep_i = (iota((64, 256), 0) < j_rank) & (iota((64, 256), 1) < i_rank)
+    cross_t = jnp.where(keep_i, tn(sides, panel[1])[64:], 0.0).astype(BF16)
     eye = (iota((64, 64), 0) == iota((64, 64), 1)).astype(F32)
     start = jnp.concatenate([eye, schur], axis=1)
     low_pp = lower_only(nt(start, shifted(leaf(start))))

time: 65.9 us -> 64.5 us (0.979)
  Pallas kernels: 39.3 us -> 37.8 us
    pallas_call x1, Pallas kernels: 22.8 us -> 21.4 us  [main_call(): pl.pallas_call(main_kernel, out_shape=(out, out), in_specs=[pl.BlockSpec(...]
  transfers between devices with their start and end apart: 16 -> 16, of which waited for: 0 -> 0; matrix products, arithmetic and copies ran while one was open for 3% -> 3% of each run, Pallas kernels for 25% -> 26%
where the time goes in v3:
time: 64.5 us; the launch traced here: 64.1 us
  Pallas kernels  37.8 us (59%)
  starting transfers between devices  17.8 us (28%)
  between operations  3.78 us (6%)
  local copies, waits for them, and re-layouts  2.57 us (4%)
  other arithmetic  2.07 us (3%)
    pallas_call x1, Pallas kernels, main_call(): pl.pallas_call(main_kernel, out_shape=(out, out), in_specs=[pl.BlockSpec(...  21.4 us
    ppermute x16, starting transfers between devices, send(): return lax.ppermute(x, axis, [(i, step(i)) for i in range(count)])  17.8 us
    pallas_call x1, Pallas kernels, middle_call(): pl.pallas_call(middle_kernel, out_shape=[jax.ShapeDtypeStruct(shape, F32)...  5.86 us
    pallas_call x1, Pallas kernels, early_call(): pl.pallas_call(early_kernel, out_shape=[jax.ShapeDtypeStruct(shape, F32)...  5.86 us
    pallas_call x1, Pallas kernels, late_call(): pl.pallas_call(late_kernel, out_shape=[square] * 3, in_specs=[pl.BlockSpe...  4.71 us
    unnamed x26, local copies, waits for them, and re-layouts  2.54 us
  transfers between devices with their start and end apart: 16, of which 0 were waited for; matrix products, arithmetic and copies ran while one was open for 3% of the time, Pallas kernels for 26%

profile of v3, /device:TPU:1, one launch (start us, length us, event | category | flops | bytes accessed | tf_op | source)
XLA Modules:
  0.0 64.1 jit_solution(16686227500365682597)
XLA Ops:
  0.6 0.9 %select_bitcast_fusion = bf16[168,256]{1,0:T(8,128)(2,1)S(1)} fusion(bf16[1,168,256]{2,1,0:T(8,128)(2,1)} %param.14, bf16[1,168,256]{2,1,0:T(8,128)(2,1)} %param.13, pred[]{:T(512)S(6)} %eq.5), kind=kLoop, calls=%fused_computation.7 | loop fusion | flops 43008 | bytes 258049 | tf_op jit(solution)/shard_map/jit(_where)/select_n | solution.py:469
  1.6 1.5 %collective-permute-start = (bf16[168,256]{1,0:T(8,128)(2,1)S(1)}, bf16[168,256]{1,0:T(8,128)(2,1)S(1)}, u32[]{:S(2)}, u32[]{:S(2)}) collective-permute-start(bf16[168,256]{1,0:T(8,128)(2,1)S(1)} %select_bitcast_fusion), channel_id=1, source_target_pairs={{0,1},{1,0},{2,3},{3,2},{4,5},{5,4},{6,7},{7,6},{8,9},{9,8},{10,11... | collective-permute-start | bytes 258056 | tf_op jit(solution)/shard_map/ppermute | solution.py:450
  3.7 0.9 %copy.13 = bf16[1,336,64]{2,1,0:T(8,128)(2,1)S(1)} copy(bf16[1,336,64]{1,2,0:T(8,128)(2,1)} %param.15) | data formatting | bytes 86016 | tf_op args[4]
  4.6 0.9 %copy.14 = bf16[1,336,64]{2,1,0:T(8,128)(2,1)S(1)} copy(bf16[1,336,64]{1,2,0:T(8,128)(2,1)} %param.16) | data formatting | bytes 86016 | tf_op args[5]
  5.5 0.1 pad_maximum_fusion.4
  5.7 0.0 collective-permute-done
  5.7 0.9 %bitcast_select_fusion.1 = (bf16[168,256]{1,0:T(8,128)(2,1)S(1)}, bf16[168,256]{1,0:T(8,128)(2,1)S(1)}) fusion(bf16[168,256]{1,0:T(8,128)(2,1)S(1)} %collective-permute-done, pred[]{:T(512)S(6)} %eq.5, bf16[1,168,256]{2,1,0:T(8,128)(2,1)} %param.13, bf16[1,168,256]{2,1,0:T(8,128)(2,1)} %param.14), kind=kLoop, calls=%fused_computation.6 | loop fusion | flops 129024 | bytes 430081 | tf_op jit(solution)/shard_map/jit(_where)/select_n | solution.py:472
  6.6 0.1 collective-permute-start.4
  6.7 3.1 %collective-permute-start.1 = (bf16[336,128]{1,0:T(8,128)(2,1)S(1)}, bf16[336,128]{1,0:T(8,128)(2,1)S(1)}, u32[]{:S(2)}, u32[]{:S(2)}) collective-permute-start(bf16[336,128]{1,0:T(8,128)(2,1)S(1)} %pad_maximum_fusion.4), channel_id=1, source_target_pairs={{0,16},{16,0},{32,48},{48,32},{64,80},{80,64},{96,112},{112,96},{1... | collective-permute-start | bytes 258056 | tf_op jit(solution)/shard_map/ppermute | solution.py:450
  9.8 0.7 %collective-permute-start.3 = (bf16[336,256]{1,0:T(8,128)(2,1)S(1)}, bf16[336,256]{1,0:T(8,128)(2,1)S(1)}, u32[]{:S(2)}, u32[]{:S(2)}) collective-permute-start(bf16[336,256]{1,0:T(8,128)(2,1)S(1)} %pad_maximum_fusion.3), channel_id=1, source_target_pairs={{0,1},{1,0},{2,3},{3,2},{4,5},{5,4},{6,7},{7,6},{8,9},{9,8},{10,11... | collective-permute-start | bytes 516104 | tf_op jit(solution)/shard_map/ppermute | solution.py:450
  10.5 0.4 collective-permute-start.2
  10.9 5.9 %early_factor.1 = (f32[256,256]{1,0:T(8,128)}, f32[256,320]{1,0:T(8,128)}, f32[256,512]{1,0:T(8,128)}, f32[256,64]{1,0:T(8,128)}) custom-call(s32[1,1]{1,0:T(1,128)S(6)} %copy.15.rank_t, f32[320,256]{1,0:T(8,128)} %sketch_hbm.1, bf16[2688,256]{1,0:T(8,128)(2,1)} %bitcast.29, bf16[2688,256]{1,0:T(8,128)(2,1)} %bitcast.31), custom_call_target="tpu_custom_call" | custom-call | flops 7000000000 | bytes 4000000 | tf_op jit(solution)/shard_map/early_factor/pallas_call | solution.py:217
  16.8 0.0 collective-permute-done.4
  16.8 0.0 collective-permute-done.1
  16.8 0.0 collective-permute-done.3
  16.8 0.0 collective-permute-done.2
  16.8 0.6 collective-permute-start.6
  17.4 0.0 collective-permute-start.12
  17.4 0.0 copy-start
  17.4 2.5 %collective-permute-start.5 = (bf16[2,336,256]{2,1,0:T(8,128)(2,1)S(1)}, bf16[2,336,256]{2,1,0:T(8,128)(2,1)S(1)}, u32[]{:S(2)}, u32[]{:S(2)}) collective-permute-start(bf16[2,336,256]{2,1,0:T(8,128)(2,1)S(1)} %pad_maximum_fusion.row0), channel_id=1, source_target_pairs={{0,2},{1,7},{2,4},{3,1},{4,6},{5,3},{6,0},{7,5},{8,10},{9,15},{10,... | collective-permute-start | bytes 1032200 | tf_op jit(solution)/shard_map/ppermute | solution.py:450
  20.0 0.0 collective-permute-done.6
  20.0 0.0 copy-start.1
  20.0 3.8 %collective-permute-start.7 = (bf16[4,336,128]{2,1,0:T(8,128)(2,1)S(1)}, bf16[4,336,128]{2,1,0:T(8,128)(2,1)S(1)}, u32[]{:S(2)}, u32[]{:S(2)}) collective-permute-start(bf16[4,336,128]{2,1,0:T(8,128)(2,1)S(1)} %pad_maximum_fusion.1.side_own), channel_id=1, source_target_pairs={{0,32},{1,97},{2,34},{3,99},{4,36},{5,101},{6,38},{7,103},{8,40},{... | collective-permute-start | bytes 1032200 | tf_op jit(solution)/shard_map/ppermute | solution.py:450
  23.9 0.0 collective-permute-done.12
  23.9 0.0 copy-start.3
  23.9 0.8 %collective-permute-start.13 = (bf16[2,336,256]{2,1,0:T(8,128)(2,1)S(1)}, bf16[2,336,256]{2,1,0:T(8,128)(2,1)S(1)}, u32[]{:S(2)}, u32[]{:S(2)}) collective-permute-start(bf16[2,336,256]{2,1,0:T(8,128)(2,1)S(1)} %pad_maximum_fusion.2.row1), channel_id=1, source_target_pairs={{0,2},{1,7},{2,4},{3,1},{4,6},{5,3},{6,0},{7,5},{8,10},{9,15},{10,... | collective-permute-start | bytes 1032200 | tf_op jit(solution)/shard_map/ppermute | solution.py:450
  24.8 5.9 %middle_factor.1 = (f32[256,512]{1,0:T(8,128)}, f32[256,64]{1,0:T(8,128)}, f32[256,64]{1,0:T(8,128)}) custom-call(f32[256,512]{1,0:T(8,128)} %get-tuple-element.42.aug_hbm), custom_call_target="tpu_custom_call" | custom-call | flops 6000000000 | bytes 2000000 | tf_op jit(solution)/shard_map/middle_factor/pallas_call | solution.py:245
  30.6 0.0 copy-done
  30.7 0.0 collective-permute-done.5.row2
  30.7 0.0 collective-permute-done.7.side_near
  30.7 0.0 copy-start.2
  30.7 0.1 collective-permute-start.10
  30.8 0.6 collective-permute-start.8
  31.4 0.9 %collective-permute-start.11 = (bf16[2,336,128]{2,1,0:T(8,128)(2,1)S(1)}, bf16[2,336,128]{2,1,0:T(8,128)(2,1)S(1)}, u32[]{:S(2)}, u32[]{:S(2)}) collective-permute-start(bf16[2,336,128]{2,1,0:T(8,128)(2,1)S(1)} %get-tuple-element.70), channel_id=1, source_target_pairs={{0,1},{1,0},{2,3},{3,2},{4,5},{5,4},{6,7},{7,6},{8,9},{9,8},{10,11... | collective-permute-start | bytes 516104 | tf_op jit(solution)/shard_map/ppermute | solution.py:450
  32.4 0.3 collective-permute-start.9
  32.7 0.0 collective-permute-done.13.row3
  32.7 0.5 collective-permute-start.14
  33.2 4.7 %late_factor.1 = (f32[256,256]{1,0:T(8,128)}, f32[256,256]{1,0:T(8,128)}, f32[256,256]{1,0:T(8,128)}) custom-call(s32[1,1]{1,0:T(1,128)S(6)} %copy.15.rank_t, f32[256,512]{1,0:T(8,128)} %get-tuple-element.50.aug_hbm, f32[256,64]{1,0:T(8,128)} %get-tuple-element.51.low0_hbm, f32[256,64]{1,0:T(8,128)} %get-tuple-element.52.low1_hbm, ...), custom_call_target="tpu_custom_call" | custom-call | flops 6000000000 | bytes 2000000 | tf_op jit(solution)/shard_map/late_factor/pallas_call | solution.py:283
  37.9 0.0 collective-permute-done.11.side_swapped
  37.9 0.0 collective-permute-done.9.side_far
  37.9 0.0 collective-permute-done.10.row4
  38.0 0.0 copy-start.6
  38.0 0.0 collective-permute-done.8.row6
  38.0 0.0 collective-permute-done.14.row5
  38.0 1.8 %collective-permute-start.15 = (bf16[2,336,256]{2,1,0:T(8,128)(2,1)S(1)}, bf16[2,336,256]{2,1,0:T(8,128)(2,1)S(1)}, u32[]{:S(2)}, u32[]{:S(2)}) collective-permute-start(bf16[2,336,256]{2,1,0:T(8,128)(2,1)S(1)} %collective-permute-done.8.row6), channel_id=1, source_target_pairs={{0,1},{1,0},{2,3},{3,2},{4,5},{5,4},{6,7},{7,6},{8,9},{9,8},{10,11... | collective-permute-start | bytes 1032200 | tf_op jit(solution)/shard_map/ppermute | solution.py:450
  41.8 0.0 collective-permute-done.15.row7
  41.9 0.7 %copy-done.9 = bf16[2,336,256]{2,1,0:T(8,128)(2,1)} copy-done((bf16[2,336,256]{2,1,0:T(8,128)(2,1)}, bf16[2,336,256]{2,1,0:T(8,128)(2,1)S(1)}, u32[]{:S(2)}) %copy-start.9) | copy-done | bytes 344088
  42.5 21.4 %recompress.1 = (f32[2688,256]{1,0:T(8,128)}, f32[2688,256]{1,0:T(8,128)}) custom-call(s32[1,1]{1,0:T(1,128)S(6)} %copy.15.rank_t, s32[1]{0:T(128)S(6)} %copy.16.rank_i, s32[1]{0:T(128)S(6)} %copy.17.rank_j, s32[1,1]{1,0:T(1,128)S(6)} %copy.18.rank_s, f32[256,256]{1,0:T(8,128)} %get-tuple-element.60.low_inv_hbm, f32[256,320]{1,0:T(8,128)} %get-tuple-element.54.sketch_t_hbm, ...), custom_call_target="tpu_custom_call" | custom-call | flops 20000000000 | bytes 15000000 | tf_op jit(solution)/shard_map/recompress/pallas_call | solution.py:433
  (22 shorter events, 0.2 us)
Async XLA Ops:
  1.6 4.1 %collective-permute-start = (bf16[168,256]{1,0:T(8,128)(2,1)S(1)}, bf16[168,256]{1,0:T(8,128)(2,1)S(1)}, u32[]{:S(2)}, u32[]{:S(2)}) collective-permute-start(bf16[168,256]{1,0:T(8,128)(2,1)S(1)} %select_bitcast_fusion), channel_id=1, source_target_pairs={{0,1},{1,0},{2,3},{3,2},{4,5},{5,4},{6,7},{7,6},{8,9},{9,8},{10,11... | collective-permute-start | bytes 258056 | tf_op jit(solution)/shard_map/ppermute | solution.py:450
  6.6 10.1 %collective-permute-start.4 = (bf16[336,128]{1,0:T(8,128)(2,1)S(1)}, bf16[336,128]{1,0:T(8,128)(2,1)S(1)}, u32[]{:S(2)}, u32[]{:S(2)}) collective-permute-start(bf16[336,128]{1,0:T(8,128)(2,1)S(1)} %pad_maximum_fusion.4), channel_id=1, source_target_pairs={{0,1},{1,0},{2,3},{3,2},{4,5},{5,4},{6,7},{7,6},{8,9},{9,8},{10,11... | collective-permute-start | bytes 258056 | tf_op jit(solution)/shard_map/ppermute | solution.py:450
  6.7 10.1 %collective-permute-start.1 = (bf16[336,128]{1,0:T(8,128)(2,1)S(1)}, bf16[336,128]{1,0:T(8,128)(2,1)S(1)}, u32[]{:S(2)}, u32[]{:S(2)}) collective-permute-start(bf16[336,128]{1,0:T(8,128)(2,1)S(1)} %pad_maximum_fusion.4), channel_id=1, source_target_pairs={{0,16},{16,0},{32,48},{48,32},{64,80},{80,64},{96,112},{112,96},{1... | collective-permute-start | bytes 258056 | tf_op jit(solution)/shard_map/ppermute | solution.py:450
  9.8 7.0 %collective-permute-start.3 = (bf16[336,256]{1,0:T(8,128)(2,1)S(1)}, bf16[336,256]{1,0:T(8,128)(2,1)S(1)}, u32[]{:S(2)}, u32[]{:S(2)}) collective-permute-start(bf16[336,256]{1,0:T(8,128)(2,1)S(1)} %pad_maximum_fusion.3), channel_id=1, source_target_pairs={{0,1},{1,0},{2,3},{3,2},{4,5},{5,4},{6,7},{7,6},{8,9},{9,8},{10,11... | collective-permute-start | bytes 516104 | tf_op jit(solution)/shard_map/ppermute | solution.py:450
  10.5 6.3 %collective-permute-start.2 = (bf16[336,256]{1,0:T(8,128)(2,1)S(1)}, bf16[336,256]{1,0:T(8,128)(2,1)S(1)}, u32[]{:S(2)}, u32[]{:S(2)}) collective-permute-start(bf16[336,256]{1,0:T(8,128)(2,1)S(1)} %pad_maximum_fusion.3), channel_id=1, source_target_pairs={{0,8},{1,9},{2,10},{3,11},{4,12},{5,13},{6,14},{7,15},{8,0},{9,1},... | collective-permute-start | bytes 516104 | tf_op jit(solution)/shard_map/ppermute | solution.py:450
  16.8 3.2 %collective-permute-start.6 = (bf16[336,128]{1,0:T(8,128)(2,1)S(1)}, bf16[336,128]{1,0:T(8,128)(2,1)S(1)}, u32[]{:S(2)}, u32[]{:S(2)}) collective-permute-start(bf16[336,128]{1,0:T(8,128)(2,1)S(1)} %collective-permute-done.1), channel_id=1, source_target_pairs={{0,1},{1,0},{2,3},{3,2},{4,5},{5,4},{6,7},{7,6},{8,9},{9,8},{10,11... | collective-permute-start | bytes 258056 | tf_op jit(solution)/shard_map/ppermute | solution.py:450
  17.4 6.5 %collective-permute-start.12 = (bf16[336,256]{1,0:T(8,128)(2,1)S(1)}, bf16[336,256]{1,0:T(8,128)(2,1)S(1)}, u32[]{:S(2)}, u32[]{:S(2)}) collective-permute-start(bf16[336,256]{1,0:T(8,128)(2,1)S(1)} %collective-permute-done.2), channel_id=1, source_target_pairs={{0,1},{1,0},{2,3},{3,2},{4,5},{5,4},{6,7},{7,6},{8,9},{9,8},{10,11... | collective-permute-start | bytes 516104 | tf_op jit(solution)/shard_map/ppermute | solution.py:450
  17.4 13.2 %copy-start = (bf16[2,336,256]{2,1,0:T(8,128)(2,1)}, bf16[2,336,256]{2,1,0:T(8,128)(2,1)S(1)}, u32[]{:S(2)}) copy-start(bf16[2,336,256]{2,1,0:T(8,128)(2,1)S(1)} %pad_maximum_fusion.row0) | copy-start | bytes 1032196
  17.4 13.2 %collective-permute-start.5 = (bf16[2,336,256]{2,1,0:T(8,128)(2,1)S(1)}, bf16[2,336,256]{2,1,0:T(8,128)(2,1)S(1)}, u32[]{:S(2)}, u32[]{:S(2)}) collective-permute-start(bf16[2,336,256]{2,1,0:T(8,128)(2,1)S(1)} %pad_maximum_fusion.row0), channel_id=1, source_target_pairs={{0,2},{1,7},{2,4},{3,1},{4,6},{5,3},{6,0},{7,5},{8,10},{9,15},{10,... | collective-permute-start | bytes 1032200 | tf_op jit(solution)/shard_map/ppermute | solution.py:450
  20.0 10.6 %copy-start.1 = (bf16[4,336,128]{2,1,0:T(8,128)(2,1)}, bf16[4,336,128]{2,1,0:T(8,128)(2,1)S(1)}, u32[]{:S(2)}) copy-start(bf16[4,336,128]{2,1,0:T(8,128)(2,1)S(1)} %pad_maximum_fusion.1.side_own) | copy-start | bytes 1032196
  20.0 10.6 %collective-permute-start.7 = (bf16[4,336,128]{2,1,0:T(8,128)(2,1)S(1)}, bf16[4,336,128]{2,1,0:T(8,128)(2,1)S(1)}, u32[]{:S(2)}, u32[]{:S(2)}) collective-permute-start(bf16[4,336,128]{2,1,0:T(8,128)(2,1)S(1)} %pad_maximum_fusion.1.side_own), channel_id=1, source_target_pairs={{0,32},{1,97},{2,34},{3,99},{4,36},{5,101},{6,38},{7,103},{8,40},{... | collective-permute-start | bytes 1032200 | tf_op jit(solution)/shard_map/ppermute | solution.py:450
  23.9 6.7 %copy-start.3 = (bf16[2,336,256]{2,1,0:T(8,128)(2,1)}, bf16[2,336,256]{2,1,0:T(8,128)(2,1)S(1)}, u32[]{:S(2)}) copy-start(bf16[2,336,256]{2,1,0:T(8,128)(2,1)S(1)} %pad_maximum_fusion.2.row1) | copy-start | bytes 1032196
  23.9 8.8 %collective-permute-start.13 = (bf16[2,336,256]{2,1,0:T(8,128)(2,1)S(1)}, bf16[2,336,256]{2,1,0:T(8,128)(2,1)S(1)}, u32[]{:S(2)}, u32[]{:S(2)}) collective-permute-start(bf16[2,336,256]{2,1,0:T(8,128)(2,1)S(1)} %pad_maximum_fusion.2.row1), channel_id=1, source_target_pairs={{0,2},{1,7},{2,4},{3,1},{4,6},{5,3},{6,0},{7,5},{8,10},{9,15},{10,... | collective-permute-start | bytes 1032200 | tf_op jit(solution)/shard_map/ppermute | solution.py:450
  30.7 7.2 %copy-start.4 = (bf16[2,336,256]{2,1,0:T(8,128)(2,1)}, bf16[2,336,256]{2,1,0:T(8,128)(2,1)S(1)}, u32[]{:S(2)}) copy-start(bf16[2,336,256]{2,1,0:T(8,128)(2,1)S(1)} %collective-permute-done.5.row2) | copy-start | bytes 1032196
  30.7 7.2 %copy-start.2 = (bf16[4,336,128]{2,1,0:T(8,128)(2,1)}, bf16[4,336,128]{2,1,0:T(8,128)(2,1)S(1)}, u32[]{:S(2)}) copy-start(bf16[4,336,128]{2,1,0:T(8,128)(2,1)S(1)} %collective-permute-done.7.side_near) | copy-start | bytes 1032196
  30.7 7.2 %collective-permute-start.10 = (bf16[2,336,256]{2,1,0:T(8,128)(2,1)S(1)}, bf16[2,336,256]{2,1,0:T(8,128)(2,1)S(1)}, u32[]{:S(2)}, u32[]{:S(2)}) collective-permute-start(bf16[2,336,256]{2,1,0:T(8,128)(2,1)S(1)} %collective-permute-done.5.row2), channel_id=1, source_target_pairs={{0,1},{1,0},{2,3},{3,2},{4,5},{5,4},{6,7},{7,6},{8,9},{9,8},{10,11... | collective-permute-start | bytes 1032200 | tf_op jit(solution)/shard_map/ppermute | solution.py:450
  30.8 7.2 %collective-permute-start.8 = (bf16[2,336,256]{2,1,0:T(8,128)(2,1)S(1)}, bf16[2,336,256]{2,1,0:T(8,128)(2,1)S(1)}, u32[]{:S(2)}, u32[]{:S(2)}) collective-permute-start(bf16[2,336,256]{2,1,0:T(8,128)(2,1)S(1)} %collective-permute-done.5.row2), channel_id=1, source_target_pairs={{0,2},{1,7},{2,4},{3,1},{4,6},{5,3},{6,0},{7,5},{8,10},{9,15},{10,... | collective-permute-start | bytes 1032200 | tf_op jit(solution)/shard_map/ppermute | solution.py:450
  31.4 6.5 %collective-permute-start.11 = (bf16[2,336,128]{2,1,0:T(8,128)(2,1)S(1)}, bf16[2,336,128]{2,1,0:T(8,128)(2,1)S(1)}, u32[]{:S(2)}, u32[]{:S(2)}) collective-permute-start(bf16[2,336,128]{2,1,0:T(8,128)(2,1)S(1)} %get-tuple-element.70), channel_id=1, source_target_pairs={{0,1},{1,0},{2,3},{3,2},{4,5},{5,4},{6,7},{7,6},{8,9},{9,8},{10,11... | collective-permute-start | bytes 516104 | tf_op jit(solution)/shard_map/ppermute | solution.py:450
  32.4 5.6 %collective-permute-start.9 = (bf16[2,336,128]{2,1,0:T(8,128)(2,1)S(1)}, bf16[2,336,128]{2,1,0:T(8,128)(2,1)S(1)}, u32[]{:S(2)}, u32[]{:S(2)}) collective-permute-start(bf16[2,336,128]{2,1,0:T(8,128)(2,1)S(1)} %get-tuple-element.71), channel_id=1, source_target_pairs={{0,32},{1,97},{2,34},{3,99},{4,36},{5,101},{6,38},{7,103},{8,40},{... | collective-permute-start | bytes 516104 | tf_op jit(solution)/shard_map/ppermute | solution.py:450
  32.7 5.2 %copy-start.5 = (bf16[2,336,256]{2,1,0:T(8,128)(2,1)}, bf16[2,336,256]{2,1,0:T(8,128)(2,1)S(1)}, u32[]{:S(2)}) copy-start(bf16[2,336,256]{2,1,0:T(8,128)(2,1)S(1)} %collective-permute-done.13.row3) | copy-start | bytes 1032196
  32.7 5.3 %collective-permute-start.14 = (bf16[2,336,256]{2,1,0:T(8,128)(2,1)S(1)}, bf16[2,336,256]{2,1,0:T(8,128)(2,1)S(1)}, u32[]{:S(2)}, u32[]{:S(2)}) collective-permute-start(bf16[2,336,256]{2,1,0:T(8,128)(2,1)S(1)} %collective-permute-done.13.row3), channel_id=1, source_target_pairs={{0,1},{1,0},{2,3},{3,2},{4,5},{5,4},{6,7},{7,6},{8,9},{9,8},{10,11... | collective-permute-start | bytes 1032200 | tf_op jit(solution)/shard_map/ppermute | solution.py:450
  37.9 3.9 %copy-start.10 = (bf16[2,336,128]{2,1,0:T(8,128)(2,1)}, bf16[2,336,128]{2,1,0:T(8,128)(2,1)S(1)}, u32[]{:S(2)}) copy-start(bf16[2,336,128]{2,1,0:T(8,128)(2,1)S(1)} %collective-permute-done.11.side_swapped) | copy-start | bytes 516100
  37.9 3.9 %copy-start.11 = (bf16[2,336,128]{2,1,0:T(8,128)(2,1)}, bf16[2,336,128]{2,1,0:T(8,128)(2,1)S(1)}, u32[]{:S(2)}) copy-start(bf16[2,336,128]{2,1,0:T(8,128)(2,1)S(1)} %collective-permute-done.9.side_far) | copy-start | bytes 516100
  38.0 3.9 %copy-start.6 = (bf16[2,336,256]{2,1,0:T(8,128)(2,1)}, bf16[2,336,256]{2,1,0:T(8,128)(2,1)S(1)}, u32[]{:S(2)}) copy-start(bf16[2,336,256]{2,1,0:T(8,128)(2,1)S(1)} %collective-permute-done.10.row4) | copy-start | bytes 1032196
  38.0 3.9 %copy-start.7 = (bf16[2,336,256]{2,1,0:T(8,128)(2,1)}, bf16[2,336,256]{2,1,0:T(8,128)(2,1)S(1)}, u32[]{:S(2)}) copy-start(bf16[2,336,256]{2,1,0:T(8,128)(2,1)S(1)} %collective-permute-done.8.row6) | copy-start | bytes 1032196
  38.0 3.9 %copy-start.8 = (bf16[2,336,256]{2,1,0:T(8,128)(2,1)}, bf16[2,336,256]{2,1,0:T(8,128)(2,1)S(1)}, u32[]{:S(2)}) copy-start(bf16[2,336,256]{2,1,0:T(8,128)(2,1)S(1)} %collective-permute-done.14.row5) | copy-start | bytes 1032196
  38.0 3.8 %collective-permute-start.15 = (bf16[2,336,256]{2,1,0:T(8,128)(2,1)S(1)}, bf16[2,336,256]{2,1,0:T(8,128)(2,1)S(1)}, u32[]{:S(2)}, u32[]{:S(2)}) collective-permute-start(bf16[2,336,256]{2,1,0:T(8,128)(2,1)S(1)} %collective-permute-done.8.row6), channel_id=1, source_target_pairs={{0,1},{1,0},{2,3},{3,2},{4,5},{5,4},{6,7},{7,6},{8,9},{9,8},{10,11... | collective-permute-start | bytes 1032200 | tf_op jit(solution)/shard_map/ppermute | solution.py:450
  41.8 0.7 %copy-start.9 = (bf16[2,336,256]{2,1,0:T(8,128)(2,1)}, bf16[2,336,256]{2,1,0:T(8,128)(2,1)S(1)}, u32[]{:S(2)}) copy-start(bf16[2,336,256]{2,1,0:T(8,128)(2,1)S(1)} %collective-permute-done.15.row7) | copy-start | bytes 1032196

commit v4 on v3

--- a/solution.py
+++ b/solution.py
@@ -10,7 +10,7 @@
 F32 = jnp.float32
 BF16 = jnp.bfloat16
 HIGH = lax.Precision.HIGHEST
-CHUNK = 896
+CHUNK = 672
 TOLERANCE = 3e-4
 VMEM_LIMIT = 60 * 1024 * 1024
 
@@ -266,13 +266,15 @@
     lows = (low0, low1, low2, low3)
     factor(aug_ref, lows, 3, 4, aug_ref[192:256, 384:512])
     low_inv[...] = gather_inverse(aug_ref)
+    first = pltpu.make_async_copy(low_inv, low_inv_hbm, out_sem.at[2])
+    first.start()
     for load in loads[1:]:
         load.wait()
     low = lower_only(jnp.concatenate([ref[...] for ref in lows], axis=1))
     y = jnp.where(iota((256, 256), 1) < rank_t[0, 0], nt(sketch_t[:, :256], low), 0.0)
     y_ref[...] = y
     x_ref[...] = nn(y, gram[...])
-    for store in copy_all([(low_inv, low_inv_hbm), (y_ref, y_hbm), (x_ref, x_hbm)], out_sem):
+    for store in copy_all([(y_ref, y_hbm), (x_ref, x_hbm)], out_sem) + [first]:
         store.wait()
 
 

time: 64.5 us -> 64.4 us (level)
  no operation moved by 1% of the time
where the time goes in v4:
time: 64.4 us; the launch traced here: 64 us
  Pallas kernels  37.7 us (59%)
  starting transfers between devices  17.8 us (28%)
  between operations  3.78 us (6%)
  local copies, waits for them, and re-layouts  2.57 us (4%)
  other arithmetic  2.07 us (3%)
    pallas_call x1, Pallas kernels, main_call(): pl.pallas_call(main_kernel, out_shape=(out, out), in_specs=[pl.BlockSpec(...  21.3 us
    ppermute x16, starting transfers between devices, send(): return lax.ppermute(x, axis, [(i, step(i)) for i in range(count)])  17.8 us
    pallas_call x1, Pallas kernels, middle_call(): pl.pallas_call(middle_kernel, out_shape=[jax.ShapeDtypeStruct(shape, F32)...  5.86 us
    pallas_call x1, Pallas kernels, early_call(): pl.pallas_call(early_kernel, out_shape=[jax.ShapeDtypeStruct(shape, F32)...  5.86 us
    pallas_call x1, Pallas kernels, late_call(): pl.pallas_call(late_kernel, out_shape=[square] * 3, in_specs=[pl.BlockSpe...  4.71 us
    unnamed x26, local copies, waits for them, and re-layouts  2.54 us
  transfers between devices with their start and end apart: 16, of which 0 were waited for; matrix products, arithmetic and copies ran while one was open for 3% of the time, Pallas kernels for 26%

profile of v4, /device:TPU:1, one launch (start us, length us, event | category | flops | bytes accessed | tf_op | source)
XLA Modules:
  0.0 64.0 jit_solution(11526046394380076808)
XLA Ops:
  0.6 0.9 %select_bitcast_fusion = bf16[168,256]{1,0:T(8,128)(2,1)S(1)} fusion(bf16[1,168,256]{2,1,0:T(8,128)(2,1)} %param.14, bf16[1,168,256]{2,1,0:T(8,128)(2,1)} %param.13, pred[]{:T(512)S(6)} %eq.5), kind=kLoop, calls=%fused_computation.7 | loop fusion | flops 43008 | bytes 258049 | tf_op jit(solution)/shard_map/jit(_where)/select_n | solution.py:471
  1.6 1.5 %collective-permute-start = (bf16[168,256]{1,0:T(8,128)(2,1)S(1)}, bf16[168,256]{1,0:T(8,128)(2,1)S(1)}, u32[]{:S(2)}, u32[]{:S(2)}) collective-permute-start(bf16[168,256]{1,0:T(8,128)(2,1)S(1)} %select_bitcast_fusion), channel_id=1, source_target_pairs={{0,1},{1,0},{2,3},{3,2},{4,5},{5,4},{6,7},{7,6},{8,9},{9,8},{10,11... | collective-permute-start | bytes 258056 | tf_op jit(solution)/shard_map/ppermute | solution.py:452
  3.7 0.9 %copy.13 = bf16[1,336,64]{2,1,0:T(8,128)(2,1)S(1)} copy(bf16[1,336,64]{1,2,0:T(8,128)(2,1)} %param.15) | data formatting | bytes 86016 | tf_op args[4]
  4.6 0.9 %copy.14 = bf16[1,336,64]{2,1,0:T(8,128)(2,1)S(1)} copy(bf16[1,336,64]{1,2,0:T(8,128)(2,1)} %param.16) | data formatting | bytes 86016 | tf_op args[5]
  5.5 0.1 pad_maximum_fusion.4
  5.7 0.0 collective-permute-done
  5.7 0.9 %bitcast_select_fusion.1 = (bf16[168,256]{1,0:T(8,128)(2,1)S(1)}, bf16[168,256]{1,0:T(8,128)(2,1)S(1)}) fusion(bf16[168,256]{1,0:T(8,128)(2,1)S(1)} %collective-permute-done, pred[]{:T(512)S(6)} %eq.5, bf16[1,168,256]{2,1,0:T(8,128)(2,1)} %param.13, bf16[1,168,256]{2,1,0:T(8,128)(2,1)} %param.14), kind=kLoop, calls=%fused_computation.6 | loop fusion | flops 129024 | bytes 430081 | tf_op jit(solution)/shard_map/jit(_where)/select_n | solution.py:474
  6.6 0.1 collective-permute-start.4
  6.7 3.1 %collective-permute-start.1 = (bf16[336,128]{1,0:T(8,128)(2,1)S(1)}, bf16[336,128]{1,0:T(8,128)(2,1)S(1)}, u32[]{:S(2)}, u32[]{:S(2)}) collective-permute-start(bf16[336,128]{1,0:T(8,128)(2,1)S(1)} %pad_maximum_fusion.4), channel_id=1, source_target_pairs={{0,16},{16,0},{32,48},{48,32},{64,80},{80,64},{96,112},{112,96},{1... | collective-permute-start | bytes 258056 | tf_op jit(solution)/shard_map/ppermute | solution.py:452
  9.8 0.7 %collective-permute-start.3 = (bf16[336,256]{1,0:T(8,128)(2,1)S(1)}, bf16[336,256]{1,0:T(8,128)(2,1)S(1)}, u32[]{:S(2)}, u32[]{:S(2)}) collective-permute-start(bf16[336,256]{1,0:T(8,128)(2,1)S(1)} %pad_maximum_fusion.3), channel_id=1, source_target_pairs={{0,1},{1,0},{2,3},{3,2},{4,5},{5,4},{6,7},{7,6},{8,9},{9,8},{10,11... | collective-permute-start | bytes 516104 | tf_op jit(solution)/shard_map/ppermute | solution.py:452
  10.5 0.4 collective-permute-start.2
  10.9 5.9 %early_factor.1 = (f32[256,256]{1,0:T(8,128)}, f32[256,320]{1,0:T(8,128)}, f32[256,512]{1,0:T(8,128)}, f32[256,64]{1,0:T(8,128)}) custom-call(s32[1,1]{1,0:T(1,128)S(6)} %copy.15.rank_t, f32[320,256]{1,0:T(8,128)} %sketch_hbm.1, bf16[2688,256]{1,0:T(8,128)(2,1)} %bitcast.29, bf16[2688,256]{1,0:T(8,128)(2,1)} %bitcast.31), custom_call_target="tpu_custom_call" | custom-call | flops 7000000000 | bytes 4000000 | tf_op jit(solution)/shard_map/early_factor/pallas_call | solution.py:217
  16.8 0.0 collective-permute-done.4
  16.8 0.0 collective-permute-done.1
  16.8 0.0 collective-permute-done.3
  16.8 0.0 collective-permute-done.2
  16.8 0.6 collective-permute-start.6
  17.4 0.0 collective-permute-start.12
  17.4 0.0 copy-start
  17.4 2.5 %collective-permute-start.5 = (bf16[2,336,256]{2,1,0:T(8,128)(2,1)S(1)}, bf16[2,336,256]{2,1,0:T(8,128)(2,1)S(1)}, u32[]{:S(2)}, u32[]{:S(2)}) collective-permute-start(bf16[2,336,256]{2,1,0:T(8,128)(2,1)S(1)} %pad_maximum_fusion.row0), channel_id=1, source_target_pairs={{0,2},{1,7},{2,4},{3,1},{4,6},{5,3},{6,0},{7,5},{8,10},{9,15},{10,... | collective-permute-start | bytes 1032200 | tf_op jit(solution)/shard_map/ppermute | solution.py:452
  20.0 0.0 collective-permute-done.6
  20.0 0.0 copy-start.1
  20.0 3.8 %collective-permute-start.7 = (bf16[4,336,128]{2,1,0:T(8,128)(2,1)S(1)}, bf16[4,336,128]{2,1,0:T(8,128)(2,1)S(1)}, u32[]{:S(2)}, u32[]{:S(2)}) collective-permute-start(bf16[4,336,128]{2,1,0:T(8,128)(2,1)S(1)} %pad_maximum_fusion.1.side_own), channel_id=1, source_target_pairs={{0,32},{1,97},{2,34},{3,99},{4,36},{5,101},{6,38},{7,103},{8,40},{... | collective-permute-start | bytes 1032200 | tf_op jit(solution)/shard_map/ppermute | solution.py:452
  23.9 0.0 collective-permute-done.12
  23.9 0.0 copy-start.3
  23.9 0.8 %collective-permute-start.13 = (bf16[2,336,256]{2,1,0:T(8,128)(2,1)S(1)}, bf16[2,336,256]{2,1,0:T(8,128)(2,1)S(1)}, u32[]{:S(2)}, u32[]{:S(2)}) collective-permute-start(bf16[2,336,256]{2,1,0:T(8,128)(2,1)S(1)} %pad_maximum_fusion.2.row1), channel_id=1, source_target_pairs={{0,2},{1,7},{2,4},{3,1},{4,6},{5,3},{6,0},{7,5},{8,10},{9,15},{10,... | collective-permute-start | bytes 1032200 | tf_op jit(solution)/shard_map/ppermute | solution.py:452
  24.8 5.9 %middle_factor.1 = (f32[256,512]{1,0:T(8,128)}, f32[256,64]{1,0:T(8,128)}, f32[256,64]{1,0:T(8,128)}) custom-call(f32[256,512]{1,0:T(8,128)} %get-tuple-element.42.aug_hbm), custom_call_target="tpu_custom_call" | custom-call | flops 6000000000 | bytes 2000000 | tf_op jit(solution)/shard_map/middle_factor/pallas_call | solution.py:245
  30.6 0.0 copy-done
  30.6 0.0 copy-done.1
  30.7 0.0 collective-permute-done.5.row2
  30.7 0.0 collective-permute-done.7.side_near
  30.7 0.1 collective-permute-start.10
  30.8 0.6 collective-permute-start.8
  31.4 0.9 %collective-permute-start.11 = (bf16[2,336,128]{2,1,0:T(8,128)(2,1)S(1)}, bf16[2,336,128]{2,1,0:T(8,128)(2,1)S(1)}, u32[]{:S(2)}, u32[]{:S(2)}) collective-permute-start(bf16[2,336,128]{2,1,0:T(8,128)(2,1)S(1)} %get-tuple-element.70), channel_id=1, source_target_pairs={{0,1},{1,0},{2,3},{3,2},{4,5},{5,4},{6,7},{7,6},{8,9},{9,8},{10,11... | collective-permute-start | bytes 516104 | tf_op jit(solution)/shard_map/ppermute | solution.py:452
  32.4 0.3 collective-permute-start.9
  32.7 0.0 collective-permute-done.13.row3
  32.7 0.5 collective-permute-start.14
  33.2 4.7 %late_factor.1 = (f32[256,256]{1,0:T(8,128)}, f32[256,256]{1,0:T(8,128)}, f32[256,256]{1,0:T(8,128)}) custom-call(s32[1,1]{1,0:T(1,128)S(6)} %copy.15.rank_t, f32[256,512]{1,0:T(8,128)} %get-tuple-element.50.aug_hbm, f32[256,64]{1,0:T(8,128)} %get-tuple-element.51.low0_hbm, f32[256,64]{1,0:T(8,128)} %get-tuple-element.52.low1_hbm, ...), custom_call_target="tpu_custom_call" | custom-call | flops 6000000000 | bytes 2000000 | tf_op jit(solution)/shard_map/late_factor/pallas_call | solution.py:285
  37.9 0.0 collective-permute-done.11.side_swapped
  37.9 0.0 collective-permute-done.9.side_far
  37.9 0.0 copy-start.11
  37.9 0.0 collective-permute-done.10.row4
  38.0 0.0 collective-permute-done.8.row6
  38.0 0.0 collective-permute-done.14.row5
  38.0 1.8 %collective-permute-start.15 = (bf16[2,336,256]{2,1,0:T(8,128)(2,1)S(1)}, bf16[2,336,256]{2,1,0:T(8,128)(2,1)S(1)}, u32[]{:S(2)}, u32[]{:S(2)}) collective-permute-start(bf16[2,336,256]{2,1,0:T(8,128)(2,1)S(1)} %collective-permute-done.8.row6), channel_id=1, source_target_pairs={{0,1},{1,0},{2,3},{3,2},{4,5},{5,4},{6,7},{7,6},{8,9},{9,8},{10,11... | collective-permute-start | bytes 1032200 | tf_op jit(solution)/shard_map/ppermute | solution.py:452
  41.8 0.0 collective-permute-done.15.row7
  41.9 0.7 %copy-done.9 = bf16[2,336,256]{2,1,0:T(8,128)(2,1)} copy-done((bf16[2,336,256]{2,1,0:T(8,128)(2,1)}, bf16[2,336,256]{2,1,0:T(8,128)(2,1)S(1)}, u32[]{:S(2)}) %copy-start.9) | copy-done | bytes 344088
  42.5 21.3 %recompress.1 = (f32[2688,256]{1,0:T(8,128)}, f32[2688,256]{1,0:T(8,128)}) custom-call(s32[1,1]{1,0:T(1,128)S(6)} %copy.15.rank_t, s32[1]{0:T(128)S(6)} %copy.16.rank_i, s32[1]{0:T(128)S(6)} %copy.17.rank_j, s32[1,1]{1,0:T(1,128)S(6)} %copy.18.rank_s, f32[256,256]{1,0:T(8,128)} %get-tuple-element.60.low_inv_hbm, f32[256,320]{1,0:T(8,128)} %get-tuple-element.54.sketch_t_hbm, ...), custom_call_target="tpu_custom_call" | custom-call | flops 20000000000 | bytes 15000000 | tf_op jit(solution)/shard_map/recompress/pallas_call | solution.py:435
  (22 shorter events, 0.2 us)
Async XLA Ops:
  1.6 4.1 %collective-permute-start = (bf16[168,256]{1,0:T(8,128)(2,1)S(1)}, bf16[168,256]{1,0:T(8,128)(2,1)S(1)}, u32[]{:S(2)}, u32[]{:S(2)}) collective-permute-start(bf16[168,256]{1,0:T(8,128)(2,1)S(1)} %select_bitcast_fusion), channel_id=1, source_target_pairs={{0,1},{1,0},{2,3},{3,2},{4,5},{5,4},{6,7},{7,6},{8,9},{9,8},{10,11... | collective-permute-start | bytes 258056 | tf_op jit(solution)/shard_map/ppermute | solution.py:452
  6.6 10.1 %collective-permute-start.4 = (bf16[336,128]{1,0:T(8,128)(2,1)S(1)}, bf16[336,128]{1,0:T(8,128)(2,1)S(1)}, u32[]{:S(2)}, u32[]{:S(2)}) collective-permute-start(bf16[336,128]{1,0:T(8,128)(2,1)S(1)} %pad_maximum_fusion.4), channel_id=1, source_target_pairs={{0,1},{1,0},{2,3},{3,2},{4,5},{5,4},{6,7},{7,6},{8,9},{9,8},{10,11... | collective-permute-start | bytes 258056 | tf_op jit(solution)/shard_map/ppermute | solution.py:452
  6.7 10.1 %collective-permute-start.1 = (bf16[336,128]{1,0:T(8,128)(2,1)S(1)}, bf16[336,128]{1,0:T(8,128)(2,1)S(1)}, u32[]{:S(2)}, u32[]{:S(2)}) collective-permute-start(bf16[336,128]{1,0:T(8,128)(2,1)S(1)} %pad_maximum_fusion.4), channel_id=1, source_target_pairs={{0,16},{16,0},{32,48},{48,32},{64,80},{80,64},{96,112},{112,96},{1... | collective-permute-start | bytes 258056 | tf_op jit(solution)/shard_map/ppermute | solution.py:452
  9.8 7.0 %collective-permute-start.3 = (bf16[336,256]{1,0:T(8,128)(2,1)S(1)}, bf16[336,256]{1,0:T(8,128)(2,1)S(1)}, u32[]{:S(2)}, u32[]{:S(2)}) collective-permute-start(bf16[336,256]{1,0:T(8,128)(2,1)S(1)} %pad_maximum_fusion.3), channel_id=1, source_target_pairs={{0,1},{1,0},{2,3},{3,2},{4,5},{5,4},{6,7},{7,6},{8,9},{9,8},{10,11... | collective-permute-start | bytes 516104 | tf_op jit(solution)/shard_map/ppermute | solution.py:452
  10.5 6.3 %collective-permute-start.2 = (bf16[336,256]{1,0:T(8,128)(2,1)S(1)}, bf16[336,256]{1,0:T(8,128)(2,1)S(1)}, u32[]{:S(2)}, u32[]{:S(2)}) collective-permute-start(bf16[336,256]{1,0:T(8,128)(2,1)S(1)} %pad_maximum_fusion.3), channel_id=1, source_target_pairs={{0,8},{1,9},{2,10},{3,11},{4,12},{5,13},{6,14},{7,15},{8,0},{9,1},... | collective-permute-start | bytes 516104 | tf_op jit(solution)/shard_map/ppermute | solution.py:452
  16.8 3.2 %collective-permute-start.6 = (bf16[336,128]{1,0:T(8,128)(2,1)S(1)}, bf16[336,128]{1,0:T(8,128)(2,1)S(1)}, u32[]{:S(2)}, u32[]{:S(2)}) collective-permute-start(bf16[336,128]{1,0:T(8,128)(2,1)S(1)} %collective-permute-done.1), channel_id=1, source_target_pairs={{0,1},{1,0},{2,3},{3,2},{4,5},{5,4},{6,7},{7,6},{8,9},{9,8},{10,11... | collective-permute-start | bytes 258056 | tf_op jit(solution)/shard_map/ppermute | solution.py:452
  17.4 6.5 %collective-permute-start.12 = (bf16[336,256]{1,0:T(8,128)(2,1)S(1)}, bf16[336,256]{1,0:T(8,128)(2,1)S(1)}, u32[]{:S(2)}, u32[]{:S(2)}) collective-permute-start(bf16[336,256]{1,0:T(8,128)(2,1)S(1)} %collective-permute-done.2), channel_id=1, source_target_pairs={{0,1},{1,0},{2,3},{3,2},{4,5},{5,4},{6,7},{7,6},{8,9},{9,8},{10,11... | collective-permute-start | bytes 516104 | tf_op jit(solution)/shard_map/ppermute | solution.py:452
  17.4 13.2 %copy-start = (bf16[2,336,256]{2,1,0:T(8,128)(2,1)}, bf16[2,336,256]{2,1,0:T(8,128)(2,1)S(1)}, u32[]{:S(2)}) copy-start(bf16[2,336,256]{2,1,0:T(8,128)(2,1)S(1)} %pad_maximum_fusion.row0) | copy-start | bytes 1032196
  17.4 13.2 %collective-permute-start.5 = (bf16[2,336,256]{2,1,0:T(8,128)(2,1)S(1)}, bf16[2,336,256]{2,1,0:T(8,128)(2,1)S(1)}, u32[]{:S(2)}, u32[]{:S(2)}) collective-permute-start(bf16[2,336,256]{2,1,0:T(8,128)(2,1)S(1)} %pad_maximum_fusion.row0), channel_id=1, source_target_pairs={{0,2},{1,7},{2,4},{3,1},{4,6},{5,3},{6,0},{7,5},{8,10},{9,15},{10,... | collective-permute-start | bytes 1032200 | tf_op jit(solution)/shard_map/ppermute | solution.py:452
  20.0 10.6 %copy-start.1 = (bf16[4,336,128]{2,1,0:T(8,128)(2,1)}, bf16[4,336,128]{2,1,0:T(8,128)(2,1)S(1)}, u32[]{:S(2)}) copy-start(bf16[4,336,128]{2,1,0:T(8,128)(2,1)S(1)} %pad_maximum_fusion.1.side_own) | copy-start | bytes 1032196
  20.0 10.6 %collective-permute-start.7 = (bf16[4,336,128]{2,1,0:T(8,128)(2,1)S(1)}, bf16[4,336,128]{2,1,0:T(8,128)(2,1)S(1)}, u32[]{:S(2)}, u32[]{:S(2)}) collective-permute-start(bf16[4,336,128]{2,1,0:T(8,128)(2,1)S(1)} %pad_maximum_fusion.1.side_own), channel_id=1, source_target_pairs={{0,32},{1,97},{2,34},{3,99},{4,36},{5,101},{6,38},{7,103},{8,40},{... | collective-permute-start | bytes 1032200 | tf_op jit(solution)/shard_map/ppermute | solution.py:452
  23.9 6.7 %copy-start.3 = (bf16[2,336,256]{2,1,0:T(8,128)(2,1)}, bf16[2,336,256]{2,1,0:T(8,128)(2,1)S(1)}, u32[]{:S(2)}) copy-start(bf16[2,336,256]{2,1,0:T(8,128)(2,1)S(1)} %pad_maximum_fusion.2.row1) | copy-start | bytes 1032196
  23.9 8.8 %collective-permute-start.13 = (bf16[2,336,256]{2,1,0:T(8,128)(2,1)S(1)}, bf16[2,336,256]{2,1,0:T(8,128)(2,1)S(1)}, u32[]{:S(2)}, u32[]{:S(2)}) collective-permute-start(bf16[2,336,256]{2,1,0:T(8,128)(2,1)S(1)} %pad_maximum_fusion.2.row1), channel_id=1, source_target_pairs={{0,2},{1,7},{2,4},{3,1},{4,6},{5,3},{6,0},{7,5},{8,10},{9,15},{10,... | collective-permute-start | bytes 1032200 | tf_op jit(solution)/shard_map/ppermute | solution.py:452
  30.7 7.2 %copy-start.4 = (bf16[2,336,256]{2,1,0:T(8,128)(2,1)}, bf16[2,336,256]{2,1,0:T(8,128)(2,1)S(1)}, u32[]{:S(2)}) copy-start(bf16[2,336,256]{2,1,0:T(8,128)(2,1)S(1)} %collective-permute-done.5.row2) | copy-start | bytes 1032196
  30.7 7.2 %copy-start.2 = (bf16[4,336,128]{2,1,0:T(8,128)(2,1)}, bf16[4,336,128]{2,1,0:T(8,128)(2,1)S(1)}, u32[]{:S(2)}) copy-start(bf16[4,336,128]{2,1,0:T(8,128)(2,1)S(1)} %collective-permute-done.7.side_near) | copy-start | bytes 1032196
  30.7 7.2 %collective-permute-start.10 = (bf16[2,336,256]{2,1,0:T(8,128)(2,1)S(1)}, bf16[2,336,256]{2,1,0:T(8,128)(2,1)S(1)}, u32[]{:S(2)}, u32[]{:S(2)}) collective-permute-start(bf16[2,336,256]{2,1,0:T(8,128)(2,1)S(1)} %collective-permute-done.5.row2), channel_id=1, source_target_pairs={{0,1},{1,0},{2,3},{3,2},{4,5},{5,4},{6,7},{7,6},{8,9},{9,8},{10,11... | collective-permute-start | bytes 1032200 | tf_op jit(solution)/shard_map/ppermute | solution.py:452
  30.8 7.2 %collective-permute-start.8 = (bf16[2,336,256]{2,1,0:T(8,128)(2,1)S(1)}, bf16[2,336,256]{2,1,0:T(8,128)(2,1)S(1)}, u32[]{:S(2)}, u32[]{:S(2)}) collective-permute-start(bf16[2,336,256]{2,1,0:T(8,128)(2,1)S(1)} %collective-permute-done.5.row2), channel_id=1, source_target_pairs={{0,2},{1,7},{2,4},{3,1},{4,6},{5,3},{6,0},{7,5},{8,10},{9,15},{10,... | collective-permute-start | bytes 1032200 | tf_op jit(solution)/shard_map/ppermute | solution.py:452
  31.4 6.5 %collective-permute-start.11 = (bf16[2,336,128]{2,1,0:T(8,128)(2,1)S(1)}, bf16[2,336,128]{2,1,0:T(8,128)(2,1)S(1)}, u32[]{:S(2)}, u32[]{:S(2)}) collective-permute-start(bf16[2,336,128]{2,1,0:T(8,128)(2,1)S(1)} %get-tuple-element.70), channel_id=1, source_target_pairs={{0,1},{1,0},{2,3},{3,2},{4,5},{5,4},{6,7},{7,6},{8,9},{9,8},{10,11... | collective-permute-start | bytes 516104 | tf_op jit(solution)/shard_map/ppermute | solution.py:452
  32.4 5.6 %collective-permute-start.9 = (bf16[2,336,128]{2,1,0:T(8,128)(2,1)S(1)}, bf16[2,336,128]{2,1,0:T(8,128)(2,1)S(1)}, u32[]{:S(2)}, u32[]{:S(2)}) collective-permute-start(bf16[2,336,128]{2,1,0:T(8,128)(2,1)S(1)} %get-tuple-element.71), channel_id=1, source_target_pairs={{0,32},{1,97},{2,34},{3,99},{4,36},{5,101},{6,38},{7,103},{8,40},{... | collective-permute-start | bytes 516104 | tf_op jit(solution)/shard_map/ppermute | solution.py:452
  32.7 5.2 %copy-start.5 = (bf16[2,336,256]{2,1,0:T(8,128)(2,1)}, bf16[2,336,256]{2,1,0:T(8,128)(2,1)S(1)}, u32[]{:S(2)}) copy-start(bf16[2,336,256]{2,1,0:T(8,128)(2,1)S(1)} %collective-permute-done.13.row3) | copy-start | bytes 1032196
  32.7 5.3 %collective-permute-start.14 = (bf16[2,336,256]{2,1,0:T(8,128)(2,1)S(1)}, bf16[2,336,256]{2,1,0:T(8,128)(2,1)S(1)}, u32[]{:S(2)}, u32[]{:S(2)}) collective-permute-start(bf16[2,336,256]{2,1,0:T(8,128)(2,1)S(1)} %collective-permute-done.13.row3), channel_id=1, source_target_pairs={{0,1},{1,0},{2,3},{3,2},{4,5},{5,4},{6,7},{7,6},{8,9},{9,8},{10,11... | collective-permute-start | bytes 1032200 | tf_op jit(solution)/shard_map/ppermute | solution.py:452
  37.9 3.9 %copy-start.10 = (bf16[2,336,128]{2,1,0:T(8,128)(2,1)}, bf16[2,336,128]{2,1,0:T(8,128)(2,1)S(1)}, u32[]{:S(2)}) copy-start(bf16[2,336,128]{2,1,0:T(8,128)(2,1)S(1)} %collective-permute-done.11.side_swapped) | copy-start | bytes 516100
  37.9 3.9 %copy-start.11 = (bf16[2,336,128]{2,1,0:T(8,128)(2,1)}, bf16[2,336,128]{2,1,0:T(8,128)(2,1)S(1)}, u32[]{:S(2)}) copy-start(bf16[2,336,128]{2,1,0:T(8,128)(2,1)S(1)} %collective-permute-done.9.side_far) | copy-start | bytes 516100
  38.0 3.9 %copy-start.6 = (bf16[2,336,256]{2,1,0:T(8,128)(2,1)}, bf16[2,336,256]{2,1,0:T(8,128)(2,1)S(1)}, u32[]{:S(2)}) copy-start(bf16[2,336,256]{2,1,0:T(8,128)(2,1)S(1)} %collective-permute-done.10.row4) | copy-start | bytes 1032196
  38.0 3.9 %copy-start.7 = (bf16[2,336,256]{2,1,0:T(8,128)(2,1)}, bf16[2,336,256]{2,1,0:T(8,128)(2,1)S(1)}, u32[]{:S(2)}) copy-start(bf16[2,336,256]{2,1,0:T(8,128)(2,1)S(1)} %collective-permute-done.8.row6) | copy-start | bytes 1032196
  38.0 3.9 %copy-start.8 = (bf16[2,336,256]{2,1,0:T(8,128)(2,1)}, bf16[2,336,256]{2,1,0:T(8,128)(2,1)S(1)}, u32[]{:S(2)}) copy-start(bf16[2,336,256]{2,1,0:T(8,128)(2,1)S(1)} %collective-permute-done.14.row5) | copy-start | bytes 1032196
  38.0 3.8 %collective-permute-start.15 = (bf16[2,336,256]{2,1,0:T(8,128)(2,1)S(1)}, bf16[2,336,256]{2,1,0:T(8,128)(2,1)S(1)}, u32[]{:S(2)}, u32[]{:S(2)}) collective-permute-start(bf16[2,336,256]{2,1,0:T(8,128)(2,1)S(1)} %collective-permute-done.8.row6), channel_id=1, source_target_pairs={{0,1},{1,0},{2,3},{3,2},{4,5},{5,4},{6,7},{7,6},{8,9},{9,8},{10,11... | collective-permute-start | bytes 1032200 | tf_op jit(solution)/shard_map/ppermute | solution.py:452
  41.8 0.7 %copy-start.9 = (bf16[2,336,256]{2,1,0:T(8,128)(2,1)}, bf16[2,336,256]{2,1,0:T(8,128)(2,1)S(1)}, u32[]{:S(2)}) copy-start(bf16[2,336,256]{2,1,0:T(8,128)(2,1)S(1)} %collective-permute-done.15.row7) | copy-start | bytes 1032196
